TPU v7x, 32 devices: a whole 2x2x4 slice. The times are simulated.
32 devices in a mesh: dp: 8 (over z, y), tensor: 4 (over x, core).
Axes of the slice: x: 2, y: 2, z: 4, core: 2. Of those that a mesh axis runs over, the one named last changes fastest.
Arguments:
- tokens: bfloat16 [1024, 2048], P('dp'), may hold values from -6 to 6
- out_grad: bfloat16 [1024, 2048], P('dp'), may hold values from -6 to 6
- row_place: int32 [1024], replicated, may hold values from 0 to 1023, as said below
- seq_lengths: int32 [8, 3], P('dp'), may hold values from 1 to 64, 128 in all within a row
- att_routes: int32 [1024, 2], P('dp'), may hold values from 0 to 7, all different within a row; in each aligned block of 128 rows (0 to 127, 128 to 255, ...) at most 64 rows name the same one
- att_gates: float32 [1024, 2], P('dp'), may hold values from 0.25 to 1
- mlp_routes: int32 [1024, 2], P('dp'), may hold values from 0 to 7, all different within a row; in each aligned block of 128 rows (0 to 127, 128 to 255, ...) at most 64 rows name the same one
- mlp_gates: float32 [1024, 2], P('dp'), may hold values from 0.25 to 1
- gain_attn: float32 [2048], replicated, may hold values from 0.5 to 1.5
- w_kv: bfloat16 [2048, 2, 2048], P(None, None, 'tensor'), may hold values from -0.125 to 0.125
- w_query: bfloat16 [8, 2048, 2048], P('dp', None, 'tensor'), may hold values from -0.125 to 0.125
- w_out: bfloat16 [8, 2048, 2048], P('dp', 'tensor'), may hold values from -0.5 to 0.5
- gain_mlp: float32 [2048], replicated, may hold values from 0.5 to 1.5
- w_gate: bfloat16 [8, 2048, 5632], P('dp', None, 'tensor'), may hold values from -0.125 to 0.125
- w_up: bfloat16 [8, 2048, 5632], P('dp', None, 'tensor'), may hold values from -0.125 to 0.125
- w_down: bfloat16 [8, 5632, 2048], P('dp', 'tensor'), may hold values from -0.15625 to 0.15625
Outputs:
- mixed: bfloat16 [1024, 2048], P('dp')
- tokens_grad: bfloat16 [1024, 2048], P('dp')
- gain_attn_grad: float32 [2048], replicated
- w_kv_grad: float32 [2048, 2, 2048], P(None, None, 'tensor')
- w_query_grad: float32 [8, 2048, 2048], P('dp', None, 'tensor')
- w_out_grad: float32 [8, 2048, 2048], P('dp', 'tensor')
- gain_mlp_grad: float32 [2048], replicated
- w_gate_grad: float32 [8, 2048, 5632], P('dp', None, 'tensor')
- w_up_grad: float32 [8, 2048, 5632], P('dp', None, 'tensor')
- w_down_grad: float32 [8, 5632, 2048], P('dp', 'tensor')
Inputs may be any that keep to these rules, and one draw needn't show every extreme that they name: `row_place`: A permutation of the working positions; of the 128 given rows on each index of dp, the same number go to every group. `seq_lengths`: each row sums to 128, and its largest entry is exactly 64. `att_routes`: the two entries of a row differ. Among the rows of one index of dp no expert is named by more than 64 rows, and one is named by exactly 64 rows in some of them. `mlp_routes`: the two entries of a row differ. Among the rows of one index of dp no expert is named by more than 64 rows, and one is named by exactly 64 rows in some of them.
All inputs are finite; a program needn't handle non-finite values.
Results may differ from a plain program's by a relative error of at most 0.019.
Values may be sent and summed in bfloat16 or wider, within the bound.
A program may use at most 256 MiB of HBM per device.

v0:
```python
import math

import jax
import jax.numpy as jnp
from jax import lax
from jax.sharding import PartitionSpec as P

HD = 128
ATT_EXPERTS = 8
EXPERTS = 8
CAP = 64


EPSILON = 1e-05
THETA = 10000.0


def inverse_rms(values_in):
    return lax.rsqrt(jnp.mean(values_in * values_in, axis=-1, keepdims=True) + EPSILON)


def norm_backward(inputs, inv_root, gain, incoming):
    weighted = incoming * gain
    inner_mean = jnp.mean(inputs * weighted, axis=-1, keepdims=True)
    return inv_root * weighted - inputs * (inv_root * inv_root * inv_root) * inner_mean


def rotate(vectors, positions, direction):
    half_dim = vectors.shape[-1] // 2
    frequency = jnp.exp(-math.log(THETA) * jnp.arange(half_dim, dtype=jnp.float32) / half_dim)
    angles = positions.astype(jnp.float32)[:, None] * frequency[None, :]
    target = (vectors.shape[0],) + (1,) * (vectors.ndim - 2) + (half_dim,)
    cosine = jnp.cos(angles).reshape(target)
    sine = direction * jnp.sin(angles).reshape(target)
    former = vectors[..., :half_dim]
    latter = vectors[..., half_dim:]
    return jnp.concatenate(
        [former * cosine - latter * sine, latter * cosine + former * sine], axis=-1
    )


def expert_slots(routes, experts, capacity):
    flattened = routes.reshape(-1)
    pair_count = flattened.shape[0]
    one_hot = (flattened[:, None] == jnp.arange(experts, dtype=jnp.int32)[None, :]).astype(
        jnp.int32
    )
    earlier = jnp.cumsum(one_hot, axis=0) - one_hot
    position = jnp.sum(earlier * one_hot, axis=1)
    slot_table = jnp.full((experts, capacity), pair_count, jnp.int32)
    slot_table = slot_table.at[flattened, position].set(jnp.arange(pair_count, dtype=jnp.int32))
    return (flattened * capacity + position, slot_table)


def pick_rows(source_rows, slot_table):
    padded = jnp.concatenate(
        [source_rows, jnp.zeros((1, source_rows.shape[1]), source_rows.dtype)], axis=0
    )
    return padded[slot_table]


def send_slices(source_rows, slot_table, group_size):
    picked = pick_rows(source_rows, slot_table)
    experts, capacity, features = picked.shape
    divided = picked.reshape(experts, capacity, group_size, features // group_size)
    return divided.transpose(0, 2, 1, 3).reshape(
        experts * group_size, capacity, features // group_size
    )


def send_copies(source_rows, slot_table, group_size):
    picked = pick_rows(source_rows, slot_table)
    experts, capacity, features = picked.shape
    copies = jnp.broadcast_to(picked[:, None], (experts, group_size, capacity, features))
    return copies.reshape(experts * group_size, capacity, features)


def owners_summed(returned, pair_where, group_size):
    owners, capacity, features = returned.shape
    summed = returned.reshape(owners // group_size, group_size, capacity, features).sum(axis=1)
    return summed.reshape(-1, features)[pair_where]


def owners_joined(returned, pair_where, group_size):
    owners, capacity, features = returned.shape
    joined = returned.reshape(owners // group_size, group_size, capacity, features).transpose(
        0, 2, 1, 3
    )
    return joined.reshape(-1, group_size * features)[pair_where]


def query_return(pieces):
    return lax.all_to_all(pieces, "dp", split_axis=0, concat_axis=0, tiled=True)


def output_return(pieces):
    return lax.all_to_all(pieces, "dp", split_axis=0, concat_axis=0, tiled=True)


def expert_return(pieces):
    return lax.all_to_all(pieces, "dp", split_axis=0, concat_axis=0, tiled=True)


def tensor_total(pieces):
    return lax.psum(pieces, "tensor")


def deal_plan(row_place, rows_dev):
    device_count = lax.axis_size("dp")
    my_index = lax.axis_index("dp")
    per_peer = rows_dev // device_count
    every_place = row_place.reshape(device_count, rows_dev)
    my_places = lax.dynamic_index_in_dim(every_place, my_index, 0, keepdims=False)
    counting = jnp.arange(rows_dev, dtype=jnp.int32)
    ordering = jnp.argsort(my_places // rows_dev * rows_dev + counting)
    wanted = every_place // rows_dev == my_index
    chosen = jnp.argsort(
        jnp.where(wanted, counting[None, :], rows_dev + counting[None, :]), axis=1
    )[:, :per_peer]
    placed = jnp.take_along_axis(every_place, chosen, axis=1) % rows_dev
    return (ordering, placed.reshape(-1))


def masked_scores(query_b, keys_b, allowed):
    raw = jnp.einsum(
        "ikjd,mjd->kjim", query_b, keys_b, preferred_element_type=jnp.float32
    ) / math.sqrt(query_b.shape[-1])
    return jnp.where(allowed[None, None], raw, -1e30)


def local(
    tokens,
    out_grad,
    row_place,
    seq_lengths,
    att_routes,
    att_gates,
    mlp_routes,
    mlp_gates,
    gain_attn,
    w_kv,
    w_query,
    w_out,
    gain_mlp,
    w_gate,
    w_up,
    w_down,
):
    rows_dev, features = tokens.shape
    device_count = lax.axis_size("dp")
    group_size = device_count // EXPERTS
    per_peer = rows_dev // device_count
    counting = jnp.arange(rows_dev, dtype=jnp.int32)
    ordering, placed = deal_plan(row_place, rows_dev)
    unplace = jnp.zeros((rows_dev,), jnp.int32).at[placed].set(counting)
    unorder = jnp.zeros((rows_dev,), jnp.int32).at[ordering].set(counting)
    dealt_x, dealt_g = (
        lax.all_to_all(
            tokens[ordering].reshape(device_count, per_peer, features),
            "dp",
            split_axis=0,
            concat_axis=0,
            tiled=True,
        ),
        lax.all_to_all(
            out_grad[ordering].reshape(device_count, per_peer, features),
            "dp",
            split_axis=0,
            concat_axis=0,
            tiled=True,
        ),
    )
    residual = dealt_x.reshape(rows_dev, features)[unplace].astype(jnp.float32)
    top_grad = dealt_g.reshape(rows_dev, features)[unplace].astype(jnp.float32)
    lengths = seq_lengths[0]
    seq_ends = jnp.cumsum(lengths)
    segment = jnp.sum((counting[:, None] >= seq_ends[None, :]).astype(jnp.int32), axis=1)
    starts = seq_ends - lengths
    member = segment[:, None] == jnp.arange(lengths.shape[0], dtype=jnp.int32)[None, :]
    begins = jnp.sum(jnp.where(member, starts[None, :], 0), axis=1)
    positions = counting - begins
    allowed = (segment[:, None] == segment[None, :]) & (counting[None, :] <= counting[:, None])
    head_count = w_kv.shape[2] // HD
    scale_attn = inverse_rms(residual)
    normed = (residual * scale_attn * gain_attn).astype(jnp.bfloat16)
    kv_proj = jnp.einsum("ld,dck->lck", normed, w_kv, preferred_element_type=jnp.float32)
    keys = rotate(kv_proj[:, 0].reshape(rows_dev, head_count, HD), positions, 1.0).astype(
        jnp.bfloat16
    )
    values = kv_proj[:, 1].reshape(rows_dev, head_count, HD).astype(jnp.bfloat16)
    att_where, att_table = expert_slots(att_routes, ATT_EXPERTS, CAP)
    query_rows = lax.all_to_all(
        send_slices(normed, att_table // 2, group_size),
        "dp",
        split_axis=0,
        concat_axis=0,
        tiled=True,
    )
    query_part = jnp.einsum(
        "scd,dh->sch", query_rows, w_query[0], preferred_element_type=jnp.float32
    )
    query_pre = owners_summed(query_return(query_part), att_where, group_size)
    query_rot = rotate(query_pre.reshape(rows_dev, 2, head_count, HD), positions, 1.0).astype(
        jnp.bfloat16
    )
    scores = masked_scores(query_rot, keys, allowed)
    highest = jnp.max(scores, axis=-1, keepdims=True)
    expo = jnp.exp(scores - highest)
    row_total = jnp.sum(expo, axis=-1, keepdims=True)
    log_total = highest + jnp.log(row_total)
    probability = expo / row_total
    attn = jnp.einsum(
        "kjim,mjd->ikjd",
        probability.astype(jnp.bfloat16),
        values,
        preferred_element_type=jnp.float32,
    )
    attn_low = attn.astype(jnp.bfloat16).reshape(rows_dev * 2, head_count * HD)
    out_rows = lax.all_to_all(
        send_copies(attn_low, att_table, group_size), "dp", split_axis=0, concat_axis=0, tiled=True
    )
    out_part = jnp.einsum("sch,hd->scd", out_rows, w_out[0], preferred_element_type=jnp.float32)
    out_pairs = owners_joined(output_return(out_part), att_where, group_size).reshape(
        rows_dev, 2, features
    )
    hidden = residual + tensor_total(jnp.sum(out_pairs * att_gates[:, :, None], axis=1))
    gate_map, up_map, down_map = (w_gate[0], w_up[0], w_down[0])
    scale_mlp = inverse_rms(hidden)
    normed2 = (hidden * scale_mlp * gain_mlp).astype(jnp.bfloat16)
    mlp_where, mlp_table = expert_slots(mlp_routes, EXPERTS, CAP)
    expert_sent = send_copies(normed2, mlp_table // 2, group_size)
    expert_rows = lax.all_to_all(expert_sent, "dp", split_axis=0, concat_axis=0, tiled=True)
    flat_rows = expert_rows.reshape(-1, features)
    gate_act = jnp.dot(flat_rows, gate_map, preferred_element_type=jnp.float32)
    up_act = jnp.dot(flat_rows, up_map, preferred_element_type=jnp.float32)
    inner = (jax.nn.silu(gate_act) * up_act).astype(jnp.bfloat16)
    expert_part = jnp.dot(inner, down_map, preferred_element_type=jnp.float32).reshape(
        expert_rows.shape
    )
    expert_pairs = owners_summed(expert_return(expert_part), mlp_where, group_size).reshape(
        rows_dev, 2, features
    )
    mixed_rows = hidden + tensor_total(jnp.sum(expert_pairs * mlp_gates[:, :, None], axis=1))
    branch_grad = (
        (top_grad[:, None, :] * mlp_gates[:, :, None])
        .astype(jnp.bfloat16)
        .reshape(rows_dev * 2, features)
    )
    grad_sent = send_copies(branch_grad, mlp_table, group_size)
    grad_back, rows_back = (
        lax.all_to_all(grad_sent, "dp", split_axis=0, concat_axis=0, tiled=True),
        lax.all_to_all(expert_sent, "dp", split_axis=0, concat_axis=0, tiled=True),
    )
    grad_rows = grad_back.reshape(-1, features)
    rows_again = rows_back.reshape(-1, features)
    gate_again = jnp.dot(rows_again, gate_map, preferred_element_type=jnp.float32)
    up_again = jnp.dot(rows_again, up_map, preferred_element_type=jnp.float32)
    inner_again = (jax.nn.silu(gate_again) * up_again).astype(jnp.bfloat16)
    contract_rows = (((0,), (0,)), ((), ()))
    contract_cols = (((1,), (1,)), ((), ()))
    d_inner = lax.dot_general(
        grad_rows, down_map, contract_cols, preferred_element_type=jnp.float32
    )
    down_grad_all = lax.dot_general(
        inner_again, grad_rows, contract_rows, preferred_element_type=jnp.float32
    )
    sigmoid_g = jax.nn.sigmoid(gate_again)
    d_up = (d_inner * gate_again * sigmoid_g).astype(jnp.bfloat16)
    d_gate = (d_inner * up_again * sigmoid_g * (1.0 + gate_again * (1.0 - sigmoid_g))).astype(
        jnp.bfloat16
    )
    gate_grad_all = lax.dot_general(
        rows_again, d_gate, contract_rows, preferred_element_type=jnp.float32
    )
    up_grad_all = lax.dot_general(
        rows_again, d_up, contract_rows, preferred_element_type=jnp.float32
    )
    d_rows = lax.dot_general(d_gate, gate_map, contract_cols, preferred_element_type=jnp.float32)
    d_rows = d_rows + lax.dot_general(
        d_up, up_map, contract_cols, preferred_element_type=jnp.float32
    )
    d_pairs = owners_summed(expert_return(d_rows.reshape(expert_rows.shape)), mlp_where, group_size)
    w_gate_grad = gate_grad_all[None]
    w_up_grad = up_grad_all[None]
    w_down_grad = down_grad_all[None]
    d_normed2 = tensor_total(jnp.sum(d_pairs.reshape(rows_dev, 2, features), axis=1))
    d_hidden = top_grad + norm_backward(hidden, scale_mlp, gain_mlp, d_normed2)
    gain_mlp_grad = jnp.sum(d_normed2 * hidden * scale_mlp, axis=0)
    att_grad = (
        (d_hidden[:, None, :] * att_gates[:, :, None])
        .astype(jnp.bfloat16)
        .reshape(rows_dev * 2, features)
    )
    grad_slices = lax.all_to_all(
        send_slices(att_grad, att_table, group_size), "dp", split_axis=0, concat_axis=0, tiled=True
    )
    w_out_grad = jnp.einsum(
        "sch,scd->hd", out_rows, grad_slices, preferred_element_type=jnp.float32
    )
    d_attn_part = jnp.einsum(
        "scd,hd->sch", grad_slices, w_out[0], preferred_element_type=jnp.float32
    )
    d_attn = owners_summed(output_return(d_attn_part), att_where, group_size)
    d_attn = d_attn.astype(jnp.bfloat16).reshape(rows_dev, 2, head_count, HD)
    probability = jnp.exp(masked_scores(query_rot, keys, allowed) - log_total)
    d_prob = jnp.einsum("ikjd,mjd->kjim", d_attn, values, preferred_element_type=jnp.float32)
    d_values = jnp.einsum(
        "kjim,ikjd->mjd",
        probability.astype(jnp.bfloat16),
        d_attn,
        preferred_element_type=jnp.float32,
    )
    delta = jnp.sum(d_prob * probability, axis=-1, keepdims=True)
    d_scores = (probability * (d_prob - delta)).astype(jnp.bfloat16)
    root_hd = math.sqrt(HD)
    d_query = (
        jnp.einsum("kjim,mjd->ikjd", d_scores, keys, preferred_element_type=jnp.float32) / root_hd
    )
    d_keys = (
        jnp.einsum("kjim,ikjd->mjd", d_scores, query_rot, preferred_element_type=jnp.float32)
        / root_hd
    )
    dq_pre = (
        rotate(d_query, positions, -1.0).astype(jnp.bfloat16).reshape(rows_dev * 2, head_count * HD)
    )
    dk_pre = rotate(d_keys, positions, -1.0).reshape(rows_dev, head_count * HD)
    d_kv = jnp.stack([dk_pre, d_values.reshape(rows_dev, head_count * HD)], axis=1).astype(
        jnp.bfloat16
    )
    dq_rows = lax.all_to_all(
        send_copies(dq_pre, att_table, group_size), "dp", split_axis=0, concat_axis=0, tiled=True
    )
    w_query_grad = jnp.einsum(
        "scd,sch->dh", query_rows, dq_rows, preferred_element_type=jnp.float32
    )
    d_slice = jnp.einsum("sch,dh->scd", dq_rows, w_query[0], preferred_element_type=jnp.float32)
    d_norm_query = owners_joined(query_return(d_slice), att_where, group_size)
    d_norm_query = jnp.sum(d_norm_query.reshape(rows_dev, 2, features), axis=1)
    w_kv_grad = jnp.einsum("ld,lck->dck", normed, d_kv, preferred_element_type=jnp.float32)
    d_norm_kv = jnp.einsum("lck,dck->ld", d_kv, w_kv, preferred_element_type=jnp.float32)
    d_normed = tensor_total(d_norm_query + d_norm_kv)
    in_grad = d_hidden + norm_backward(residual, scale_attn, gain_attn, d_normed)
    gain_attn_grad = jnp.sum(d_normed * residual * scale_attn, axis=0)
    w_kv_grad, gain_attn_grad, gain_mlp_grad = (
        lax.psum(w_kv_grad.astype(jnp.bfloat16), "dp").astype(jnp.float32),
        lax.psum(gain_attn_grad.astype(jnp.bfloat16), "dp").astype(jnp.float32),
        lax.psum(gain_mlp_grad.astype(jnp.bfloat16), "dp").astype(jnp.float32),
    )
    send_mixed = mixed_rows.astype(jnp.bfloat16)[placed].reshape(device_count, per_peer, features)
    send_input = in_grad.astype(jnp.bfloat16)[placed].reshape(device_count, per_peer, features)
    back_mixed, back_input = (
        lax.all_to_all(send_mixed, "dp", split_axis=0, concat_axis=0, tiled=True),
        lax.all_to_all(send_input, "dp", split_axis=0, concat_axis=0, tiled=True),
    )
    mixed = back_mixed.reshape(rows_dev, features)[unorder]
    tokens_grad = back_input.reshape(rows_dev, features)[unorder]
    return (
        mixed,
        tokens_grad,
        gain_attn_grad,
        w_kv_grad,
        w_query_grad[None],
        w_out_grad[None],
        gain_mlp_grad,
        w_gate_grad,
        w_up_grad,
        w_down_grad,
    )


def solution(mesh):
    placed = (
        P("dp", None),
        P("dp", None),
        P(),
        P("dp", None),
        P("dp", None),
        P("dp", None),
        P("dp", None),
        P("dp", None),
        P(),
        P(None, None, "tensor"),
        P("dp", None, "tensor"),
        P("dp", "tensor", None),
        P(),
        P("dp", None, "tensor"),
        P("dp", None, "tensor"),
        P("dp", "tensor", None),
    )
    return jax.shard_map(
        local,
        mesh=mesh,
        in_specs=placed,
        out_specs=(
            P("dp", None),
            P("dp", None),
            P(),
            P(None, None, "tensor"),
            P("dp", None, "tensor"),
            P("dp", "tensor", None),
            P(),
            P("dp", None, "tensor"),
            P("dp", None, "tensor"),
            P("dp", "tensor", None),
        ),
        check_vma=False,
    )
```

profile of v0, /device:TPU:0, one launch (start us, length us, event | category | flops | bytes accessed | tf_op | source)
XLA Modules:
  0.0 1165.7 jit_solution(52868065690082007)
XLA Ops:
  14.5 7.3 all-to-all-start
  24.6 11.2 scatter_fusion
  45.3 6.1 all-to-all-start.1
  51.7 47.5 %all-to-all-done.1 = bf16[8,64,2048]{2,1,0:T(8,128)(2,1)} async-done(((bf16[8,64,2048]{2,1,0:T(8,128)(2,1)}), bf16[8,64,2048]{2,1,0:T(8,128)(2,1)}, u32[]{:S(2)}, u32[]{:S(2)}) %all-to-all-start.1) | async-done | bytes 2097184 | tf_op jit(solution)/shard_map/all_to_all | solution.py:192
  116.5 16.7 %all-to-all-done.2 = f32[8,64,512]{2,1,0:T(8,128)S(1)} async-done(((f32[8,64,512]{2,1,0:T(8,128)}), f32[8,64,512]{2,1,0:T(8,128)S(1)}, u32[]{:S(2)}, u32[]{:S(2)}) %all-to-all-start.2) | async-done | bytes 1048608 | tf_op jit(solution)/shard_map/all_to_all | solution.py:93
  147.3 12.8 %all-to-all-done.3 = bf16[8,64,512]{2,1,0:T(8,128)(2,1)S(1)} async-done(((bf16[8,64,512]{2,1,0:T(8,128)(2,1)}), bf16[8,64,512]{2,1,0:T(8,128)(2,1)S(1)}, u32[]{:S(2)}, u32[]{:S(2)}) %all-to-all-start.3) | async-done | bytes 524320 | tf_op jit(solution)/shard_map/all_to_all | solution.py:219
  167.3 11.3 all-to-all-done.8
  184.8 11.2 scatter_fusion.1
  208.6 67.2 %all-to-all-done.4 = f32[8,64,2048]{2,1,0:T(8,128)} async-done(((f32[8,64,2048]{2,1,0:T(8,128)}), f32[8,64,2048]{2,1,0:T(8,128)}, u32[]{:S(2)}, u32[]{:S(2)}) %all-to-all-start.4) | async-done | bytes 4194336 | tf_op jit(solution)/shard_map/all_to_all | solution.py:97
  295.6 37.6 %all-reduce.13.cloned.1.call-done = f32[128,2048]{1,0:T(8,128)} async-done(((f32[128,2048]{1,0:T(8,128)}), f32[128,2048]{1,0:T(8,128)}) %all-reduce.13.cloned.1.call-update) | async-done | bytes 1048592 | tf_op jit(solution)/shard_map/psum | solution.py:105
  339.1 5.8 all-to-all-start.5
  344.9 8.3 fusion.2
  353.2 39.5 %all-to-all-done.5 = bf16[8,64,2048]{2,1,0:T(8,128)(2,1)} async-done(((bf16[8,64,2048]{2,1,0:T(8,128)(2,1)}), bf16[8,64,2048]{2,1,0:T(8,128)(2,1)}, u32[]{:S(2)}, u32[]{:S(2)}) %all-to-all-start.5) | async-done | bytes 2097184 | tf_op jit(solution)/shard_map/all_to_all | solution.py:232
  392.8 6.5 fusion.6
  399.4 9.1 multiply_convert_fusion.1
  421.8 92.3 %all-to-all-done.10 = f32[8,64,2048]{2,1,0:T(8,128)} async-done(((f32[8,64,2048]{2,1,0:T(8,128)}), f32[8,64,2048]{2,1,0:T(8,128)}, u32[]{:S(2)}, u32[]{:S(2)}) %all-to-all-start.10) | async-done | bytes 4194336 | tf_op jit(solution)/shard_map/all_to_all | solution.py:101
  528.6 34.8 %all-reduce.15.cloned.1.call-done = f32[128,2048]{1,0:T(8,128)} async-done(((f32[128,2048]{1,0:T(8,128)}), f32[128,2048]{1,0:T(8,128)}) %all-reduce.15.cloned.1.call-update) | async-done | bytes 1048592 | tf_op jit(solution)/shard_map/psum | solution.py:105
  578.3 53.4 %all_to_all.81 = bf16[8,64,2048]{2,1,0:T(8,128)(2,1)S(1)} all-to-all(bf16[8,64,2048]{2,1,0:T(8,128)(2,1)} %bitcast.224), channel_id=1, replica_groups=mesh['dp'=8,'tensor'=4] {'dp'}, dimensions={0} | all-to-all | bytes 4194304 | tf_op jit(solution)/shard_map/all_to_all | solution.py:294
  639.0 14.0 %all-to-all-done.12 = bf16[8,64,512]{2,1,0:T(8,128)(2,1)S(1)} async-done(((bf16[8,64,512]{2,1,0:T(8,128)(2,1)}), bf16[8,64,512]{2,1,0:T(8,128)(2,1)S(1)}, u32[]{:S(2)}, u32[]{:S(2)}) %all-to-all-start.12) | async-done | bytes 524320 | tf_op jit(solution)/shard_map/all_to_all | solution.py:97
  665.2 8.5 fusion
  688.8 86.9 %all-to-all-done.6 = f32[8,64,2048]{2,1,0:T(8,128)} async-done(((f32[8,64,2048]{2,1,0:T(8,128)}), f32[8,64,2048]{2,1,0:T(8,128)}, u32[]{:S(2)}, u32[]{:S(2)}) %all-to-all-start.6) | async-done | bytes 4194336 | tf_op jit(solution)/shard_map/all_to_all | solution.py:101
  780.3 5.9 gather_fusion.7
  800.2 72.6 %all-to-all-done.14 = f32[8,64,2048]{2,1,0:T(8,128)} async-done(((f32[8,64,2048]{2,1,0:T(8,128)}), f32[8,64,2048]{2,1,0:T(8,128)}, u32[]{:S(2)}, u32[]{:S(2)}) %all-to-all-start.14) | async-done | bytes 4194336 | tf_op jit(solution)/shard_map/all_to_all | solution.py:93
  872.8 5.9 gather_fusion.17
  895.9 9.8 convolution_bitcast_fusion
  905.7 8.0 convolution_bitcast_fusion.2
  913.7 28.4 %all-reduce.19.cloned.1.call-done = (f32[128,2048]{1,0:T(8,128)}, f32[128,2048]{1,0:T(8,128)}) async-done(((f32[128,2048]{1,0:T(8,128)}, f32[128,2048]{1,0:T(8,128)}), (f32[128,2048]{1,0:T(8,128)}, f32[128,2048]{1,0:T(8,128)})) %all-reduce.19.cloned.1.call-update) | async-done | bytes 2097168 | tf_op jit(solution)/shard_map/psum | solution.py:105
  952.7 10.1 convolution_bitcast_fusion.1
  964.6 17.8 %all-to-all-done.15 = bf16[8,16,2048]{2,1,0:T(8,128)(2,1)S(1)} async-done(((bf16[8,16,2048]{2,1,0:T(8,128)(2,1)}), bf16[8,16,2048]{2,1,0:T(8,128)(2,1)S(1)}, u32[]{:S(2)}, u32[]{:S(2)}) %all-to-all-start.15) | async-done | bytes 524320 | tf_op jit(solution)/shard_map/all_to_all | solution.py:353
  996.3 128.9 %all-reduce.17.cloned.1.call-done = bf16[2048,2,512]{2,0,1:T(8,128)(2,1)} async-done(((bf16[2048,2,512]{2,0,1:T(8,128)(2,1)}), bf16[2048,2,512]{2,0,1:T(8,128)(2,1)}) %all-reduce.17.cloned.1.call-update) | async-done | bytes 4194320 | tf_op jit(solution)/shard_map/psum | solution.py:345
  1125.1 9.8 copy.116
  1134.9 19.4 %all-reduce.7 = (bf16[2048]{0:T(1024)(128)(2,1)S(1)}, bf16[2048]{0:T(1024)(128)(2,1)S(1)}) all-reduce(bf16[2048]{0:T(1024)(128)(2,1)S(1)} %get-tuple-element.46, bf16[2048]{0:T(1024)(128)(2,1)S(1)} %copy-done.42), channel_id=1, replica_groups=mesh['dp'=8,'tensor'=4] {'dp'}, use_global_device_ids=true, to_apply=%region_31.32 | all-reduce | flops 4096 | bytes 16384 | tf_op jit(solution)/shard_map/psum | solution.py:346
  (330 shorter events, 246.0 us)
Async XLA Ops:
  7.2 156.9 %copy-start = (bf16[1,512,2048]{2,1,0:T(8,128)(2,1)S(1)}, bf16[1,512,2048]{2,1,0:T(8,128)(2,1)}, u32[]{:S(2)}) copy-start(bf16[1,512,2048]{2,1,0:T(8,128)(2,1)} %param.27) | copy-start | bytes 6291460
  14.5 24.4 %all-to-all-start = ((bf16[8,16,2048]{2,1,0:T(8,128)(2,1)}), bf16[8,16,2048]{2,1,0:T(8,128)(2,1)S(1)}, u32[]{:S(2)}, u32[]{:S(2)}) async-start(bf16[8,16,2048]{2,1,0:T(8,128)(2,1)} %bitcast.2), calls=%async_computation | async-start | bytes 1048576 | tf_op jit(solution)/shard_map/all_to_all | solution.py:158
  45.3 53.9 %all-to-all-start.1 = ((bf16[8,64,2048]{2,1,0:T(8,128)(2,1)}), bf16[8,64,2048]{2,1,0:T(8,128)(2,1)}, u32[]{:S(2)}, u32[]{:S(2)}) async-start(bf16[8,64,2048]{2,1,0:T(8,128)(2,1)} %bitcast.222), calls=%async_computation.1 | async-start | bytes 4194304 | tf_op jit(solution)/shard_map/all_to_all | solution.py:192
  51.7 81.5 %copy-start.40 = (s32[1024]{0:T(1024)}, s32[1024]{0:T(1024)S(1)}, u32[]{:S(2)}) copy-start(s32[1024]{0:T(1024)S(1)} %pad_clamp_fusion.6) | copy-start | bytes 12292
  103.7 29.6 %all-to-all-start.2 = ((f32[8,64,512]{2,1,0:T(8,128)}), f32[8,64,512]{2,1,0:T(8,128)S(1)}, u32[]{:S(2)}, u32[]{:S(2)}) async-start(f32[8,64,512]{2,1,0:T(8,128)} %fusion.31), calls=%async_computation.2 | async-start | bytes 2097152 | tf_op jit(solution)/shard_map/all_to_all | solution.py:93
  116.5 20.3 %copy-start.24 = (bf16[128,4,64]{2,0,1:T(8,128)(2,1)}, bf16[128,4,64]{2,0,1:T(8,128)(2,1)S(1)}, u32[]{:S(2)}) copy-start(bf16[128,4,64]{2,0,1:T(8,128)(2,1)S(1)} %get-tuple-element.61) | copy-start | bytes 196612
  141.8 18.3 %all-to-all-start.3 = ((bf16[8,64,512]{2,1,0:T(8,128)(2,1)}), bf16[8,64,512]{2,1,0:T(8,128)(2,1)S(1)}, u32[]{:S(2)}, u32[]{:S(2)}) async-start(bf16[8,64,512]{2,1,0:T(8,128)(2,1)} %bitcast.230), calls=%async_computation.3 | async-start | bytes 1048576 | tf_op jit(solution)/shard_map/all_to_all | solution.py:219
  160.2 18.5 %all-to-all-start.8 = ((bf16[8,16,2048]{2,1,0:T(8,128)(2,1)}), bf16[8,16,2048]{2,1,0:T(8,128)(2,1)S(1)}, u32[]{:S(2)}, u32[]{:S(2)}) async-start(bf16[8,16,2048]{2,1,0:T(8,128)(2,1)} %bitcast.228), calls=%async_computation.8 | async-start | bytes 1048576 | tf_op jit(solution)/shard_map/all_to_all | solution.py:165
  178.7 97.1 %all-to-all-start.4 = ((f32[8,64,2048]{2,1,0:T(8,128)}), f32[8,64,2048]{2,1,0:T(8,128)}, u32[]{:S(2)}, u32[]{:S(2)}) async-start(f32[8,64,2048]{2,1,0:T(8,128)} %fusion.27), calls=%async_computation.4 | async-start | bytes 8388608 | tf_op jit(solution)/shard_map/all_to_all | solution.py:97
  275.8 63.3 %all-to-all-start.9 = ((bf16[8,64,2048]{2,1,0:T(8,128)(2,1)}), bf16[8,64,2048]{2,1,0:T(8,128)(2,1)}, u32[]{:S(2)}, u32[]{:S(2)}) async-start(bf16[8,64,2048]{2,1,0:T(8,128)(2,1)} %bitcast.221), calls=%async_computation.9 | async-start | bytes 4194304 | tf_op jit(solution)/shard_map/all_to_all | solution.py:251
  280.3 52.9 %all-reduce.13.cloned.1.call-start = ((), (), s32[]{:S(2)}) async-start(), calls=%async_computation.16 | async-start | bytes 2097152 | tf_op jit(solution)/shard_map/psum | solution.py:105
  289.7 43.5 %copy-start.7 = (bf16[128,2048]{1,0:T(8,128)(2,1)S(1)}, bf16[128,2048]{1,0:T(8,128)(2,1)}, u32[]{:S(2)}) copy-start(bf16[128,2048]{1,0:T(8,128)(2,1)} %copy-done.6) | copy-start | bytes 1572868
  295.5 40.1 %copy-start.32 = (f32[2048]{0:T(1024)S(1)}, f32[2048]{0:T(1024)}, u32[]{:S(2)}) copy-start(f32[2048]{0:T(1024)} %param.28) | copy-start | bytes 24580
  339.1 53.7 %all-to-all-start.5 = ((bf16[8,64,2048]{2,1,0:T(8,128)(2,1)}), bf16[8,64,2048]{2,1,0:T(8,128)(2,1)}, u32[]{:S(2)}, u32[]{:S(2)}) async-start(bf16[8,64,2048]{2,1,0:T(8,128)(2,1)} %bitcast.223), calls=%async_computation.5 | async-start | bytes 4194304 | tf_op jit(solution)/shard_map/all_to_all | solution.py:232
  416.9 97.1 %all-to-all-start.10 = ((f32[8,64,2048]{2,1,0:T(8,128)}), f32[8,64,2048]{2,1,0:T(8,128)}, u32[]{:S(2)}, u32[]{:S(2)}) async-start(f32[8,64,2048]{2,1,0:T(8,128)} %bitcast.225), calls=%async_computation.10 | async-start | bytes 8388608 | tf_op jit(solution)/shard_map/all_to_all | solution.py:101
  421.5 141.9 %all-reduce.15.cloned.1.call-start = ((), (), s32[]{:S(2)}) async-start(), calls=%async_computation.17 | async-start | bytes 2097152 | tf_op jit(solution)/shard_map/psum | solution.py:105
  421.7 98.1 %copy-start.44 = (s32[1024]{0:T(1024)}, s32[1024]{0:T(1024)S(1)}, u32[]{:S(2)}) copy-start(s32[1024]{0:T(1024)S(1)} %pad_clamp_fusion.3) | copy-start | bytes 12292
  523.3 40.2 %copy-start.4 = (f32[128,2048]{1,0:T(8,128)S(1)}, f32[128,2048]{1,0:T(8,128)}, u32[]{:S(2)}) copy-start(f32[128,2048]{1,0:T(8,128)} %copy-done.3) | copy-start | bytes 3145732
  635.1 21.0 %copy-start.10 = (f32[2,4,128,128]{2,3,0,1:T(8,128)S(1)}, f32[2,4,128,128]{2,3,0,1:T(8,128)}, u32[]{:S(2)}) copy-start(f32[2,4,128,128]{2,3,0,1:T(8,128)} %copy-done.9) | copy-start | bytes 1572868
  635.1 17.9 %all-to-all-start.12 = ((bf16[8,64,512]{2,1,0:T(8,128)(2,1)}), bf16[8,64,512]{2,1,0:T(8,128)(2,1)S(1)}, u32[]{:S(2)}, u32[]{:S(2)}) async-start(bf16[8,64,512]{2,1,0:T(8,128)(2,1)} %fusion.25), calls=%async_computation.12 | async-start | bytes 1048576 | tf_op jit(solution)/shard_map/all_to_all | solution.py:97
  661.1 18.0 %all-to-all-start.13 = ((bf16[8,64,512]{2,1,0:T(8,128)(2,1)}), bf16[8,64,512]{2,1,0:T(8,128)(2,1)}, u32[]{:S(2)}, u32[]{:S(2)}) async-start(bf16[8,64,512]{2,1,0:T(8,128)(2,1)} %bitcast.229), calls=%async_computation.13 | async-start | bytes 1048576 | tf_op jit(solution)/shard_map/all_to_all | solution.py:330
  679.1 96.5 %all-to-all-start.6 = ((f32[8,64,2048]{2,1,0:T(8,128)}), f32[8,64,2048]{2,1,0:T(8,128)}, u32[]{:S(2)}, u32[]{:S(2)}) async-start(f32[8,64,2048]{2,1,0:T(8,128)} %fusion), calls=%async_computation.6 | async-start | bytes 8388608 | tf_op jit(solution)/shard_map/all_to_all | solution.py:101
  775.7 97.1 %all-to-all-start.14 = ((f32[8,64,2048]{2,1,0:T(8,128)}), f32[8,64,2048]{2,1,0:T(8,128)}, u32[]{:S(2)}, u32[]{:S(2)}) async-start(f32[8,64,2048]{2,1,0:T(8,128)} %fusion.29), calls=%async_computation.14 | async-start | bytes 8388608 | tf_op jit(solution)/shard_map/all_to_all | solution.py:93
  780.3 161.8 %all-reduce.19.cloned.1.call-start = ((), (), s32[]{:S(2)}) async-start(), calls=%async_computation.19 | async-start | bytes 4194304 | tf_op jit(solution)/shard_map/psum | solution.py:105
  891.0 234.1 %all-reduce.17.cloned.1.call-start = ((), (), s32[]{:S(2)}) async-start(), calls=%async_computation.18 | async-start | bytes 8388608 | tf_op jit(solution)/shard_map/psum | solution.py:345
  905.7 36.4 %copy-start.8 = (bf16[128,2048]{1,0:T(8,128)(2,1)S(1)}, bf16[128,2048]{1,0:T(8,128)(2,1)}, u32[]{:S(2)}) copy-start(bf16[128,2048]{1,0:T(8,128)(2,1)} %copy-done.6) | copy-start | bytes 1572868
  905.7 36.4 %copy-start.34 = (f32[2048]{0:T(1024)S(1)}, f32[2048]{0:T(1024)}, u32[]{:S(2)}) copy-start(f32[2048]{0:T(1024)} %param.24) | copy-start | bytes 24580
  905.7 36.4 %copy-start.48 = (f32[128]{0:T(128)S(1)}, f32[128]{0:T(128)}, u32[]{:S(2)}) copy-start(f32[128]{0:T(128)} %copy-done.47) | copy-start | bytes 1540
  905.7 38.0 %copy-start.53 = (f32[128]{0:T(128)S(1)}, f32[128]{0:T(128)}, u32[]{:S(2)}) copy-start(f32[128]{0:T(128)} %get-tuple-element.80) | copy-start | bytes 1540
  947.2 35.3 %all-to-all-start.15 = ((bf16[8,16,2048]{2,1,0:T(8,128)(2,1)}), bf16[8,16,2048]{2,1,0:T(8,128)(2,1)S(1)}, u32[]{:S(2)}, u32[]{:S(2)}) async-start(bf16[8,16,2048]{2,1,0:T(8,128)(2,1)} %bitcast.227), calls=%async_computation.15 | async-start | bytes 1048576 | tf_op jit(solution)/shard_map/all_to_all | solution.py:353
  982.4 174.8 %all-to-all-start.7 = ((bf16[8,16,2048]{2,1,0:T(8,128)(2,1)}), bf16[8,16,2048]{2,1,0:T(8,128)(2,1)S(1)}, u32[]{:S(2)}, u32[]{:S(2)}) async-start(bf16[8,16,2048]{2,1,0:T(8,128)(2,1)} %bitcast.226), calls=%async_computation.7 | async-start | bytes 1048576 | tf_op jit(solution)/shard_map/all_to_all | solution.py:352
  996.3 138.6 %copy-start.42 = (bf16[2048]{0:T(1024)(128)(2,1)S(1)}, bf16[2048]{0:T(1024)(128)(2,1)}, u32[]{:S(2)}) copy-start(bf16[2048]{0:T(1024)(128)(2,1)} %get-tuple-element.44) | copy-start | bytes 12292
  (54 other events, 291.5 us)
Sparse Core Ops, SparseCore 0:
  25.5 2.2 sort.39.cloned.1.call-done
  295.6 37.5 all-reduce.12
  528.6 34.7 all-reduce.14
  891.1 50.8 all-reduce.18
  946.6 178.4 all-reduce.16
  (1 shorter events, 0.0 us)
where the time goes:
time: 1180 us; the launch traced here: 1170 us
  waiting for transfers between devices  714 us (61%)
  local copies, waits for them, and re-layouts  141 us (12%)
  matrix products  109 us (9%)
  blocking collectives  72.8 us (6%)
  starting transfers between devices  70.7 us (6%)
  other arithmetic  43.5 us (4%)
  between operations  15.2 us (1%)
    all_to_all x2, waiting for transfers between devices, expert_return(): return lax.all_to_all(pieces, 'dp', split_axis=0, concat_axis=0, tiled=True)  179 us
    psum x1, waiting for transfers between devices, local(): lax.psum(w_kv_grad.astype(jnp.bfloat16), 'dp').astype(jnp.float32)  129 us
    psum x3, waiting for transfers between devices, tensor_total(): return lax.psum(pieces, 'tensor')  101 us
    all_to_all x2, waiting for transfers between devices, query_return(): return lax.all_to_all(pieces, 'dp', split_axis=0, concat_axis=0, tiled=True)  89.3 us
    all_to_all x2, waiting for transfers between devices, output_return(): return lax.all_to_all(pieces, 'dp', split_axis=0, concat_axis=0, tiled=True)  81.1 us
    all_to_all x1, blocking collectives, local(): lax.all_to_all(send_slices(att_grad, att_table, group_size), 'dp', split_...  53.4 us
    all_to_all x1, waiting for transfers between devices, local(): lax.all_to_all(send_slices(normed, att_table // 2, group_size), 'dp', spl...  47.5 us
    all_to_all x1, waiting for transfers between devices, local(): lax.all_to_all(expert_sent, 'dp', split_axis=0, concat_axis=0, tiled=True)  39.5 us
  transfers between devices with their start and end apart: 19, of which 16 were waited for; matrix products, arithmetic and copies ran while one was open for 16% of the time, Pallas kernels for 0%

commit v1 on v0

--- a/solution.py
+++ b/solution.py
@@ -1,8 +1,11 @@
+import functools
 import math
 
 import jax
 import jax.numpy as jnp
 from jax import lax
+from jax.experimental import pallas as pl
+from jax.experimental.pallas import tpu as pltpu
 from jax.sharding import PartitionSpec as P
 
 HD = 128
@@ -368,6 +371,366 @@
     )
 
 
+MESH = pl.DeviceIdType.MESH
+VM = pltpu.VMEM
+DMA = pltpu.SemaphoreType.DMA
+BF = jnp.bfloat16
+F32 = jnp.float32
+
+def rcopy(src, dst, ss, rs, dp, tn):
+    return pltpu.make_async_remote_copy(src_ref=src, dst_ref=dst, send_sem=ss, recv_sem=rs,
+        device_id={"dp": dp, "tensor": tn}, device_id_type=MESH)
+
+def greet(targets):
+    b = pltpu.get_barrier_semaphore()
+    for dp, tn in targets:
+        pl.semaphore_signal(b, inc=1, device_id={"dp": dp, "tensor": tn}, device_id_type=MESH)
+    pl.semaphore_wait(b, len(targets))
+
+def ranks():
+    g = lax.axis_index("dp"); t = lax.axis_index("tensor")
+    return g, t, lax.rem(t + 2, 4), t + 1 - 2 * lax.rem(t, 2)
+
+def params(cid):
+    return pltpu.CompilerParams(collective_id=cid, has_side_effects=True, vmem_limit_bytes=56*2**20)
+
+def gather_body(n, mode, src, out, ssem, rsem, xs, xr, cs, cr, c2s, c2r, lsem):
+    g, t, tx, tc = ranks()
+    w = src.shape[-1]
+    greet([(lax.rem(g + o, n), t) for o in range(1, n)] + [(g, tx), (g, tc)])
+    cols = pl.ds(pl.multiple_of(t * w, w), w)
+    colsx = pl.ds(pl.multiple_of(tx * w, w), w)
+    pick = (lambda d: src.at[d]) if mode == "rows" else (lambda d: src)
+    at = (lambda b, cc: out.at[:, b, :, cc]) if mode == "deal" else (lambda b, cc: out.at[b, :, cc])
+    sends = []
+    for o in range(1, n):
+        d = lax.rem(g + o, n)
+        c = rcopy(pick(d), at(g, cols), ssem.at[o], rsem.at[o], d, t)
+        c.start(); sends.append(c)
+    loc = pltpu.make_async_copy(pick(g), at(g, cols), lsem)
+    loc.start(); loc.wait()
+    fx = []; fc = []; fc2 = []
+    for o in range(n):
+        b = lax.rem(g - o + n, n)
+        if o > 0: sends[o - 1].wait_recv()
+        c = rcopy(at(b, cols), at(b, cols), xs.at[o], xr.at[o], g, tx); c.start(); fx.append(c)
+        c = rcopy(at(b, cols), at(b, cols), cs.at[o], cr.at[o], g, tc); c.start(); fc.append(c)
+    for o in range(n):
+        b = lax.rem(g - o + n, n)
+        fx[o].wait_recv()
+        c = rcopy(at(b, colsx), at(b, colsx), c2s.at[o], c2r.at[o], g, tc); c.start(); fc2.append(c)
+    for c in fc + fc2: c.wait_recv()
+    for c in sends + fx + fc + fc2: c.wait_send()
+
+def gather(src, n, bcast=False, deal=False, cid=0, space=VM):
+    r, w = src.shape[-2:]
+    mode = "deal" if deal else "copy" if bcast else "rows"
+    shape = (n, n, r, 4 * w) if deal else (n, r, 4 * w)
+    return pl.pallas_call(functools.partial(gather_body, n, mode),
+        out_shape=jax.ShapeDtypeStruct(shape, src.dtype),
+        in_specs=[pl.BlockSpec(memory_space=VM)], out_specs=pl.BlockSpec(memory_space=space),
+        scratch_shapes=[DMA((n,))]*8 + [DMA],
+        name="gather_rows", compiler_params=params(cid))(src)
+
+def reduce_body(n, nb, src, out, cbuf, cin, xbuf, xin, dbuf, cs, cr, xs, xr, ds_, dr):
+    g, t, tx, tc = ranks()
+    tcx = lax.rem(tc + 2, 4); w = out.shape[-1]
+    greet([(lax.rem(g + o, n), t) for o in range(1, n)] + [(g, tx), (g, tc)])
+    sl = lambda q: pl.ds(pl.multiple_of(q * w, w), w)
+    order = list(range(1, n)) + [0] + list(range(n, nb))
+    at = lambda o: lax.rem(g + o, n) if o < n else o
+    C = {}; X = {}; Dd = {}
+    for o in order:
+        d = at(o)
+        cbuf[o, 0] = src[d, :, sl(tc)].astype(BF)
+        cbuf[o, 1] = src[d, :, sl(tcx)].astype(BF)
+        C[o] = rcopy(cbuf.at[o], cin.at[o], cs.at[o], cr.at[o], g, tc); C[o].start()
+    for o in order:
+        C[o].wait_recv()
+        xbuf[o] = (src[at(o), :, sl(tx)] + cin[o, 1].astype(F32)).astype(BF)
+        X[o] = rcopy(xbuf.at[o], xin.at[o], xs.at[o], xr.at[o], g, tx); X[o].start()
+    for o in order:
+        d = at(o)
+        X[o].wait_recv()
+        total = (src[d, :, sl(t)] + cin[o, 0].astype(F32) + xin[o].astype(F32)).astype(BF)
+        if 0 < o < n:
+            dbuf[o] = total
+            Dd[o] = rcopy(dbuf.at[o], out.at[g], ds_.at[o], dr.at[o], d, t); Dd[o].start()
+        elif o == 0:
+            out[g] = total
+        else:
+            out[o] = total
+    for c in Dd.values(): c.wait_recv()
+    for c in list(C.values()) + list(X.values()) + list(Dd.values()): c.wait_send()
+
+def reduce(src, n, cid=1):
+    nb, r, w = src.shape; w //= 4
+    return pl.pallas_call(functools.partial(reduce_body, n, nb),
+        out_shape=jax.ShapeDtypeStruct((nb, r, w), BF),
+        in_specs=[pl.BlockSpec(memory_space=VM)], out_specs=pl.BlockSpec(memory_space=VM),
+        scratch_shapes=[VM((nb,2,r,w),BF), VM((nb,2,r,w),BF), VM((nb,r,w),BF), VM((nb,r,w),BF), VM((n,r,w),BF)] + [DMA((nb,))]*4 + [DMA((n,))]*2,
+        name="reduce_rows", compiler_params=params(cid))(src)
+
+def a2a_body(n, src, out, ss, rs):
+    g, t, tx, tc = ranks()
+    greet([(lax.rem(g + o, n), t) for o in range(1, n)])
+    cs = []
+    for o in range(1, n):
+        d = lax.rem(g + o, n)
+        c = rcopy(src.at[d], out.at[g], ss.at[o], rs.at[o], d, t); c.start(); cs.append(c)
+    out[g] = src[g]
+    for c in cs: c.wait()
+
+def a2a(src, n, cid=2):
+    return pl.pallas_call(functools.partial(a2a_body, n),
+        out_shape=jax.ShapeDtypeStruct(src.shape, src.dtype),
+        in_specs=[pl.BlockSpec(memory_space=VM)], out_specs=pl.BlockSpec(memory_space=VM),
+        scratch_shapes=[DMA((n,))]*2,
+        name="a2a_rows", compiler_params=params(cid))(src)
+
+def a2a_copy_body(n, src, out, ss, rs):
+    g, t, tx, tc = ranks()
+    greet([(lax.rem(g + o, n), t) for o in range(1, n)])
+    cs = []
+    for o in range(1, n):
+        d = lax.rem(g + o, n)
+        c = rcopy(src, out.at[g], ss.at[o], rs.at[o], d, t); c.start(); cs.append(c)
+    out[g] = src[...]
+    for c in cs: c.wait()
+
+def a2a_copy(src, n, cid):
+    return pl.pallas_call(functools.partial(a2a_copy_body, n),
+        out_shape=jax.ShapeDtypeStruct((n,) + src.shape, src.dtype),
+        in_specs=[pl.BlockSpec(memory_space=VM)], out_specs=pl.BlockSpec(memory_space=VM),
+        scratch_shapes=[DMA((n,))]*2,
+        name="copy_rows", compiler_params=params(cid))(src)
+
+def dot(a, b, dims):
+    return lax.dot_general(a, b, dims, preferred_element_type=F32)
+
+
+def mm(a, b):
+    return dot(a, b, (((a.ndim - 1,), (0,)), ((), ())))
+
+
+def mm_t(a, b):
+    return dot(a, b, (((1,), (1,)), ((), ())))
+
+
+def mm_rows(a, b):
+    return dot(a, b, (((0,), (0,)), ((), ())))
+
+
+def slots_of(route_a, route_b, names, cap):
+    tokens = route_a.shape[-1]
+    member = (route_a == names) | (route_b == names)
+    before = (jnp.arange(tokens)[:, None] < jnp.arange(tokens)[None, :]).astype(BF)
+    rank = mm(member.astype(BF), before)
+    slot = jnp.arange(cap, dtype=F32)[None, :, None]
+    return ((rank[:, None, :] == slot) & member[:, None, :]).astype(BF)
+
+
+def slot_gate(table, route_a, route_b, gate_a, gate_b, names):
+    per_token = jnp.where(route_a == names, gate_a, 0.0) + jnp.where(route_b == names, gate_b, 0.0)
+    return jnp.sum(table.astype(F32) * per_token[:, None, :], axis=-1)
+
+
+def weigh(table, gates, rows):
+    slots = table.reshape(-1, table.shape[-1])
+    scaled = rows.reshape(slots.shape[0], -1).astype(F32) * gates.reshape(-1, 1)
+    high = scaled.astype(BF)
+    low = (scaled - high.astype(F32)).astype(BF)
+    return mm_rows(slots, high) + mm_rows(slots, low)
+
+
+def angles(positions):
+    half = HD // 2
+    frequency = jnp.exp(-math.log(THETA) * jnp.arange(half, dtype=F32) / half)
+    turned = positions[..., None] * frequency
+    return jnp.cos(turned)[..., None, :], jnp.sin(turned)[..., None, :]
+
+
+def turn(vectors, cosine, sine):
+    half = HD // 2
+    a, b = vectors[..., :half], vectors[..., half:]
+    return jnp.concatenate([a * cosine - b * sine, b * cosine + a * sine], axis=-1)
+
+
+def fast_local(
+    tokens, out_grad, row_place, seq_lengths, att_routes, att_gates, mlp_routes, mlp_gates,
+    gain_attn, w_kv, w_query, w_out, gain_mlp, w_gate, w_up, w_down,
+):
+    rows, features = tokens.shape
+    n = lax.axis_size("dp")
+    g, t = lax.axis_index("dp"), lax.axis_index("tensor")
+    width = features // 4
+    per = rows // n
+    heads = w_kv.shape[2] // HD
+    hw = heads * HD
+    part = lambda a: lax.dynamic_slice_in_dim(a, t * width, width, a.ndim - 1)
+    counting = jnp.arange(rows, dtype=jnp.int32)
+
+    place = row_place.reshape(n, rows)
+    group = place // rows
+    earlier = (group[:, :, None] == group[:, None, :]) & (counting[None, :] < counting[:, None])
+    arrival = jnp.sum(earlier.astype(jnp.int32), axis=-1)
+    mine = lax.dynamic_index_in_dim(group * per + arrival, g, 0, keepdims=False)
+    sorter = (mine[None, :] == counting[:, None]).astype(BF)
+    x_sorted = mm(sorter, part(tokens)).astype(BF).reshape(n, per, width)
+    dy_sorted = mm(sorter, part(out_grad)).astype(BF).reshape(n, per, width)
+    x_all = gather(x_sorted, n, deal=True, cid=1).reshape(n, rows, features)
+
+    here = (group == g) & True
+    spot = (jnp.arange(n, dtype=jnp.int32)[:, None] * per + arrival)
+    work_of = jnp.sum(
+        jnp.where(here[None] & (spot[None] == counting[:, None, None]), place[None] % rows, 0), axis=(1, 2)
+    )
+    ends = jnp.cumsum(seq_lengths[0])
+    segment = jnp.sum((counting[:, None] >= ends[None, :]).astype(jnp.int32), axis=1)
+    begins = jnp.sum(
+        jnp.where(segment[:, None] == jnp.arange(ends.shape[0])[None, :], (ends - seq_lengths[0])[None, :], 0), axis=1
+    )
+    carried = jnp.stack(
+        [v.astype(F32) for v in (
+            att_routes[:, 0], att_routes[:, 1], att_gates[:, 0], att_gates[:, 1],
+            mlp_routes[:, 0], mlp_routes[:, 1], mlp_gates[:, 0], mlp_gates[:, 1],
+            counting - begins, segment, counting)] + [jnp.zeros((rows,), F32)] * 5)
+    moved = jnp.sum(
+        jnp.where(work_of[None, :, None] == counting[None, None, :], carried[:, None, :], 0.0), axis=2
+    )
+    meta_all = a2a_copy(moved, n, cid=8)
+    ar0, ar1, ag0, ag1, mr0, mr1, mg0, mg1, pos, seg, wpos = [meta_all[:, i] for i in range(11)]
+    me = g.astype(F32)
+    names = jnp.arange(n, dtype=F32)[:, None]
+    own = lambda a: lax.dynamic_index_in_dim(a, g, 0, keepdims=False)
+
+    att_in = slots_of(ar0, ar1, me, CAP)
+    att_in_gate = slot_gate(att_in, ar0, ar1, ag0, ag1, me)
+    mlp_in = slots_of(mr0, mr1, me, CAP)
+    mlp_in_gate = slot_gate(mlp_in, mr0, mr1, mg0, mg1, me)
+    o_ar0, o_ar1, o_ag0, o_ag1 = own(ar0)[None], own(ar1)[None], own(ag0)[None], own(ag1)[None]
+    o_mr0, o_mr1, o_mg0, o_mg1 = own(mr0)[None], own(mr1)[None], own(mg0)[None], own(mg1)[None]
+    att_out = slots_of(o_ar0, o_ar1, names, CAP)
+    att_out_gate = slot_gate(att_out, o_ar0, o_ar1, o_ag0, o_ag1, names)
+    mlp_out = slots_of(o_mr0, o_mr1, names, CAP)
+    mlp_out_gate = slot_gate(mlp_out, o_mr0, o_mr1, o_mg0, o_mg1, names)
+
+    xf = x_all.astype(F32)
+    scale_attn = inverse_rms(xf)
+    normed = (xf * scale_attn * gain_attn).astype(BF)
+    normed_flat = normed.reshape(n * rows, features)
+    kv = mm(normed_flat, w_kv.reshape(features, 2 * hw)).reshape(n, rows, 2, heads, HD)
+    key_cos, key_sin = angles(pos)
+    keys = turn(kv[:, :, 0], key_cos, key_sin).astype(BF)
+    values = kv[:, :, 1].astype(BF)
+    picked = jnp.einsum("gst,gtd->gsd", att_in, normed, preferred_element_type=F32).astype(BF)
+    picked = picked.reshape(n * CAP, features)
+    slot_pos = jnp.sum(att_in.astype(F32) * pos[:, None, :], axis=-1)
+    slot_seg = jnp.sum(att_in.astype(F32) * seg[:, None, :], axis=-1)
+    slot_wpos = jnp.sum(att_in.astype(F32) * wpos[:, None, :], axis=-1)
+    q_cos, q_sin = angles(slot_pos)
+    query = turn(mm(picked, w_query[0]).reshape(n, CAP, heads, HD), q_cos, q_sin).astype(BF)
+    allowed = (slot_seg[:, :, None] == seg[:, None, :]) & (wpos[:, None, :] <= slot_wpos[:, :, None])
+    root = math.sqrt(HD)
+    scores = jnp.einsum("gshd,gmhd->ghsm", query, keys, preferred_element_type=F32) / root
+    scores = jnp.where(allowed[:, None], scores, -1e30)
+    probs = jax.nn.softmax(scores, axis=-1)
+    probs_low = probs.astype(BF)
+    attn = jnp.einsum("ghsm,gmhd->gshd", probs_low, values, preferred_element_type=F32)
+    attn = attn.astype(BF).reshape(n * CAP, hw)
+    query_back = lax.all_to_all(query.reshape(n, CAP, hw), "dp", split_axis=0, concat_axis=0, tiled=True)
+    obr = reduce(mm(attn, w_out[0]).reshape(n, CAP, features), n, cid=2)
+    x_own = part(own(x_all)).astype(F32)
+    hidden = x_own + weigh(att_out, att_out_gate, obr)
+
+    mlp_rows = mlp_out.reshape(n * CAP, rows)
+    hid_rows = gather(mm(mlp_rows, hidden.astype(BF)).astype(BF).reshape(n, CAP, width), n, cid=0)
+    dy_all = gather(dy_sorted, n, deal=True, cid=1).reshape(n, rows, features)
+    d_mbr = jnp.einsum("gst,gtd->gsd", mlp_in, dy_all, preferred_element_type=F32) * mlp_in_gate[..., None]
+    d_mbr = d_mbr.astype(BF).reshape(n * CAP, features)
+    hid_rows = hid_rows.reshape(n * CAP, features).astype(F32)
+    normed2 = (hid_rows * inverse_rms(hid_rows) * gain_mlp).astype(BF)
+    gate_map, up_map, down_map = w_gate[0], w_up[0], w_down[0]
+    gate_act = mm(normed2, gate_map)
+    up_act = mm(normed2, up_map)
+    sigmoid_g = jax.nn.sigmoid(gate_act)
+    inner = (gate_act * sigmoid_g * up_act).astype(BF)
+    d_inner = mm_t(d_mbr, down_map)
+    d_up = (d_inner * gate_act * sigmoid_g).astype(BF)
+    d_gate = (d_inner * up_act * sigmoid_g * (1.0 + gate_act * (1.0 - sigmoid_g))).astype(BF)
+    d_rows = mm_t(d_gate, gate_map) + mm_t(d_up, up_map)
+    d_pairs = reduce(d_rows.reshape(n, CAP, features), n, cid=2)
+    mbr = reduce(mm(inner, down_map).reshape(n, CAP, features), n, cid=2)
+    mixed_rows = hidden + weigh(mlp_out, mlp_out_gate, mbr)
+    w_gate_grad = mm_rows(normed2, d_gate)[None]
+    w_up_grad = mm_rows(normed2, d_up)[None]
+    w_down_grad = mm_rows(inner, d_mbr)[None]
+    d_normed2 = mm_rows(mlp_rows, d_pairs.reshape(n * CAP, width))
+    gain_mlp_t, gain_attn_t = part(gain_mlp), part(gain_attn)
+    dy_own = part(own(dy_all)).astype(F32)
+    e2 = gain_mlp_t * d_normed2
+    square, inner_sum = lax.psum(
+        (jnp.sum(hidden * hidden, axis=1, keepdims=True), jnp.sum(hidden * e2, axis=1, keepdims=True)), "tensor")
+    scale_mlp = lax.rsqrt(square / features + EPSILON)
+    d_hidden = dy_own + scale_mlp * e2 - hidden * (scale_mlp * scale_mlp * scale_mlp) * (inner_sum / features)
+    gain_mlp_part = jnp.sum(d_normed2 * hidden * scale_mlp, axis=0)
+
+    att_rows = att_out.reshape(n * CAP, rows)
+    d_obr = gather(mm(att_rows, d_hidden.astype(BF)).astype(BF).reshape(n, CAP, width), n, cid=0)
+    d_obr = (d_obr.astype(F32) * att_in_gate[..., None]).astype(BF).reshape(n * CAP, features)
+    d_attn = mm_t(d_obr, w_out[0]).astype(BF).reshape(n, CAP, heads, HD)
+    d_attn_back = a2a(d_attn.reshape(n, CAP, hw), n, cid=4)
+    w_out_grad = mm_rows(attn, d_obr)[None]
+    d_probs = jnp.einsum("gshd,gmhd->ghsm", d_attn, values, preferred_element_type=F32)
+    delta = jnp.sum(d_probs * probs, axis=-1, keepdims=True)
+    d_scores = (probs * (d_probs - delta)).astype(BF)
+    d_query = jnp.einsum("ghsm,gmhd->gshd", d_scores, keys, preferred_element_type=F32) / root
+    dq_pre = turn(d_query, q_cos, -q_sin).astype(BF).reshape(n * CAP, hw)
+    w_query_grad = mm_rows(picked, dq_pre)[None]
+    d_norm_q = mm_t(dq_pre, w_query[0]).reshape(n, CAP, features)
+
+    b_query = query_back.reshape(n * CAP, heads, HD)
+    b_d_attn = d_attn_back.reshape(n * CAP, heads, HD)
+    b_keys, b_values, b_seg, b_wpos = own(keys), own(values), own(seg), own(wpos)
+    r_seg = jnp.sum(att_rows.astype(F32) * b_seg[None, :], axis=-1)
+    r_wpos = jnp.sum(att_rows.astype(F32) * b_wpos[None, :], axis=-1)
+    b_allowed = (r_seg[:, None] == b_seg[None, :]) & (b_wpos[None, :] <= r_wpos[:, None])
+    b_scores = jnp.einsum("shd,mhd->hsm", b_query, b_keys, preferred_element_type=F32) / root
+    b_probs = jax.nn.softmax(jnp.where(b_allowed[None], b_scores, -1e30), axis=-1)
+    b_d_probs = jnp.einsum("shd,mhd->hsm", b_d_attn, b_values, preferred_element_type=F32)
+    b_delta = jnp.sum(b_d_probs * b_probs, axis=-1, keepdims=True)
+    b_d_scores = (b_probs * (b_d_probs - b_delta)).astype(BF)
+    d_values = jnp.einsum("hsm,shd->mhd", b_probs.astype(BF), b_d_attn, preferred_element_type=F32)
+    d_keys = jnp.einsum("hsm,shd->mhd", b_d_scores, b_query, preferred_element_type=F32) / root
+    d_keys = turn(d_keys, own(key_cos), -own(key_sin))
+    d_kv = jnp.concatenate([d_keys.reshape(rows, hw), d_values.reshape(rows, hw)], axis=1).astype(BF)
+    d_kv_all = a2a_copy(d_kv, n, cid=5)
+    w_kv_grad = mm_rows(normed_flat, d_kv_all.reshape(n * rows, 2 * hw)).reshape(features, 2, hw)
+    d_norm_kv = mm_t(d_kv, w_kv.reshape(features, 2 * hw)).reshape(rows // CAP, CAP, features)
+
+    d_norm = reduce(jnp.concatenate([d_norm_q, d_norm_kv], axis=0), n, cid=3)
+    d_normed = mm_rows(att_rows, d_norm[:n].reshape(n * CAP, width))
+    d_normed = d_normed + d_norm[n:].reshape(rows, width).astype(F32)
+    scale_own = own(scale_attn)
+    e1 = gain_attn_t * d_normed
+    sum_1 = lax.psum(jnp.sum(x_own * e1, axis=1, keepdims=True), "tensor")
+    in_grad = d_hidden + scale_own * e1 - x_own * (scale_own * scale_own * scale_own) * (sum_1 / features)
+    gain_attn_part = jnp.sum(d_normed * x_own * scale_own, axis=0)
+
+    gains = jnp.concatenate([gain_mlp_part[None], gain_attn_part[None], jnp.zeros((6, width), F32)], axis=0)
+    gains = jnp.sum(gather(gains, n, bcast=True, cid=7), axis=0)
+    back = jnp.concatenate(
+        [mixed_rows.astype(BF).reshape(n, per, width), in_grad.astype(BF).reshape(n, per, width)], axis=1
+    )
+    back = gather(back, n, cid=6)
+    mixed = mm_rows(sorter, back[:, :per].reshape(rows, features)).astype(BF)
+    tokens_grad = mm_rows(sorter, back[:, per:].reshape(rows, features)).astype(BF)
+    return (
+        mixed, tokens_grad, gains[1], w_kv_grad, w_query_grad, w_out_grad, gains[0],
+        w_gate_grad, w_up_grad, w_down_grad,
+    )
+
+
 def solution(mesh):
     placed = (
         P("dp", None),
@@ -387,8 +750,9 @@
         P("dp", None, "tensor"),
         P("dp", "tensor", None),
     )
+    dealt = mesh.shape["dp"] == EXPERTS and mesh.shape["tensor"] == 4
     return jax.shard_map(
-        local,
+        fast_local if dealt else local,
         mesh=mesh,
         in_specs=placed,
         out_specs=(

time: 1180 us -> 621 us (0.53)
  waiting for transfers between devices: 714 us -> 0.01 us
  Pallas kernels: 0 us -> 339 us
  local copies, waits for them, and re-layouts: 141 us -> 67.6 us
  starting transfers between devices: 70.7 us -> 7.8 us
  blocking collectives: 72.8 us -> 21.4 us
  matrix products: 109 us -> 122 us
  between operations: 15.2 us -> 2.23 us
    all_to_all x15 -> x1, waiting for transfers between devices: 484 us -> 0.01 us  [fast_local(): lax.all_to_all(query.reshape(n, CAP, hw), 'dp', split_axis=0, concat_axis...]
    pallas_call x0 -> x13, Pallas kernels: none -> 339 us  [the longest x6 157 us: gather(): pl.pallas_call(functools.partial(gather_body, n, mode), out_shape=jax.Sha...]
    psum x4 -> x0, waiting for transfers between devices: 230 us -> none  [the longest x1 129 us: local(): lax.psum(w_kv_grad.astype(jnp.bfloat16), 'dp').astype(jnp.float32)]
    all_to_all x15 -> x1, starting transfers between devices: 70.4 us -> 7.8 us  [fast_local(): lax.all_to_all(query.reshape(n, CAP, hw), 'dp', split_axis=0, concat_axis...]
    gather x23 -> x0, local copies, waits for them, and re-layouts: 60 us -> none  [the longest x6 18.4 us: pick_rows(): return padded[slot_table]]
    all_to_all x1 -> x0, blocking collectives: 53.4 us -> none  [local(): lax.all_to_all(send_slices(att_grad, att_table, group_size), 'dp', split_...]
    scatter x4 -> x0, local copies, waits for them, and re-layouts: 24.8 us -> none  [the longest x2 22.4 us: expert_slots(): slot_table.at[flattened, position]]
    reduce_sum x11 -> x10, other arithmetic: 25.1 us -> 6.84 us  [the longest x1 2.35 us: fast_local(): jnp.sum(jnp.where(here[None] & (spot[None] == counting[:, None, None]), p...]
  transfers between devices with their start and end apart: 19 -> 1, of which waited for: 16 -> 0; matrix products, arithmetic and copies ran while one was open for 16% -> 26% of each run, Pallas kernels for 0% -> 30%
where the time goes in v1:
time: 621 us; the launch traced here: 612 us
  Pallas kernels  339 us (55%)
  matrix products  122 us (20%)
  local copies, waits for them, and re-layouts  67.6 us (11%)
  other arithmetic  51.8 us (8%)
  blocking collectives  21.4 us (3%)
  starting transfers between devices  7.8 us (1%)
    pallas_call x6, Pallas kernels, gather(): pl.pallas_call(functools.partial(gather_body, n, mode), out_shape=jax.Sha...  157 us
    pallas_call x4, Pallas kernels, reduce(): pl.pallas_call(functools.partial(reduce_body, n, nb), out_shape=jax.Shape...  116 us
    dot_general x34, matrix products, dot(): return lax.dot_general(a, b, dims, preferred_element_type=F32)  101 us
    pallas_call x2, Pallas kernels, a2a_copy(): pl.pallas_call(functools.partial(a2a_copy_body, n), out_shape=jax.ShapeDt...  51.3 us
    unnamed x160, local copies, waits for them, and re-layouts  24.1 us
    psum x2, blocking collectives, fast_local(): lax.psum((jnp.sum(hidden * hidden, axis=1, keepdims=True), jnp.sum(hidden...  15.3 us
    pallas_call x1, Pallas kernels, a2a(): pl.pallas_call(functools.partial(a2a_body, n), out_shape=jax.ShapeDtypeSt...  15.2 us
    dot_general x3, local copies, waits for them, and re-layouts, dot(): return lax.dot_general(a, b, dims, preferred_element_type=F32)  13.2 us
  transfers between devices with their start and end apart: 1, of which 0 were waited for; matrix products, arithmetic and copies ran while one was open for 26% of the time, Pallas kernels for 30%

profile of v1, /device:TPU:0, one launch (start us, length us, event | category | flops | bytes accessed | tf_op | source)
XLA Modules:
  0.0 612.1 jit_solution(5159595581150721947)
XLA Ops:
  10.0 10.0 %copy_rows.2 = f32[8,16,128]{2,1,0:T(8,128)} custom-call(f32[16,128]{1,0:T(8,128)} %select_reduce_fusion.src), custom_call_target="tpu_custom_call" | custom-call | tf_op jit(solution)/shard_map/copy_rows/pallas_call | solution.py:502
  23.6 3.9 copy.109
  29.3 38.3 %gather_rows.6 = bf16[8,8,16,2048]{3,2,1,0:T(8,128)(2,1)} custom-call(bf16[8,16,512]{2,1,0:T(8,128)(2,1)} %bitcast.389), custom_call_target="tpu_custom_call" | custom-call | tf_op jit(solution)/shard_map/gather_rows/pallas_call | solution.py:429
  80.7 7.8 %all-to-all-start = ((bf16[8,64,512]{2,1,0:T(8,128)(2,1)}), bf16[8,64,512]{2,1,0:T(8,128)(2,1)}, u32[]{:S(2)}, u32[]{:S(2)}) async-start(bf16[8,64,512]{2,1,0:T(8,128)(2,1)} %copy_bitcast_fusion), calls=%async_computation | async-start | bytes 1048576 | tf_op jit(solution)/shard_map/all_to_all | solution.py:641
  93.9 5.4 fusion.4
  102.5 6.4 %copy.108 = bf16[1024,2048]{1,0:T(8,128)(2,1)} copy(bf16[1024,2048]{0,1:T(8,128)(2,1)} %bitcast.365) | data formatting | bytes 8388608 | tf_op jit(solution)/shard_map/dot_general | solution.py:509
  108.9 7.6 %fusion.209 = f32[8,128,2,4,128]{1,4,3,2,0:T(8,128)S(1)} fusion(bf16[8,128,2048,1,1]{2,1,4,3,0:T(8,128)(2,1)} %bitcast.370, bf16[2,4,128,2048,1]{3,2,1,0,4:T(8,128)(2,1)} %bitcast.373), kind=kOutput, calls=%fused_computation.346 | convolution fusion | flops 4294967296 | bytes 12582912 | tf_op jit(solution)/shard_map/dot_general | solution.py:509
  133.8 25.1 %reduce_rows.4 = bf16[8,64,512]{2,1,0:T(8,128)(2,1)} custom-call(f32[8,64,2048]{2,1,0:T(8,128)} %fusion.30.src), custom_call_target="tpu_custom_call" | custom-call | tf_op jit(solution)/shard_map/reduce_rows/pallas_call | solution.py:468
  165.3 24.1 %gather_rows.7 = bf16[8,64,2048]{2,1,0:T(8,128)(2,1)} custom-call(bf16[8,64,512]{2,1,0:T(8,128)(2,1)} %bitcast.378), custom_call_target="tpu_custom_call" | custom-call | tf_op jit(solution)/shard_map/gather_rows/pallas_call | solution.py:429
  197.4 41.5 %gather_rows.8 = bf16[8,8,16,2048]{3,2,1,0:T(8,128)(2,1)} custom-call(bf16[8,16,512]{2,1,0:T(8,128)(2,1)} %bitcast.388), custom_call_target="tpu_custom_call" | custom-call | tf_op jit(solution)/shard_map/gather_rows/pallas_call | solution.py:429
  239.0 7.6 %psum.21 = f32[128,1]{0,1:T(1,128)S(1)} all-reduce(f32[128,1]{0,1:T(1,128)S(1)} %bitcast.414), channel_id=1, replica_groups=mesh['dp'=8,'tensor'=4] {'tensor'}, use_global_device_ids=true, to_apply=%region_16.17 | all-reduce | flops 128 | bytes 1024 | tf_op jit(solution)/shard_map/psum | solution.py:672
  250.4 6.6 %fusion.7 = f32[512,1408]{1,0:T(8,128)S(1)} fusion(bf16[512,2048]{1,0:T(8,128)(2,1)S(1)} %bitcast.382, bf16[1,1408,2048]{2,1,0:T(8,128)(2,1)} %param.31), kind=kOutput, calls=%fused_computation.13 | convolution fusion | flops 2952790016 | bytes 10747904 | tf_op jit(solution)/shard_map/dot_general | solution.py:509
  260.5 5.4 multiply_convert_fusion.9
  269.4 5.0 fusion.22
  274.4 27.9 %reduce_rows.6 = bf16[8,64,512]{2,1,0:T(8,128)(2,1)} custom-call(f32[8,64,2048]{2,1,0:T(8,128)} %bitcast.372), custom_call_target="tpu_custom_call" | custom-call | tf_op jit(solution)/shard_map/reduce_rows/pallas_call | solution.py:468
  304.3 7.7 %psum.22 = f32[128,1]{0,1:T(1,128)} all-reduce(f32[128,1]{0,1:T(1,128)} %bitcast.415), channel_id=1, replica_groups=mesh['dp'=8,'tensor'=4] {'tensor'}, use_global_device_ids=true, to_apply=%region_19.20 | all-reduce | flops 128 | bytes 1024 | tf_op jit(solution)/shard_map/psum | solution.py:672
  314.8 22.1 %gather_rows.9 = bf16[8,64,2048]{2,1,0:T(8,128)(2,1)} custom-call(bf16[8,64,512]{2,1,0:T(8,128)(2,1)} %bitcast.377), custom_call_target="tpu_custom_call" | custom-call | tf_op jit(solution)/shard_map/gather_rows/pallas_call | solution.py:429
  352.8 7.9 %reshape.1006 = bf16[2048,1024,1]{1,0,2:T(8,128)(2,1)} reshape(bf16[2048,2,512]{2,1,0:T(2,128)(2,1)} %param.25) | data formatting | bytes 8388608 | tf_op jit(solution)/shard_map/reshape | solution.py:622
  366.2 6.1 %convolution_bitcast_fusion = f32[1,1408,2048]{2,1,0:T(8,128)} fusion(bf16[512,1408]{1,0:T(8,128)(2,1)S(1)} %copy-done.64, bf16[512,2048]{1,0:T(8,128)(2,1)S(1)} %bitcast.383), kind=kOutput, calls=%fused_computation.4 | convolution fusion | flops 2952790016 | bytes 15073280 | tf_op jit(solution)/shard_map/dot_general | solution.py:509
  372.4 5.1 fusion.5.src
  377.5 26.3 %reduce_rows.5 = bf16[8,64,512]{2,1,0:T(8,128)(2,1)} custom-call(f32[8,64,2048]{2,1,0:T(8,128)} %fusion.5.src), custom_call_target="tpu_custom_call" | custom-call | tf_op jit(solution)/shard_map/reduce_rows/pallas_call | solution.py:468
  406.9 15.2 %a2a_rows.1 = bf16[8,64,512]{2,1,0:T(8,128)(2,1)} custom-call(bf16[8,64,512]{2,1,0:T(8,128)(2,1)} %bitcast.381), custom_call_target="tpu_custom_call" | custom-call | tf_op jit(solution)/shard_map/a2a_rows/pallas_call | solution.py:485
  426.6 4.5 convolution_bitcast_fusion.3
  431.2 6.3 %convolution_bitcast_fusion.2 = f32[1,2048,1408]{2,1,0:T(8,128)} fusion(bf16[512,2048]{1,0:T(8,128)(2,1)S(1)} %copy-done.18, bf16[512,1408]{1,0:T(8,128)(2,1)S(1)} %copy-done.69), kind=kOutput, calls=%fused_computation.6 | convolution fusion | flops 2952790016 | bytes 15073280 | tf_op jit(solution)/shard_map/dot_general | solution.py:509
  441.0 6.3 %convolution_bitcast_fusion.1 = f32[1,2048,1408]{2,1,0:T(8,128)} fusion(bf16[512,2048]{1,0:T(8,128)(2,1)S(1)} %copy-done.18, bf16[512,1408]{1,0:T(8,128)(2,1)S(1)} %copy-done.67), kind=kOutput, calls=%fused_computation.5 | convolution fusion | flops 2952790016 | bytes 15073280 | tf_op jit(solution)/shard_map/dot_general | solution.py:509
  455.2 41.3 %copy_rows.3 = bf16[8,128,1024]{2,1,0:T(8,128)(2,1)} custom-call(bf16[128,1024]{1,0:T(8,128)(2,1)} %pad_maximum_fusion.6.src), custom_call_target="tpu_custom_call" | custom-call | tf_op jit(solution)/shard_map/copy_rows/pallas_call | solution.py:502
  499.3 6.6 %fusion.210 = f32[2048,2,512]{2,0,1:T(8,128)S(1)} fusion(bf16[1024,2048,1]{1,0,2:T(8,128)(2,1)} %bitcast.371, bf16[2,512,1024]{2,1,0:T(8,128)(2,1)S(1)} %bitcast.380), kind=kOutput, calls=%fused_computation.347 | convolution fusion | flops 4294967296 | bytes 14680064 | tf_op jit(solution)/shard_map/dot_general | solution.py:509
  506.0 16.5 %copy.98 = f32[2048,2,512]{2,1,0:T(2,128)} copy(f32[2048,2,512]{2,0,1:T(8,128)S(1)} %fusion.210) | data formatting | bytes 16777216
  527.6 36.5 %reduce_rows.7 = bf16[10,64,512]{2,1,0:T(8,128)(2,1)} custom-call(f32[10,64,2048]{2,1,0:T(8,128)} %pad_maximum_fusion.src), custom_call_target="tpu_custom_call" | custom-call | tf_op jit(solution)/shard_map/reduce_rows/pallas_call | solution.py:468
  566.6 6.1 %psum.23 = f32[128,1]{0,1:T(1,128)S(1)} all-reduce(f32[128,1]{0,1:T(1,128)S(1)} %bitcast.426), channel_id=1, replica_groups=mesh['dp'=8,'tensor'=4] {'tensor'}, use_global_device_ids=true, to_apply=%region_28.29 | all-reduce | flops 128 | bytes 1024 | tf_op jit(solution)/shard_map/psum | solution.py:716
  573.4 14.8 %gather_rows.11 = f32[8,8,2048]{2,1,0:T(8,128)} custom-call(f32[8,512]{1,0:T(8,128)} %maximum_maximum_fusion.src), custom_call_target="tpu_custom_call" | custom-call | tf_op jit(solution)/shard_map/gather_rows/pallas_call | solution.py:429
  592.0 16.1 %gather_rows.10 = bf16[8,32,2048]{2,1,0:T(8,128)(2,1)} custom-call(bf16[8,32,512]{2,1,0:T(8,128)(2,1)} %pad_maximum_fusion.5.src), custom_call_target="tpu_custom_call" | custom-call | tf_op jit(solution)/shard_map/gather_rows/pallas_call | solution.py:429
  (301 shorter events, 141.7 us)
Async XLA Ops:
  0.6 129.9 %copy-start = (bf16[1,512,2048]{2,1,0:T(8,128)(2,1)S(1)}, bf16[1,512,2048]{2,1,0:T(8,128)(2,1)}, u32[]{:S(2)}) copy-start(bf16[1,512,2048]{2,1,0:T(8,128)(2,1)} %param.27) | copy-start | bytes 6291460
  27.6 43.1 %copy-start.37 = (s32[128]{0:T(128)}, s32[128]{0:T(128)S(1)}, u32[]{:S(2)}) copy-start(s32[128]{0:T(128)S(1)} %fusion.167) | copy-start | bytes 1540
  29.3 44.1 %copy-start.36 = (f32[2048]{0:T(1024)S(1)}, f32[2048]{0:T(1024)}, u32[]{:S(2)}) copy-start(f32[2048]{0:T(1024)} %param.24) | copy-start | bytes 24580
  80.7 366.6 %all-to-all-start = ((bf16[8,64,512]{2,1,0:T(8,128)(2,1)}), bf16[8,64,512]{2,1,0:T(8,128)(2,1)}, u32[]{:S(2)}, u32[]{:S(2)}) async-start(bf16[8,64,512]{2,1,0:T(8,128)(2,1)} %copy_bitcast_fusion), calls=%async_computation | async-start | bytes 1048576 | tf_op jit(solution)/shard_map/all_to_all | solution.py:641
  91.0 68.9 %copy-start.34 = (pred[8,128]{1,0:T(8,128)(4,1)}, pred[8,128]{1,0:T(8,128)(4,1)S(1)}, u32[]{:S(2)}) copy-start(pred[8,128]{1,0:T(8,128)(4,1)S(1)} %fusion.163) | copy-start | bytes 3076
  133.8 25.2 %copy-start.58 = (f32[128]{0:T(128)S(1)}, f32[128]{0:T(128)}, u32[]{:S(2)}) copy-start(f32[128]{0:T(128)} %copy-done.57) | copy-start | bytes 1540
  133.8 25.2 %copy-start.60 = (f32[128]{0:T(128)S(1)}, f32[128]{0:T(128)}, u32[]{:S(2)}) copy-start(f32[128]{0:T(128)} %copy-done.59) | copy-start | bytes 1540
  133.8 25.2 %copy-start.49 = (f32[128]{0:T(128)S(1)}, f32[128]{0:T(128)}, u32[]{:S(2)}) copy-start(f32[128]{0:T(128)} %fusion.178) | copy-start | bytes 1540
  133.8 25.2 %copy-start.51 = (f32[128]{0:T(128)S(1)}, f32[128]{0:T(128)}, u32[]{:S(2)}) copy-start(f32[128]{0:T(128)} %fusion.177) | copy-start | bytes 1540
  133.8 27.5 %copy-start.27 = (pred[8,128]{1,0:T(8,128)(4,1)S(1)}, pred[8,128]{1,0:T(8,128)(4,1)}, u32[]{:S(2)}) copy-start(pred[8,128]{1,0:T(8,128)(4,1)} %fusion.162) | copy-start | bytes 3076
  133.8 27.5 %copy-start.41 = (f32[512]{0:T(512)S(1)}, f32[512]{0:T(512)}, u32[]{:S(2)}) copy-start(f32[512]{0:T(512)} %eq.398) | copy-start | bytes 6148
  165.3 30.3 %copy-start.30 = (pred[8,1,128]{2,1,0:T(4,128)(4,1)S(1)}, pred[8,1,128]{2,1,0:T(4,128)(4,1)}, u32[]{:S(2)}) copy-start(pred[8,1,128]{2,1,0:T(4,128)(4,1)} %get-tuple-element.80) | copy-start | bytes 3076
  165.3 30.4 %copy-start.38 = (s32[128]{0:T(128)S(1)}, s32[128]{0:T(128)}, u32[]{:S(2)}) copy-start(s32[128]{0:T(128)} %copy-done.37) | copy-start | bytes 1540
  192.1 46.9 %copy-start.61 = (f32[128]{0:T(128)S(1)}, f32[128]{0:T(128)}, u32[]{:S(2)}) copy-start(f32[128]{0:T(128)} %get-tuple-element.104) | copy-start | bytes 1540
  192.1 55.0 %copy-start.31 = (f32[8,1,128]{2,1,0:T(1,128)S(1)}, f32[8,1,128]{2,1,0:T(1,128)}, u32[]{:S(2)}) copy-start(f32[8,1,128]{2,1,0:T(1,128)} %get-tuple-element.70) | copy-start | bytes 12292
  247.1 55.2 %copy-start.44 = (f32[128]{0:T(128)}, f32[128]{0:T(128)S(1)}, u32[]{:S(2)}) copy-start(f32[128]{0:T(128)S(1)} %get-tuple-element.101) | copy-start | bytes 1540
  274.4 27.9 %copy-start.25 = (f32[512]{0:T(512)S(1)}, f32[512]{0:T(512)}, u32[]{:S(2)}) copy-start(f32[512]{0:T(512)} %dynamic_slice.83) | copy-start | bytes 6148
  274.4 27.9 %copy-start.28 = (pred[8,128]{1,0:T(8,128)(4,1)S(1)}, pred[8,128]{1,0:T(8,128)(4,1)}, u32[]{:S(2)}) copy-start(pred[8,128]{1,0:T(8,128)(4,1)} %fusion.162) | copy-start | bytes 3076
  352.7 11.6 %copy-start.2 = (bf16[8,64,2048]{2,1,0:T(8,128)(2,1)S(1)}, bf16[8,64,2048]{2,1,0:T(8,128)(2,1)}, u32[]{:S(2)}) copy-start(bf16[8,64,2048]{2,1,0:T(8,128)(2,1)} %gather_rows.7) | copy-start | bytes 6291460
  352.7 11.6 %copy-start.40 = (f32[512]{0:T(512)S(1)}, f32[512]{0:T(512)}, u32[]{:S(2)}) copy-start(f32[512]{0:T(512)} %rsqrt.40) | copy-start | bytes 6148
  377.5 48.7 %copy-start.12 = (bf16[8,64,4,128]{3,1,2,0:T(8,128)(2,1)S(1)}, bf16[8,64,4,128]{3,1,2,0:T(8,128)(2,1)}, u32[]{:S(2)}) copy-start(bf16[8,64,4,128]{3,1,2,0:T(8,128)(2,1)} %pad_maximum_fusion.4) | copy-start | bytes 1572868
  403.8 22.8 %copy-start.8 = (bf16[8,64,2048]{2,1,0:T(8,128)(2,1)S(1)}, bf16[8,64,2048]{2,1,0:T(8,128)(2,1)}, u32[]{:S(2)}) copy-start(bf16[8,64,2048]{2,1,0:T(8,128)(2,1)} %copy-done.7) | copy-start | bytes 6291460
  506.0 16.5 %copy-start.5 = (bf16[2048,1024,1]{1,0,2:T(8,128)(2,1)S(1)}, bf16[2048,1024,1]{1,0,2:T(8,128)(2,1)}, u32[]{:S(2)}) copy-start(bf16[2048,1024,1]{1,0,2:T(8,128)(2,1)} %reshape.1006) | copy-start | bytes 12582916
  527.6 37.5 %copy-start.35 = (pred[8,128]{1,0:T(8,128)(4,1)S(1)}, pred[8,128]{1,0:T(8,128)(4,1)}, u32[]{:S(2)}) copy-start(pred[8,128]{1,0:T(8,128)(4,1)} %copy-done.34) | copy-start | bytes 3076
  527.6 37.5 %copy-start.42 = (f32[512]{0:T(512)S(1)}, f32[512]{0:T(512)}, u32[]{:S(2)}) copy-start(f32[512]{0:T(512)} %dynamic_slice.85) | copy-start | bytes 6148
  527.6 45.1 %copy-start.43 = (f32[512]{0:T(512)S(1)}, f32[512]{0:T(512)}, u32[]{:S(2)}) copy-start(f32[512]{0:T(512)} %get-tuple-element.42) | copy-start | bytes 6148
  527.6 62.3 %copy-start.26 = (f32[512]{0:T(512)S(1)}, f32[512]{0:T(512)}, u32[]{:S(2)}) copy-start(f32[512]{0:T(512)} %dynamic_slice.83) | copy-start | bytes 6148
  527.6 62.3 %copy-start.45 = (f32[128]{0:T(128)S(1)}, f32[128]{0:T(128)}, u32[]{:S(2)}) copy-start(f32[128]{0:T(128)} %copy-done.44) | copy-start | bytes 1540
  527.6 62.3 %copy-start.46 = (f32[128]{0:T(128)S(1)}, f32[128]{0:T(128)}, u32[]{:S(2)}) copy-start(f32[128]{0:T(128)} %get-tuple-element.100) | copy-start | bytes 1540
  527.6 62.3 %copy-start.48 = (f32[128]{0:T(128)S(1)}, f32[128]{0:T(128)}, u32[]{:S(2)}) copy-start(f32[128]{0:T(128)} %copy-done.47) | copy-start | bytes 1540
  564.2 45.2 %copy-start.39 = (s32[128]{0:T(128)S(1)}, s32[128]{0:T(128)}, u32[]{:S(2)}) copy-start(s32[128]{0:T(128)} %copy-done.37) | copy-start | bytes 1540
  572.7 38.9 %copy-start.1 = (bf16[1,512,2048]{2,1,0:T(8,128)(2,1)S(1)}, bf16[1,512,2048]{2,1,0:T(8,128)(2,1)}, u32[]{:S(2)}) copy-start(bf16[1,512,2048]{2,1,0:T(8,128)(2,1)} %param.27) | copy-start | bytes 6291460
  (47 other events, 245.0 us)

commit v2 on v1

--- a/solution.py
+++ b/solution.py
@@ -3,6 +3,7 @@
 
 import jax
 import jax.numpy as jnp
+import numpy as np
 from jax import lax
 from jax.experimental import pallas as pl
 from jax.experimental.pallas import tpu as pltpu
@@ -521,6 +522,555 @@
     return dot(a, b, (((0,), (0,)), ((), ())))
 
 
+class Ring:
+    def __init__(self, n):
+        self.n = n
+        self.g, self.t, self.tx, self.tc = ranks()
+        self.tcx = lax.rem(self.tc + 2, 4)
+        self.tail = []
+
+    def to(self, o):
+        return lax.rem(self.g + o, self.n)
+
+    def greet_all(self):
+        greet([(self.to(o), self.t) for o in range(1, self.n)] + [(self.g, self.tx), (self.g, self.tc)])
+
+    def greet_everyone(self):
+        greet([(self.to(o), self.t) for o in range(1, self.n)] + [(self.g, q) for q in (self.tx, self.tc, self.tcx)])
+
+    def send(self, src, dst, ss, rs, dp, tn):
+        c = rcopy(src, dst, ss, rs, dp, tn)
+        c.start()
+        self.tail.append(c)
+        return c
+
+    def finish(self):
+        for c in self.tail:
+            c.wait_send()
+        self.tail = []
+
+
+def cols_of(q, j, width, cw):
+    return pl.ds(pl.multiple_of(q * width + j * cw, cw), cw)
+
+
+REDUCE_SEMS = lambda nc, n: [DMA((nc,))] * 4 + [DMA((nc, n))] * 2
+GATHER_SEMS = lambda nc, n: [DMA((nc, n))] * 2 + [DMA((nc,))] * 6
+REDUCE_BUFS = lambda nc, n, r, cw: [
+    VM((nc, 2, n, r, cw), BF), VM((nc, 2, n, r, cw), BF), VM((nc, 2, n, r, cw), F32),
+    VM((nc, n, r, cw), BF), VM((nc, n, r, cw), BF), VM((nc, n, r, cw), BF), VM((nc, n, r, cw), BF)]
+
+
+class Reduce:
+    def __init__(self, ring, partial, bufs, sems):
+        self.ring, self.partial = ring, partial
+        self.cbuf, self.cin, self.pbuf, self.xbuf, self.xin, self.dbuf, self.rbuf = bufs
+        self.cs, self.cr, self.xs, self.xr, self.ds, self.dr = sems
+        self.c, self.x, self.d = {}, {}, {}
+
+    def core(self):
+        k = self.ring
+        nc, _, n, r, cw = self.cbuf.shape
+        for i, q in enumerate((k.tc, k.tcx)):
+            v = self.partial(q).astype(BF)
+            for j in range(nc):
+                self.cbuf[j, i] = v[:, j * cw:(j + 1) * cw].reshape(n, r, cw)
+        for j in range(nc):
+            self.c[j] = k.send(self.cbuf.at[j], self.cin.at[j], self.cs.at[j], self.cr.at[j], k.g, k.tc)
+        for i, q in ((1, k.tx), (0, k.t)):
+            v = self.partial(q)
+            for j in range(nc):
+                self.pbuf[j, i] = v[:, j * cw:(j + 1) * cw].reshape(n, r, cw)
+            if i:
+                for j in range(nc):
+                    self.cross(j)
+
+    def cross(self, j):
+        k = self.ring
+        self.c[j].wait_recv()
+        self.xbuf[j] = (self.pbuf[j, 1] + self.cin[j, 1].astype(F32)).astype(BF)
+        self.x[j] = k.send(self.xbuf.at[j], self.xin.at[j], self.xs.at[j], self.xr.at[j], k.g, k.tx)
+
+    def home(self, j):
+        k = self.ring
+        self.x[j].wait_recv()
+        self.dbuf[j] = (self.pbuf[j, 0] + self.cin[j, 0].astype(F32) + self.xin[j].astype(F32)).astype(BF)
+        for o in range(1, k.n):
+            d = k.to(o)
+            self.d[j, o] = k.send(
+                self.dbuf.at[j, d], self.rbuf.at[j, k.g], self.ds.at[j, o], self.dr.at[j, o], d, k.t)
+        self.rbuf[j, k.g] = self.dbuf[j, k.g]
+
+    def rows(self, j):
+        for o in range(1, self.ring.n):
+            self.d[j, o].wait_recv()
+        return self.rbuf[j].reshape(-1, self.rbuf.shape[-1])
+
+
+class Gather:
+    def __init__(self, ring, width, full, sbuf, sems):
+        self.ring, self.width, self.full, self.sbuf = ring, width, full, sbuf
+        self.ss, self.rs, self.xs, self.xr, self.cs, self.cr, self.c2s, self.c2r = sems
+        self.d, self.x, self.c = {}, {}, []
+
+    def at(self, q, j):
+        return cols_of(q, j, self.width, self.sbuf.shape[-1])
+
+    def out(self, j, rows):
+        k, cc = self.ring, self.at(self.ring.t, j)
+        self.sbuf[j] = rows.reshape(self.sbuf.shape[1:])
+        for o in range(1, k.n):
+            d = k.to(o)
+            self.d[j, o] = k.send(
+                self.sbuf.at[j, d], self.full.at[k.g, :, cc], self.ss.at[j, o], self.rs.at[j, o], d, k.t)
+        self.full[k.g, :, cc] = self.sbuf[j, k.g]
+
+    def cross(self, j):
+        k, ref = self.ring, self.full.at[:, :, self.at(self.ring.t, j)]
+        for o in range(1, k.n):
+            self.d[j, o].wait_recv()
+        self.x[j] = k.send(ref, ref, self.xs.at[j], self.xr.at[j], k.g, k.tx)
+        self.c.append(k.send(ref, ref, self.cs.at[j], self.cr.at[j], k.g, k.tc))
+
+    def core(self, j):
+        k, ref = self.ring, self.full.at[:, :, self.at(self.ring.tx, j)]
+        self.x[j].wait_recv()
+        self.c.append(k.send(ref, ref, self.c2s.at[j], self.c2r.at[j], k.g, k.tc))
+
+    def finish(self):
+        for c in self.c:
+            c.wait_recv()
+
+
+def paired(reduce_one, gather_one, middle, nc):
+    reduce_one.core()
+    steps = []
+    for j in range(nc):
+        steps += [(2 * j, 0, lambda j=j: reduce_one.home(j)), (2 * j + 3, 1, lambda j=j: gather_one.out(j, middle(j, reduce_one.rows(j))))]
+        steps += [(2 * j + 7, 2, lambda j=j: gather_one.cross(j)), (2 * j + 9, 3, lambda j=j: gather_one.core(j))]
+    for _, _, step in sorted(steps, key=lambda s: s[:2]):
+        step()
+    gather_one.finish()
+
+
+NC = 4
+
+
+def split_bf(v):
+    high = v.astype(BF)
+    return high, (v - high.astype(F32)).astype(BF)
+
+
+def hidden_body(n, attn, wo, x_own, comb, gates, pick, hidden, full, scale, *scratch):
+    bufs, sbuf, sq, sq_in, qs, qr, sems = scratch[:7], *scratch[7:12], scratch[12:]
+    ring = Ring(n)
+    ring.greet_everyone()
+    rows, width = x_own.shape
+    shared = []
+    cw = width // NC
+
+    def partial(q):
+        return mm(attn[...], wo[:, cols_of(q, 0, width, width)])
+
+    def middle(j, rows):
+        high, low = split_bf(rows.astype(F32) * gates[...])
+        got = x_own[:, j * cw:(j + 1) * cw] + mm(comb[...], high) + mm(comb[...], low)
+        hidden[:, j * cw:(j + 1) * cw] = got
+        high, low = split_bf(got * got)
+        ones = jnp.ones((8, cw), BF)
+        squares = mm_t(ones, high) + mm_t(ones, low)
+        sq[...] = squares if j == 0 else sq[...] + squares
+        if j == NC - 1:
+            for i, q in enumerate([ring.tc, ring.tx, ring.tcx]):
+                shared.append(ring.send(sq, sq_in.at[i], qs.at[i], qr.at[i], ring.g, q))
+        return mm(pick[...], got.astype(BF)).astype(BF)
+
+    red = Reduce(ring, partial, bufs, sems[:6])
+    gat = Gather(ring, width, full, sbuf, sems[6:])
+    paired(red, gat, middle, NC)
+    for c in shared:
+        c.wait_recv()
+    total = (sq[...] + sq_in[0] + sq_in[1] + sq_in[2])[:1]
+    eye = lax.broadcasted_iota(jnp.int32, (rows, rows), 0) == lax.broadcasted_iota(jnp.int32, (rows, rows), 1)
+    column = jnp.sum(jnp.where(eye, total, 0.0), axis=1, keepdims=True)
+    scale[...] = lax.rsqrt(column / (4 * width) + EPSILON)
+    ring.finish()
+
+
+def hidden_rows(attn, wo, x_own, comb, gates, pick, n, cid):
+    slots = attn.shape[0]
+    r, (rows, width) = slots // n, x_own.shape
+    return pl.pallas_call(
+        functools.partial(hidden_body, n),
+        out_shape=(
+            jax.ShapeDtypeStruct((rows, width), F32), jax.ShapeDtypeStruct((n, r, 4 * width), BF),
+            jax.ShapeDtypeStruct((rows, 1), F32)),
+        in_specs=[pl.BlockSpec(memory_space=VM)] * 6,
+        out_specs=[pl.BlockSpec(memory_space=VM)] * 3,
+        scratch_shapes=REDUCE_BUFS(NC, n, r, width // NC) + [VM((NC, n, r, width // NC), BF)]
+        + [VM((8, rows), F32), VM((3, 8, rows), F32), DMA((3,)), DMA((3,))]
+        + REDUCE_SEMS(NC, n) + GATHER_SEMS(NC, n),
+        name="hidden_rows", compiler_params=params(cid),
+    )(attn, wo, x_own, comb, gates, pick)
+
+
+def expert_body(
+    n, hid_rows, d_mbr, gain, wg_hbm, wu_hbm, wd_hbm, hidden, dy_own, gain_t, scale, mlp_t, mlp_gates, mlp_rows, att_rows,
+    full, d_hidden, mixed, gain_part, n2, inner, d_gate, d_up, *scratch,
+):
+    ring = Ring(n)
+    bufs, bufs2 = scratch[:7], scratch[7:14]
+    sbuf, wg, wu, wd, r_own, r_in, r_to, r_back = scratch[14:22]
+    wsem, rss, rsr, rds, rdr = scratch[22:27]
+    sems = scratch[27:]
+    ff = wg.shape[1]
+    rows, width = hidden.shape
+    slots = n2.shape[0]
+    features = 4 * width
+    cw = width // NC
+    loads = [pltpu.make_async_copy(a, b, wsem.at[i]) for i, (a, b) in enumerate([(wg_hbm, wg), (wu_hbm, wu), (wd_hbm, wd)])]
+    for c in loads:
+        c.start()
+    ring.greet_everyone()
+
+    def norm_rows(i, _):
+        at = pl.ds(pl.multiple_of(i * 64, 64), 64)
+        v = hid_rows[i].astype(F32)
+        s = lax.rsqrt(jnp.mean(v * v, axis=-1, keepdims=True) + EPSILON)
+        n2[at, :] = (v * s * gain[...]).astype(BF)
+        return _
+
+    lax.fori_loop(0, n, norm_rows, 0)
+    for c in loads:
+        c.wait()
+    r_own[...] = jnp.zeros_like(r_own)
+
+    def units(at, size):
+        a = n2[...]
+        gate = mm(a, wg[:, at])
+        up = mm(a, wu[:, at])
+        d_in = mm_t(d_mbr[...], wd[at, :])
+        sig = jax.nn.sigmoid(gate)
+        silu = gate * sig
+        inner[:, at] = (silu * up).astype(BF)
+        du = (d_in * silu).astype(BF)
+        dg = (d_in * up * sig * (1.0 + gate * (1.0 - sig))).astype(BF)
+        d_up[:, at] = du
+        d_gate[:, at] = dg
+        both = (gate * dg.astype(F32) + up * du.astype(F32)).astype(BF)
+        r_own[...] += mm_t(jnp.ones((8, size), BF), both)
+
+    tile = 256
+
+    def unit_tile(i, _):
+        units(pl.ds(pl.multiple_of(i * tile, tile), tile), tile)
+        return _
+
+    lax.fori_loop(0, ff // tile, unit_tile, 0)
+    if ff % tile:
+        units(pl.ds(ff // tile * tile, ff % tile), ff % tile)
+
+    others = [ring.tc, ring.tx, ring.tcx]
+    r_sends = [ring.send(r_own, r_in.at[i], rss.at[i], rsr.at[i], ring.g, q) for i, q in enumerate(others)]
+
+    def partial(q):
+        at = cols_of(q, 0, width, width)
+        return mm_t(d_gate[...], wg[at, :]) + mm_t(d_up[...], wu[at, :])
+
+    def partial_mixed(q):
+        return mm(inner[...], wd[:, cols_of(q, 0, width, width)])
+
+    pairs = {}
+
+    def share_r():
+        for c in r_sends:
+            c.wait_recv()
+        r_to[...] = r_own[...] + r_in[0] + r_in[1] + r_in[2]
+        for o in range(1, n):
+            d = ring.to(o)
+            half = pl.ds(pl.multiple_of(d // 2 * 128, 128), 128)
+            pairs[o] = ring.send(r_to.at[:, half], r_back.at[ring.g], rds.at[o], rdr.at[o], d, ring.t)
+        r_back[ring.g] = r_to[:, pl.ds(pl.multiple_of(ring.g // 2 * 128, 128), 128)]
+
+    total_r = {}
+
+    def take_r():
+        for o in range(1, n):
+            pairs[o].wait_recv()
+        odd = lax.rem(ring.g, 2) == 1
+        got = jnp.concatenate(
+            [jnp.where(odd, r_back[e][:, 64:], r_back[e][:, :64]) for e in range(n)], axis=1)
+        high = got.astype(BF)
+        low = (got - high.astype(F32)).astype(BF)
+        total_r[0] = (mm_t(mlp_t[...], high) + mm_t(mlp_t[...], low))[:, :1] / features
+
+    def middle(j, got):
+        if j == 0:
+            take_r()
+        cc = slice(j * cw, (j + 1) * cw)
+        s2, h = scale[...], hidden[:, cc]
+        d_n = mm(mlp_t[...], got)
+        d_h = dy_own[:, cc] + s2 * (gain_t[:, cc] * d_n) - h * (s2 * s2) * total_r[0]
+        d_hidden[:, cc] = d_h
+        gain_part[:, cc] = jnp.broadcast_to(jnp.sum(d_n * h * s2, axis=0, keepdims=True), (8, cw))
+        return mm(att_rows[...], d_h.astype(BF)).astype(BF)
+
+    red = Reduce(ring, partial, bufs, sems[:6])
+    gat = Gather(ring, width, full, sbuf, sems[6:14])
+    red2 = Reduce(ring, partial_mixed, bufs2, sems[14:20])
+
+    def settle(j):
+        got = red2.rows(j)
+        scaled = got.astype(F32) * mlp_gates[...]
+        high = scaled.astype(BF)
+        low = (scaled - high.astype(F32)).astype(BF)
+        cc = slice(j * cw, (j + 1) * cw)
+        mixed[:, cc] = (hidden[:, cc] + mm(mlp_t[...], high) + mm(mlp_t[...], low)).astype(BF)
+
+    red.core()
+    share_r()
+    steps = []
+    for j in range(NC):
+        steps += [(2 * j, 1, lambda j=j: red.home(j)), (2 * j + 3, 2, lambda j=j: gat.out(j, middle(j, red.rows(j))))]
+        steps += [(2 * j + 7, 3, lambda j=j: gat.cross(j)), (2 * j + 9, 4, lambda j=j: gat.core(j))]
+        steps += [(2 * j + 12, 7, lambda j=j: red2.home(j)), (2 * j + 16, 8, lambda j=j: settle(j))]
+    steps += [(9.5, 5, red2.core)]
+    steps.sort(key=lambda s: s[:2])
+    for _, _, run in steps:
+        run()
+    gat.finish()
+    ring.finish()
+
+
+def expert_layer(hid_rows, d_mbr, gain, wg, wu, wd, hidden, dy_own, gain_t, scale, mlp_t, mlp_gates, mlp_rows, att_rows, n, cid):
+    r, features = hid_rows.shape[1:]
+    ff = wg.shape[1]
+    rows, width = hidden.shape
+    slots, cw = n * r, width // NC
+    any_, vm = pl.BlockSpec(memory_space=pl.ANY), pl.BlockSpec(memory_space=VM)
+    sds = jax.ShapeDtypeStruct
+    return pl.pallas_call(
+        functools.partial(expert_body, n),
+        out_shape=(
+            sds((n, r, features), BF), sds((rows, width), F32), sds((rows, width), BF), sds((8, width), F32),
+            sds((slots, features), BF), sds((slots, ff), BF), sds((slots, ff), BF), sds((slots, ff), BF)),
+        in_specs=[vm, vm, vm, any_, any_, any_] + [vm] * 8,
+        out_specs=[vm] * 8,
+        scratch_shapes=REDUCE_BUFS(NC, n, r, cw) + REDUCE_BUFS(NC, n, r, cw) + [
+            VM((NC, n, r, cw), BF), VM((features, ff), BF), VM((features, ff), BF), VM((ff, features), BF),
+            VM((8, slots), F32), VM((3, 8, slots), F32), VM((8, slots), F32), VM((n, 8, 128), F32),
+            DMA((3,)), DMA((3,)), DMA((3,)), DMA((n,)), DMA((n,))]
+        + REDUCE_SEMS(NC, n) + GATHER_SEMS(NC, n) + REDUCE_SEMS(NC, n),
+        name="expert_layer", compiler_params=params(cid),
+    )(hid_rows, d_mbr, gain, wg, wu, wd, hidden, dy_own, gain_t, scale, mlp_t, mlp_gates, mlp_rows, att_rows)
+
+
+META = {name: i for i, name in enumerate(
+    ("ar0", "ar1", "ag0", "ag1", "mr0", "mr1", "mg0", "mg1", "pos", "seg", "wpos"))}
+
+
+def iota(shape, dim):
+    return lax.broadcasted_iota(jnp.int32, shape, dim)
+
+
+def slot_table(meta, first, name, cap):
+    member = (meta[first:first + 1] == name) | (meta[first + 1:first + 2] == name)
+    tokens = meta.shape[1]
+    before = jnp.where(iota((tokens, tokens), 0) < iota((tokens, tokens), 1), 1.0, 0.0).astype(BF)
+    rank = mm(jnp.broadcast_to(jnp.where(member, 1.0, 0.0), (8, tokens)).astype(BF), before)[:1]
+    return jnp.where((rank == iota((cap, tokens), 0).astype(F32)) & member, 1.0, 0.0).astype(BF)
+
+
+def allowed_pairs(meta, meta_t):
+    seg, wpos = META["seg"], META["wpos"]
+    same = meta_t[:, seg:seg + 1] == meta[seg:seg + 1]
+    return jnp.where(same & (meta[wpos:wpos + 1] <= meta_t[:, wpos:wpos + 1]), 1.0, 0.0).astype(BF)
+
+
+def position_rows(meta_t):
+    pos = META["pos"]
+    tokens = meta_t.shape[0]
+    return jnp.where(meta_t[:, pos:pos + 1] == iota((tokens, tokens), 1).astype(F32), 1.0, 0.0).astype(BF)
+
+
+def looked_up(rows, table):
+    got = mm(rows, table)
+    w = got.shape[1] // 3
+    return got[:, :w] + got[:, w:2 * w] + got[:, 2 * w:]
+
+
+def turned(v, cosine, sine):
+    out = []
+    for h in range(v.shape[1] // HD):
+        u = v[:, h * HD:(h + 1) * HD]
+        out.append(u * cosine + pltpu.roll(u, HD // 2, 1) * sine)
+    return jnp.concatenate(out, axis=1)
+
+
+def angle_tables(positions):
+    half = HD // 2
+    frequency = np.exp(-math.log(THETA) * np.arange(half) / half)
+    turned_by = np.arange(positions)[:, None] * frequency[None, :]
+    cosine = np.concatenate([np.cos(turned_by)] * 2, axis=1).astype(np.float32)
+    sine = np.concatenate([-np.sin(turned_by), np.sin(turned_by)], axis=1).astype(np.float32)
+
+    def parts(v):
+        out, left = [], v
+        for _ in range(3):
+            p = left.astype(jnp.bfloat16)
+            out.append(p)
+            left = left - p.astype(np.float32)
+        return np.concatenate(out, axis=1)
+
+    return jnp.asarray(parts(cosine)), jnp.asarray(parts(sine))
+
+
+def softmax_rows(scores):
+    top = jnp.max(scores, axis=-1, keepdims=True)
+    expo = jnp.exp(scores - top)
+    return expo / jnp.sum(expo, axis=-1, keepdims=True)
+
+
+def attend_body(
+    x, gain, w_k, w_v, w_q, meta, meta_t, cos_t, sin_t,
+    normed, picked, keys, values, query, attn, scale, bias, turn_slots, k_scr, v_scr, q_scr, n_scr,
+):
+    me = lax.axis_index("dp").astype(F32)
+    pair, rows, features = x.shape
+    cap = picked.shape[1]
+    heads = w_q.shape[1] // HD
+    flat = x[...].reshape(pair * rows, features).astype(F32)
+    s = lax.rsqrt(jnp.mean(flat * flat, axis=-1, keepdims=True) + EPSILON)
+    scale[...] = s.reshape(pair, rows, 1)
+    low = (flat * s * gain[...]).astype(BF)
+    n_scr[...] = low
+    normed[...] = low.reshape(pair, rows, features)
+    k_all, v_all = mm(n_scr[...], w_k[...]), mm(n_scr[...], w_v[...])
+    slots = []
+    for p in range(pair):
+        m, m_t = meta[p], meta_t[p]
+        table = slot_table(m, META["ar0"], me, cap)
+        at_pos = position_rows(m_t)
+        rr = slice(p * rows, (p + 1) * rows)
+        kk = turned(k_all[rr], looked_up(at_pos, cos_t[...]), looked_up(at_pos, sin_t[...])).astype(BF)
+        k_scr[p] = kk
+        v_scr[p] = v_all[rr].astype(BF)
+        picked[p] = mm(table, n_scr[rr, :]).astype(BF)
+        slot_pos = mm(table, at_pos).astype(BF)
+        turn_slots[p, :, :HD] = looked_up(slot_pos, cos_t[...])
+        turn_slots[p, :, HD:] = looked_up(slot_pos, sin_t[...])
+        bias[p] = (mm(table, allowed_pairs(m, m_t)) - 1.0) * 1e30
+        slots.append(table)
+    keys[...] = k_scr[...]
+    values[...] = v_scr[...]
+    q_all = mm(picked[...].reshape(pair * cap, features), w_q[...])
+    for p in range(pair):
+        qq = turned(q_all[p * cap:(p + 1) * cap], turn_slots[p, :, :HD], turn_slots[p, :, HD:]).astype(BF)
+        q_scr[p] = qq
+        query[p] = qq
+    for p in range(pair):
+        for h in range(heads):
+            hh = slice(h * HD, (h + 1) * HD)
+            scores = mm_t(q_scr[p, :, hh], k_scr[p, :, hh]) / math.sqrt(HD) + bias[p]
+            probs = softmax_rows(scores).astype(BF)
+            attn[p, :, hh] = mm(probs, v_scr[p, :, hh]).astype(BF)
+
+
+def attend(x_all, gain, w_k, w_v, w_q, meta, meta_t, cos_t, sin_t):
+    n, rows, features = x_all.shape
+    hw, cap, pair = w_q.shape[1], CAP, 2
+    sds = jax.ShapeDtypeStruct
+    block = lambda *s: pl.BlockSpec((pair,) + s, lambda i: (i,) + (0,) * len(s))
+    whole = lambda a: pl.BlockSpec(a.shape, lambda i: (0,) * a.ndim)
+    return pl.pallas_call(
+        attend_body, grid=(n // pair,),
+        out_shape=(
+            sds((n, rows, features), BF), sds((n, cap, features), BF), sds((n, rows, hw), BF), sds((n, rows, hw), BF),
+            sds((n, cap, hw), BF), sds((n, cap, hw), BF), sds((n, rows, 1), F32), sds((n, cap, rows), F32),
+            sds((n, cap, 2 * HD), F32)),
+        in_specs=[block(rows, features), whole(gain), whole(w_k), whole(w_v), whole(w_q), block(16, rows), block(rows, 16),
+                  whole(cos_t), whole(sin_t)],
+        out_specs=(
+            block(rows, features), block(cap, features), block(rows, hw), block(rows, hw), block(cap, hw), block(cap, hw),
+            block(rows, 1), block(cap, rows), block(cap, 2 * HD)),
+        scratch_shapes=[VM((pair, rows, hw), BF), VM((pair, rows, hw), BF), VM((pair, cap, hw), BF), VM((pair * rows, features), BF)],
+        name="attend", compiler_params=pltpu.CompilerParams(vmem_limit_bytes=56 * 2**20),
+    )(x_all, gain, w_k, w_v, w_q, meta, meta_t, cos_t, sin_t)
+
+
+def attend_back_body(rows_in, gates, w_o, query, keys, values, bias, turn_slots, d_obr, d_attn, dq_pre, o_scr):
+    pair, cap, features = rows_in.shape
+    heads = w_o.shape[0] // HD
+    for p in range(pair):
+        o_scr[p * cap:(p + 1) * cap] = (rows_in[p].astype(F32) * gates[p]).astype(BF)
+    d_obr[...] = o_scr[...].reshape(pair, cap, features)
+    back = mm_t(o_scr[...], w_o[...]).astype(BF)
+    root = math.sqrt(HD)
+    for p in range(pair):
+        d_o = back[p * cap:(p + 1) * cap]
+        d_attn[p] = d_o
+        dq = []
+        for h in range(heads):
+            hh = slice(h * HD, (h + 1) * HD)
+            probs = softmax_rows(mm_t(query[p, :, hh], keys[p, :, hh]) / root + bias[p])
+            d_probs = mm_t(d_o[:, hh], values[p, :, hh])
+            delta = jnp.sum(d_probs * probs, axis=-1, keepdims=True)
+            d_scores = (probs * (d_probs - delta)).astype(BF)
+            dq.append(mm(d_scores, keys[p, :, hh]) / root)
+        dq = jnp.concatenate(dq, axis=1)
+        dq_pre[p] = turned(dq, turn_slots[p, :, :HD], -turn_slots[p, :, HD:]).astype(BF)
+
+
+def attend_back(rows_in, gates, w_o, query, keys, values, bias, turn_slots):
+    n, cap, features = rows_in.shape
+    hw, rows, pair = w_o.shape[0], keys.shape[1], 2
+    sds = jax.ShapeDtypeStruct
+    block = lambda *s: pl.BlockSpec((pair,) + s, lambda i: (i,) + (0,) * len(s))
+    return pl.pallas_call(
+        attend_back_body, grid=(n // pair,),
+        out_shape=(sds((n, cap, features), BF), sds((n, cap, hw), BF), sds((n, cap, hw), BF)),
+        in_specs=[block(cap, features), block(cap, 1), pl.BlockSpec(w_o.shape, lambda i: (0, 0)), block(cap, hw), block(rows, hw),
+                  block(rows, hw), block(cap, rows), block(cap, 2 * HD)],
+        out_specs=(block(cap, features), block(cap, hw), block(cap, hw)),
+        scratch_shapes=[VM((pair * cap, features), BF)],
+        name="attend_back", compiler_params=pltpu.CompilerParams(vmem_limit_bytes=56 * 2**20),
+    )(rows_in, gates, w_o, query, keys, values, bias, turn_slots)
+
+
+def keys_back_body(query, d_attn, keys, values, meta, meta_t, cos_t, sin_t, d_kv, *, cap):
+    n = query.shape[0]
+    hw = keys.shape[1]
+    m, m_t = meta[...], meta_t[...]
+    tables = jnp.concatenate([slot_table(m, META["ar0"], float(e), cap) for e in range(n)], axis=0)
+    bias = (mm(tables, allowed_pairs(m, m_t)) - 1.0) * 1e30
+    at_pos = position_rows(m_t)
+    cosine, sine = looked_up(at_pos, cos_t[...]), looked_up(at_pos, sin_t[...])
+    root = math.sqrt(HD)
+    for h in range(hw // HD):
+        hh = slice(h * HD, (h + 1) * HD)
+        q = query[:, :, hh].reshape(n * cap, HD)
+        d_o = d_attn[:, :, hh].reshape(n * cap, HD)
+        k, v = keys[:, hh], values[:, hh]
+        probs = softmax_rows(mm_t(q, k) / root + bias)
+        d_probs = mm_t(d_o, v)
+        delta = jnp.sum(d_probs * probs, axis=-1, keepdims=True)
+        d_scores = (probs * (d_probs - delta)).astype(BF)
+        d_kv[:, hw + h * HD:hw + (h + 1) * HD] = mm_rows(probs.astype(BF), d_o).astype(BF)
+        d_k = mm_rows(d_scores, q) / root
+        d_kv[:, hh] = turned(d_k, cosine, -sine).astype(BF)
+
+
+def keys_back(query, d_attn, keys, values, meta, meta_t, cos_t, sin_t):
+    rows, hw = keys.shape
+    args = (query, d_attn, keys, values, meta, meta_t, cos_t, sin_t)
+    return pl.pallas_call(
+        functools.partial(keys_back_body, cap=query.shape[1]),
+        out_shape=jax.ShapeDtypeStruct((rows, 2 * hw), BF),
+        in_specs=[pl.BlockSpec(memory_space=VM)] * len(args), out_specs=pl.BlockSpec(memory_space=VM),
+        name="keys_back", compiler_params=pltpu.CompilerParams(vmem_limit_bytes=56 * 2**20),
+    )(*args)
+
+
 def slots_of(route_a, route_b, names, cap):
     tokens = route_a.shape[-1]
     member = (route_a == names) | (route_b == names)
@@ -565,8 +1115,7 @@
     g, t = lax.axis_index("dp"), lax.axis_index("tensor")
     width = features // 4
     per = rows // n
-    heads = w_kv.shape[2] // HD
-    hw = heads * HD
+    hw = w_kv.shape[2]
     part = lambda a: lax.dynamic_slice_in_dim(a, t * width, width, a.ndim - 1)
     counting = jnp.arange(rows, dtype=jnp.int32)
 
@@ -577,7 +1126,6 @@
     mine = lax.dynamic_index_in_dim(group * per + arrival, g, 0, keepdims=False)
     sorter = (mine[None, :] == counting[:, None]).astype(BF)
     x_sorted = mm(sorter, part(tokens)).astype(BF).reshape(n, per, width)
-    dy_sorted = mm(sorter, part(out_grad)).astype(BF).reshape(n, per, width)
     x_all = gather(x_sorted, n, deal=True, cid=1).reshape(n, rows, features)
 
     here = (group == g) & True
@@ -615,97 +1163,42 @@
     mlp_out = slots_of(o_mr0, o_mr1, names, CAP)
     mlp_out_gate = slot_gate(mlp_out, o_mr0, o_mr1, o_mg0, o_mg1, names)
 
-    xf = x_all.astype(F32)
-    scale_attn = inverse_rms(xf)
-    normed = (xf * scale_attn * gain_attn).astype(BF)
-    normed_flat = normed.reshape(n * rows, features)
-    kv = mm(normed_flat, w_kv.reshape(features, 2 * hw)).reshape(n, rows, 2, heads, HD)
-    key_cos, key_sin = angles(pos)
-    keys = turn(kv[:, :, 0], key_cos, key_sin).astype(BF)
-    values = kv[:, :, 1].astype(BF)
-    picked = jnp.einsum("gst,gtd->gsd", att_in, normed, preferred_element_type=F32).astype(BF)
-    picked = picked.reshape(n * CAP, features)
-    slot_pos = jnp.sum(att_in.astype(F32) * pos[:, None, :], axis=-1)
-    slot_seg = jnp.sum(att_in.astype(F32) * seg[:, None, :], axis=-1)
-    slot_wpos = jnp.sum(att_in.astype(F32) * wpos[:, None, :], axis=-1)
-    q_cos, q_sin = angles(slot_pos)
-    query = turn(mm(picked, w_query[0]).reshape(n, CAP, heads, HD), q_cos, q_sin).astype(BF)
-    allowed = (slot_seg[:, :, None] == seg[:, None, :]) & (wpos[:, None, :] <= slot_wpos[:, :, None])
-    root = math.sqrt(HD)
-    scores = jnp.einsum("gshd,gmhd->ghsm", query, keys, preferred_element_type=F32) / root
-    scores = jnp.where(allowed[:, None], scores, -1e30)
-    probs = jax.nn.softmax(scores, axis=-1)
-    probs_low = probs.astype(BF)
-    attn = jnp.einsum("ghsm,gmhd->gshd", probs_low, values, preferred_element_type=F32)
-    attn = attn.astype(BF).reshape(n * CAP, hw)
-    query_back = lax.all_to_all(query.reshape(n, CAP, hw), "dp", split_axis=0, concat_axis=0, tiled=True)
-    obr = reduce(mm(attn, w_out[0]).reshape(n, CAP, features), n, cid=2)
+    meta_t = meta_all.transpose(0, 2, 1)
+    cos_t, sin_t = angle_tables(rows)
+    normed, picked, keys, values, query, attn, scale_attn, bias, turn_slots = attend(
+        x_all, gain_attn[None], w_kv[:, 0], w_kv[:, 1], w_query[0], meta_all, meta_t, cos_t, sin_t)
+    normed_flat, picked = normed.reshape(n * rows, features), picked.reshape(n * CAP, features)
+    attn = attn.reshape(n * CAP, hw)
+    query_back = lax.all_to_all(query, "dp", split_axis=0, concat_axis=0, tiled=True)
     x_own = part(own(x_all)).astype(F32)
-    hidden = x_own + weigh(att_out, att_out_gate, obr)
-
+    att_rows = att_out.reshape(n * CAP, rows)
     mlp_rows = mlp_out.reshape(n * CAP, rows)
-    hid_rows = gather(mm(mlp_rows, hidden.astype(BF)).astype(BF).reshape(n, CAP, width), n, cid=0)
-    dy_all = gather(dy_sorted, n, deal=True, cid=1).reshape(n, rows, features)
+    hidden, hid_rows, scale_mlp = hidden_rows(
+        attn, w_out[0], x_own, att_rows.T, att_out_gate.reshape(-1, 1), mlp_rows, n, cid=9)
+    dy_all = lax.all_gather(mm(sorter, out_grad).astype(BF), "dp", axis=0).reshape(n, n, per, features)
+    dy_all = dy_all.transpose(1, 0, 2, 3).reshape(n, rows, features)
     d_mbr = jnp.einsum("gst,gtd->gsd", mlp_in, dy_all, preferred_element_type=F32) * mlp_in_gate[..., None]
     d_mbr = d_mbr.astype(BF).reshape(n * CAP, features)
-    hid_rows = hid_rows.reshape(n * CAP, features).astype(F32)
-    normed2 = (hid_rows * inverse_rms(hid_rows) * gain_mlp).astype(BF)
-    gate_map, up_map, down_map = w_gate[0], w_up[0], w_down[0]
-    gate_act = mm(normed2, gate_map)
-    up_act = mm(normed2, up_map)
-    sigmoid_g = jax.nn.sigmoid(gate_act)
-    inner = (gate_act * sigmoid_g * up_act).astype(BF)
-    d_inner = mm_t(d_mbr, down_map)
-    d_up = (d_inner * gate_act * sigmoid_g).astype(BF)
-    d_gate = (d_inner * up_act * sigmoid_g * (1.0 + gate_act * (1.0 - sigmoid_g))).astype(BF)
-    d_rows = mm_t(d_gate, gate_map) + mm_t(d_up, up_map)
-    d_pairs = reduce(d_rows.reshape(n, CAP, features), n, cid=2)
-    mbr = reduce(mm(inner, down_map).reshape(n, CAP, features), n, cid=2)
-    mixed_rows = hidden + weigh(mlp_out, mlp_out_gate, mbr)
+    dy_own = part(own(dy_all)).astype(F32)
+    gain_mlp_t, gain_attn_t = part(gain_mlp), part(gain_attn)
+    d_obr, d_hidden, mixed_rows, gain_mlp_part, normed2, inner, d_gate, d_up = expert_layer(
+        hid_rows, d_mbr, gain_mlp[None], w_gate[0], w_up[0], w_down[0], hidden, dy_own, gain_mlp_t[None], scale_mlp,
+        mlp_rows.T, mlp_out_gate.reshape(-1, 1), mlp_rows, att_rows, n, cid=10)
     w_gate_grad = mm_rows(normed2, d_gate)[None]
     w_up_grad = mm_rows(normed2, d_up)[None]
     w_down_grad = mm_rows(inner, d_mbr)[None]
-    d_normed2 = mm_rows(mlp_rows, d_pairs.reshape(n * CAP, width))
-    gain_mlp_t, gain_attn_t = part(gain_mlp), part(gain_attn)
-    dy_own = part(own(dy_all)).astype(F32)
-    e2 = gain_mlp_t * d_normed2
-    square, inner_sum = lax.psum(
-        (jnp.sum(hidden * hidden, axis=1, keepdims=True), jnp.sum(hidden * e2, axis=1, keepdims=True)), "tensor")
-    scale_mlp = lax.rsqrt(square / features + EPSILON)
-    d_hidden = dy_own + scale_mlp * e2 - hidden * (scale_mlp * scale_mlp * scale_mlp) * (inner_sum / features)
-    gain_mlp_part = jnp.sum(d_normed2 * hidden * scale_mlp, axis=0)
-
-    att_rows = att_out.reshape(n * CAP, rows)
-    d_obr = gather(mm(att_rows, d_hidden.astype(BF)).astype(BF).reshape(n, CAP, width), n, cid=0)
-    d_obr = (d_obr.astype(F32) * att_in_gate[..., None]).astype(BF).reshape(n * CAP, features)
-    d_attn = mm_t(d_obr, w_out[0]).astype(BF).reshape(n, CAP, heads, HD)
-    d_attn_back = a2a(d_attn.reshape(n, CAP, hw), n, cid=4)
+
+    d_obr, d_attn, dq_pre = attend_back(
+        d_obr, att_in_gate[..., None], w_out[0], query, keys, values, bias, turn_slots)
+    d_attn_back = a2a(d_attn, n, cid=4)
+    d_obr, dq_pre = d_obr.reshape(n * CAP, features), dq_pre.reshape(n * CAP, hw)
     w_out_grad = mm_rows(attn, d_obr)[None]
-    d_probs = jnp.einsum("gshd,gmhd->ghsm", d_attn, values, preferred_element_type=F32)
-    delta = jnp.sum(d_probs * probs, axis=-1, keepdims=True)
-    d_scores = (probs * (d_probs - delta)).astype(BF)
-    d_query = jnp.einsum("ghsm,gmhd->gshd", d_scores, keys, preferred_element_type=F32) / root
-    dq_pre = turn(d_query, q_cos, -q_sin).astype(BF).reshape(n * CAP, hw)
     w_query_grad = mm_rows(picked, dq_pre)[None]
     d_norm_q = mm_t(dq_pre, w_query[0]).reshape(n, CAP, features)
-
-    b_query = query_back.reshape(n * CAP, heads, HD)
-    b_d_attn = d_attn_back.reshape(n * CAP, heads, HD)
-    b_keys, b_values, b_seg, b_wpos = own(keys), own(values), own(seg), own(wpos)
-    r_seg = jnp.sum(att_rows.astype(F32) * b_seg[None, :], axis=-1)
-    r_wpos = jnp.sum(att_rows.astype(F32) * b_wpos[None, :], axis=-1)
-    b_allowed = (r_seg[:, None] == b_seg[None, :]) & (b_wpos[None, :] <= r_wpos[:, None])
-    b_scores = jnp.einsum("shd,mhd->hsm", b_query, b_keys, preferred_element_type=F32) / root
-    b_probs = jax.nn.softmax(jnp.where(b_allowed[None], b_scores, -1e30), axis=-1)
-    b_d_probs = jnp.einsum("shd,mhd->hsm", b_d_attn, b_values, preferred_element_type=F32)
-    b_delta = jnp.sum(b_d_probs * b_probs, axis=-1, keepdims=True)
-    b_d_scores = (b_probs * (b_d_probs - b_delta)).astype(BF)
-    d_values = jnp.einsum("hsm,shd->mhd", b_probs.astype(BF), b_d_attn, preferred_element_type=F32)
-    d_keys = jnp.einsum("hsm,shd->mhd", b_d_scores, b_query, preferred_element_type=F32) / root
-    d_keys = turn(d_keys, own(key_cos), -own(key_sin))
-    d_kv = jnp.concatenate([d_keys.reshape(rows, hw), d_values.reshape(rows, hw)], axis=1).astype(BF)
+    d_kv = keys_back(query_back, d_attn_back, own(keys), own(values), own(meta_all), own(meta_t), cos_t, sin_t)
     d_kv_all = a2a_copy(d_kv, n, cid=5)
-    w_kv_grad = mm_rows(normed_flat, d_kv_all.reshape(n * rows, 2 * hw)).reshape(features, 2, hw)
+    w_kv_grad = jnp.einsum(
+        "ld,lck->dck", normed_flat, d_kv_all.reshape(n * rows, 2, hw), preferred_element_type=F32)
     d_norm_kv = mm_t(d_kv, w_kv.reshape(features, 2 * hw)).reshape(rows // CAP, CAP, features)
 
     d_norm = reduce(jnp.concatenate([d_norm_q, d_norm_kv], axis=0), n, cid=3)
@@ -717,10 +1210,10 @@
     in_grad = d_hidden + scale_own * e1 - x_own * (scale_own * scale_own * scale_own) * (sum_1 / features)
     gain_attn_part = jnp.sum(d_normed * x_own * scale_own, axis=0)
 
-    gains = jnp.concatenate([gain_mlp_part[None], gain_attn_part[None], jnp.zeros((6, width), F32)], axis=0)
+    gains = jnp.concatenate([gain_mlp_part[:1], gain_attn_part[None], jnp.zeros((6, width), F32)], axis=0)
     gains = jnp.sum(gather(gains, n, bcast=True, cid=7), axis=0)
     back = jnp.concatenate(
-        [mixed_rows.astype(BF).reshape(n, per, width), in_grad.astype(BF).reshape(n, per, width)], axis=1
+        [mixed_rows.reshape(n, per, width), in_grad.astype(BF).reshape(n, per, width)], axis=1
     )
     back = gather(back, n, cid=6)
     mixed = mm_rows(sorter, back[:, :per].reshape(rows, features)).astype(BF)

time: 621 us -> 528 us (0.85)
  matrix products: 122 us -> 43.9 us
  other arithmetic: 51.8 us -> 18.4 us
  Pallas kernels: 339 us -> 361 us
  blocking collectives: 21.4 us -> 6.97 us
  between operations: 2.23 us -> 15 us
  starting transfers between devices: 7.8 us -> 15.2 us
  local copies, waits for them, and re-layouts: 67.6 us -> 60.4 us
    pallas_call x0 -> x5, Pallas kernels: none -> 184 us  [the longest x1 92.7 us: expert_layer(): pl.pallas_call(functools.partial(expert_body, n), out_shape=(sds((n, r, f...]
    pallas_call x6 -> x3, Pallas kernels: 157 us -> 76 us  [gather(): pl.pallas_call(functools.partial(gather_body, n, mode), out_shape=jax.Sha...]
    pallas_call x4 -> x1, Pallas kernels: 116 us -> 35.9 us  [reduce(): pl.pallas_call(functools.partial(reduce_body, n, nb), out_shape=jax.Shape...]
    dot_general x34 -> x16, matrix products: 101 us -> 35.5 us  [dot(): return lax.dot_general(a, b, dims, preferred_element_type=F32)]
    psum x2 -> x0, blocking collectives: 15.3 us -> none  [fast_local(): lax.psum((jnp.sum(hidden * hidden, axis=1, keepdims=True), jnp.sum(hidden...]
    dot_general x3 -> x0, local copies, waits for them, and re-layouts: 13.2 us -> none  [dot(): return lax.dot_general(a, b, dims, preferred_element_type=F32)]
    convert_element_type x5 -> x3, other arithmetic: 13.8 us -> 2.71 us  [the longest x1 1.73 us: fast_local(): x_own = part(own(x_all)).astype(F32)]
    all_to_all x1, starting transfers between devices: 7.8 us -> 15.1 us  [fast_local(): lax.all_to_all(query, 'dp', split_axis=0, concat_axis=0, tiled=True)]
  transfers between devices with their start and end apart: 1 -> 2, of which waited for: 0 -> 0; matrix products, arithmetic and copies ran while one was open for 26% -> 10% of each run, Pallas kernels for 30% -> 48%
where the time goes in v2:
time: 528 us; the launch traced here: 521 us
  Pallas kernels  361 us (68%)
  local copies, waits for them, and re-layouts  60.4 us (11%)
  matrix products  43.9 us (8%)
  other arithmetic  18.4 us (3%)
  starting transfers between devices  15.2 us (3%)
  between operations  15 us (3%)
  blocking collectives  6.97 us (1%)
    pallas_call x1, Pallas kernels, expert_layer(): pl.pallas_call(functools.partial(expert_body, n), out_shape=(sds((n, r, f...  92.7 us
    pallas_call x3, Pallas kernels, gather(): pl.pallas_call(functools.partial(gather_body, n, mode), out_shape=jax.Sha...  76 us
    pallas_call x2, Pallas kernels, a2a_copy(): pl.pallas_call(functools.partial(a2a_copy_body, n), out_shape=jax.ShapeDt...  52.2 us
    pallas_call x1, Pallas kernels, hidden_rows(): pl.pallas_call(functools.partial(hidden_body, n), out_shape=(jax.ShapeDty...  47.4 us
    pallas_call x1, Pallas kernels, reduce(): pl.pallas_call(functools.partial(reduce_body, n, nb), out_shape=jax.Shape...  35.9 us
    dot_general x16, matrix products, dot(): return lax.dot_general(a, b, dims, preferred_element_type=F32)  35.5 us
    pallas_call x1, Pallas kernels, attend(): pl.pallas_call(attend_body, grid=(n // pair,), out_shape=(sds((n, rows, f...  24.2 us
    unnamed x45, local copies, waits for them, and re-layouts  17.9 us
  transfers between devices with their start and end apart: 2, of which 0 were waited for; matrix products, arithmetic and copies ran while one was open for 10% of the time, Pallas kernels for 48%

profile of v2, /device:TPU:0, one launch (start us, length us, event | category | flops | bytes accessed | tf_op | source)
XLA Modules:
  0.0 520.6 jit_solution(3739749092808385086)
XLA Ops:
  14.3 2.4 select_reduce_fusion.1
  17.7 10.2 %copy_rows.2.meta = f32[8,16,128]{2,1,0:T(8,128)} custom-call(f32[16,128]{1,0:T(8,128)} %select_reduce_fusion.src), custom_call_target="tpu_custom_call" | custom-call | tf_op jit(solution)/shard_map/copy_rows/pallas_call | solution.py:503
  28.0 1.8 copy.54
  29.8 1.9 convolution_convert_fusion.3
  31.7 45.3 %gather_rows.3 = bf16[8,8,16,2048]{3,2,1,0:T(8,128)(2,1)} custom-call(bf16[8,16,512]{2,1,0:T(8,128)(2,1)} %bitcast.221), custom_call_target="tpu_custom_call" | custom-call | tf_op jit(solution)/shard_map/gather_rows/pallas_call | solution.py:430
  77.0 6.0 %fusion.55 = (bf16[2048,1,512]{2,1,0:T(2,128)(2,1)S(1)}, bf16[2048,1,512]{2,1,0:T(2,128)(2,1)S(1)}) fusion(bf16[2048,2,512]{2,1,0:T(2,128)(2,1)S(1)} %copy-done.2), kind=kLoop, calls=%fused_computation.146 | loop fusion | bytes 8388608 | tf_op jit(solution)/shard_map/slice | solution.py:1169
  83.0 3.2 copy_bitcast_fusion
  86.2 24.2 %attend.1 = (bf16[8,128,2048]{2,1,0:T(8,128)(2,1)}, bf16[8,64,2048]{2,1,0:T(8,128)(2,1)}, bf16[8,128,512]{2,1,0:T(8,128)(2,1)}, bf16[8,128,512]{2,1,0:T(8,128)(2...) custom-call(bf16[8,128,2048]{2,1,0:T(8,128)(2,1)} %bitcast.199, ...), custom_call_target="tpu_custom_call" | custom-call | tf_op jit(solution)/shard_map/attend/pallas_call | solution.py:985
  110.5 15.1 %all-to-all-start = ((bf16[8,64,512]{2,1,0:T(8,128)(2,1)}), bf16[8,64,512]{2,1,0:T(8,128)(2,1)S(1)}, u32[]{:S(2)}, u32[]{:S(2)}) async-start(bf16[8,64,512]{2,1,0:T(8,128)(2,1)} %get-tuple-element.41.query), calls=%async_computation | async-start | bytes 1048576 | tf_op jit(solution)/shard_map/all_to_all | solution.py:1172
  126.4 7.7 %reshape.621 = bf16[2048,1024,1]{1,0,2:T(8,128)(2,1)} reshape(bf16[2048,2,512]{2,1,0:T(2,128)(2,1)} %param.27) | data formatting | bytes 8388608 | tf_op jit(solution)/shard_map/reshape | solution.py:1202
  142.6 1.7 bitcast_convert_fusion.1.x_own
  144.4 47.4 %hidden_rows.1 = (f32[128,512]{1,0:T(8,128)}, bf16[8,64,2048]{2,1,0:T(8,128)(2,1)}, f32[128,1]{1,0:T(8,128)}) custom-call(bf16[512,512]{1,0:T(8,128)(2,1)} %bitcast.219, bf16[512,2048]{1,0:T(8,128)(2,1)} %bitcast.206, f32[128,512]{1,0:T(8,128)} %bitcast_convert_fusion.1.x_own, bf16[128,512]{1,0:T(8,128)(2,1)} %copy.55.comb, f32[512,1]{1,0:T(8,128)} %reshape.626.gates, ...), custom_call_target="tpu_custom_call" | custom-call | tf_op jit(solution)/shard_map/hidden_rows/pallas_call | solution.py:703
  197.7 2.5 copy.57
  201.0 2.0 multiply_convert_fusion
  203.1 92.7 %expert_layer.1 = (bf16[8,64,2048]{2,1,0:T(8,128)(2,1)}, f32[128,512]{1,0:T(8,128)}, bf16[128,512]{1,0:T(8,128)(2,1)}, f32[8,512]{1,0:T(8,128)}, bf16[512,2048]{...) custom-call(bf16[8,64,2048]{2,1,0:T(8,128)(2,1)} %get-tuple-element.34.hid_rows, ...), custom_call_target="tpu_custom_call" | custom-call | tf_op jit(solution)/shard_map/expert_layer/pallas_call | solution.py:852
  295.8 14.9 %attend_back.1 = (bf16[8,64,2048]{2,1,0:T(8,128)(2,1)}, bf16[8,64,512]{2,1,0:T(8,128)(2,1)}, bf16[8,64,512]{2,1,0:T(8,128)(2,1)}) custom-call(bf16[8,64,2048]{2,1,0:T(8,128)(2,1)} %get-tuple-element.40.rows_in, f32[8,64,1]{2,1,0:T(8,128)} %copy.60.gates, bf16[512,2048]{1,0:T(8,128)(2,1)} %bitcast.207, bf16[8,64,512]{2,1,0:T(8,128)(2,1)} %get-tuple-element.41.query, ...), custom_call_target="tpu_custom_call" | custom-call | tf_op jit(solution)/shard_map/attend_back/pallas_call | solution.py:1029
  310.7 12.8 %a2a_rows.1.d_attn = bf16[8,64,512]{2,1,0:T(8,128)(2,1)} custom-call(bf16[8,64,512]{2,1,0:T(8,128)(2,1)} %get-tuple-element.47.src), custom_call_target="tpu_custom_call" | custom-call | tf_op jit(solution)/shard_map/a2a_rows/pallas_call | solution.py:486
  325.1 4.6 keys_back.1.src
  329.7 42.0 %copy_rows.3 = bf16[8,128,1024]{2,1,0:T(8,128)(2,1)} custom-call(bf16[128,1024]{1,0:T(8,128)(2,1)} %keys_back.1.src), custom_call_target="tpu_custom_call" | custom-call | tf_op jit(solution)/shard_map/copy_rows/pallas_call | solution.py:503
  371.6 3.3 reshape.614
  374.9 6.4 %fusion.2 = f32[2048,2,512]{2,0,1:T(8,128)S(1)} fusion(bf16[1024,2048,1]{1,0,2:T(8,128)(2,1)} %bitcast.240, bf16[1024,2,512]{2,1,0:T(2,128)(2,1)S(1)} %reshape.614), kind=kOutput, calls=%fused_computation.14 | convolution fusion | flops 4294967296 | bytes 14680064 | tf_op jit(solution)/shard_map/ld,lck->dck/dot_general | solution.py:1200
  381.4 16.7 %copy.65 = f32[2048,2,512]{2,1,0:T(2,128)} copy(f32[2048,2,512]{2,0,1:T(8,128)S(1)} %fusion.2) | data formatting | bytes 16777216
  399.7 3.3 convolution_bitcast_fusion.4
  404.5 3.0 pad_maximum_fusion.src
  407.6 35.9 %reduce_rows.1 = bf16[10,64,512]{2,1,0:T(8,128)(2,1)} custom-call(f32[10,64,2048]{2,1,0:T(8,128)} %pad_maximum_fusion.src), custom_call_target="tpu_custom_call" | custom-call | tf_op jit(solution)/shard_map/reduce_rows/pallas_call | solution.py:469
  445.9 7.0 %psum.7 = f32[128,1]{0,1:T(1,128)S(1)} all-reduce(f32[128,1]{0,1:T(1,128)S(1)} %bitcast.243), channel_id=1, replica_groups=mesh['dp'=8,'tensor'=4] {'tensor'}, use_global_device_ids=true, to_apply=%region_11.12 | all-reduce | flops 128 | bytes 1024 | tf_op jit(solution)/shard_map/psum | solution.py:1209
  453.5 14.1 %gather_rows.5 = f32[8,8,2048]{2,1,0:T(8,128)} custom-call(f32[8,512]{1,0:T(8,128)} %maximum_maximum_fusion.src), custom_call_target="tpu_custom_call" | custom-call | tf_op jit(solution)/shard_map/gather_rows/pallas_call | solution.py:430
  471.2 16.5 %gather_rows.4 = bf16[8,32,2048]{2,1,0:T(8,128)(2,1)} custom-call(bf16[8,32,512]{2,1,0:T(8,128)(2,1)} %pad_maximum_fusion.1.src), custom_call_target="tpu_custom_call" | custom-call | tf_op jit(solution)/shard_map/gather_rows/pallas_call | solution.py:430
  491.3 3.3 convolution_bitcast_fusion.3
  494.6 6.1 %convolution_bitcast_fusion = f32[1,1408,2048]{2,1,0:T(8,128)} fusion(bf16[512,1408]{1,0:T(8,128)(2,1)S(1)} %copy-done.20, bf16[512,2048]{1,0:T(8,128)(2,1)S(1)} %bitcast.209), kind=kOutput, calls=%fused_computation | convolution fusion | flops 2952790016 | bytes 15073280 | tf_op jit(solution)/shard_map/dot_general | solution.py:510
  500.8 6.3 %convolution_bitcast_fusion.2 = f32[1,2048,1408]{2,1,0:T(8,128)} fusion(bf16[512,2048]{1,0:T(8,128)(2,1)S(1)} %copy-done.17, bf16[512,1408]{1,0:T(8,128)(2,1)S(1)} %copy-done.19), kind=kOutput, calls=%fused_computation.2 | convolution fusion | flops 2952790016 | bytes 15073280 | tf_op jit(solution)/shard_map/dot_general | solution.py:510
  507.1 6.3 %convolution_bitcast_fusion.1 = f32[1,2048,1408]{2,1,0:T(8,128)} fusion(bf16[512,2048]{1,0:T(8,128)(2,1)S(1)} %copy-done.17, bf16[512,1408]{1,0:T(8,128)(2,1)S(1)} %copy-done.18), kind=kOutput, calls=%fused_computation.1 | convolution fusion | flops 2952790016 | bytes 15073280 | tf_op jit(solution)/shard_map/dot_general | solution.py:510
  (125 shorter events, 38.8 us)
Async XLA Ops:
  7.2 2.0 copy-start
  7.2 190.5 %all-gather.3.cloned.1.call-start = ((), (), s32[]{:S(2)}) async-start(), calls=%async_computation.1 | async-start | bytes 4718592 | tf_op jit(solution)/shard_map/all_gather | solution.py:1178
  29.8 47.2 %copy-start.2 = (bf16[2048,2,512]{2,1,0:T(2,128)(2,1)S(1)}, bf16[2048,2,512]{2,1,0:T(2,128)(2,1)}, u32[]{:S(2)}) copy-start(bf16[2048,2,512]{2,1,0:T(2,128)(2,1)} %param.27) | copy-start | bytes 12582916
  110.5 213.8 %all-to-all-start = ((bf16[8,64,512]{2,1,0:T(8,128)(2,1)}), bf16[8,64,512]{2,1,0:T(8,128)(2,1)S(1)}, u32[]{:S(2)}, u32[]{:S(2)}) async-start(bf16[8,64,512]{2,1,0:T(8,128)(2,1)} %get-tuple-element.41.query), calls=%async_computation | async-start | bytes 1048576 | tf_op jit(solution)/shard_map/all_to_all | solution.py:1172
  126.4 9.2 %copy-start.12 = (f32[8,16,128]{2,1,0:T(8,128)S(1)}, f32[8,16,128]{2,1,0:T(8,128)}, u32[]{:S(2)}) copy-start(f32[8,16,128]{2,1,0:T(8,128)} %copy_rows.2.meta) | copy-start | bytes 196612
  136.2 8.2 %copy-start.7 = (bf16[512,128]{1,0:T(8,128)(2,1)}, bf16[512,128]{1,0:T(8,128)(2,1)S(1)}, u32[]{:S(2)}) copy-start(bf16[512,128]{1,0:T(8,128)(2,1)S(1)} %get-tuple-element.109.pick.mlp_rows) | copy-start | bytes 393220
  136.2 64.0 %copy-start.11 = (bf16[512,128]{1,0:T(8,128)(2,1)}, bf16[512,128]{1,0:T(8,128)(2,1)S(1)}, u32[]{:S(2)}) copy-start(bf16[512,128]{1,0:T(8,128)(2,1)S(1)} %get-tuple-element.110.att_rows) | copy-start | bytes 393220
  324.3 0.8 copy-start.8
  381.3 16.8 %copy-start.4 = (bf16[1,2048,512]{2,1,0:T(8,128)(2,1)S(1)}, bf16[1,2048,512]{2,1,0:T(8,128)(2,1)}, u32[]{:S(2)}) copy-start(bf16[1,2048,512]{2,1,0:T(8,128)(2,1)} %param.28) | copy-start | bytes 6291460
  381.4 16.8 %copy-start.13 = (bf16[8,64,512]{2,1,0:T(8,128)(2,1)S(1)}, bf16[8,64,512]{2,1,0:T(8,128)(2,1)}, u32[]{:S(2)}) copy-start(bf16[8,64,512]{2,1,0:T(8,128)(2,1)} %get-tuple-element.46) | copy-start | bytes 1572868
  398.1 1.6 copy-start.16
  399.7 3.3 copy-start.3
  399.7 3.3 copy-start.6
  407.5 61.8 %copy-start.14 = (f32[128,512]{1,0:T(8,128)S(1)}, f32[128,512]{1,0:T(8,128)}, u32[]{:S(2)}) copy-start(f32[128,512]{1,0:T(8,128)} %get-tuple-element.38) | copy-start | bytes 786436
  407.6 62.9 %copy-start.15 = (bf16[128,512]{1,0:T(8,128)(2,1)S(1)}, bf16[128,512]{1,0:T(8,128)(2,1)}, u32[]{:S(2)}) copy-start(bf16[128,512]{1,0:T(8,128)(2,1)} %get-tuple-element.37) | copy-start | bytes 393220
  445.9 45.5 %copy-start.9 = (bf16[8,64,2048]{2,1,0:T(8,128)(2,1)S(1)}, bf16[8,64,2048]{2,1,0:T(8,128)(2,1)}, u32[]{:S(2)}) copy-start(bf16[8,64,2048]{2,1,0:T(8,128)(2,1)} %get-tuple-element.51) | copy-start | bytes 6291460
  445.9 45.5 %copy-start.10 = (bf16[8,64,512]{2,1,0:T(8,128)(2,1)S(1)}, bf16[8,64,512]{2,1,0:T(8,128)(2,1)}, u32[]{:S(2)}) copy-start(bf16[8,64,512]{2,1,0:T(8,128)(2,1)} %get-tuple-element.33) | copy-start | bytes 1572868
  490.2 4.4 copy-start.5
  490.2 4.4 copy-start.20
  494.6 6.1 %copy-start.17 = (bf16[512,2048]{1,0:T(8,128)(2,1)S(1)}, bf16[512,2048]{1,0:T(8,128)(2,1)}, u32[]{:S(2)}) copy-start(bf16[512,2048]{1,0:T(8,128)(2,1)} %get-tuple-element.52) | copy-start | bytes 6291460
  494.6 6.1 %copy-start.19 = (bf16[512,1408]{1,0:T(8,128)(2,1)S(1)}, bf16[512,1408]{1,0:T(8,128)(2,1)}, u32[]{:S(2)}) copy-start(bf16[512,1408]{1,0:T(8,128)(2,1)} %get-tuple-element.53) | copy-start | bytes 4325380
  500.8 6.3 %copy-start.18 = (bf16[512,1408]{1,0:T(8,128)(2,1)S(1)}, bf16[512,1408]{1,0:T(8,128)(2,1)}, u32[]{:S(2)}) copy-start(bf16[512,1408]{1,0:T(8,128)(2,1)} %get-tuple-element.54) | copy-start | bytes 4325380
  507.1 6.3 %copy-start.1 = (bf16[128,2048]{1,0:T(8,128)(2,1)S(1)}, bf16[128,2048]{1,0:T(8,128)(2,1)}, u32[]{:S(2)}) copy-start(bf16[128,2048]{1,0:T(8,128)(2,1)} %param.19) | copy-start | bytes 1572868
Sparse Core Ops, SparseCore 0:
  10.5 90.2 all-gather.2

commit v3 on v2

--- a/solution.py
+++ b/solution.py
@@ -528,9 +528,10 @@
         self.g, self.t, self.tx, self.tc = ranks()
         self.tcx = lax.rem(self.tc + 2, 4)
         self.tail = []
+        self.dest = [lax.rem(self.g + o, n) for o in range(n)]
 
     def to(self, o):
-        return lax.rem(self.g + o, self.n)
+        return self.dest[o]
 
     def greet_all(self):
         greet([(self.to(o), self.t) for o in range(1, self.n)] + [(self.g, self.tx), (self.g, self.tc)])
@@ -609,37 +610,42 @@
 
 class Gather:
     def __init__(self, ring, width, full, sbuf, sems):
-        self.ring, self.width, self.full, self.sbuf = ring, width, full, sbuf
-        self.ss, self.rs, self.xs, self.xr, self.cs, self.cr, self.c2s, self.c2r = sems
-        self.d, self.x, self.c = {}, {}, []
-
-    def at(self, q, j):
-        return cols_of(q, j, self.width, self.sbuf.shape[-1])
+        self.ring, self.full, self.sbuf = ring, full, sbuf
+        ss, rs, xs, xr, cs, cr, c2s, c2r = sems
+        k, (nc, n, _, cw) = ring, sbuf.shape
+        self.d, self.x, self.c, self.c2, self.own = {}, {}, {}, {}, {}
+        for j in range(nc):
+            cc, cx = cols_of(k.t, j, width, cw), cols_of(k.tx, j, width, cw)
+            self.own[j] = cc
+            for o in range(1, n):
+                d = k.to(o)
+                self.d[j, o] = rcopy(sbuf.at[j, d], full.at[k.g, :, cc], ss.at[j, o], rs.at[j, o], d, k.t)
+            ref, ref2 = full.at[:, :, cc], full.at[:, :, cx]
+            self.x[j] = rcopy(ref, ref, xs.at[j], xr.at[j], k.g, k.tx)
+            self.c[j] = rcopy(ref, ref, cs.at[j], cr.at[j], k.g, k.tc)
+            self.c2[j] = rcopy(ref2, ref2, c2s.at[j], c2r.at[j], k.g, k.tc)
 
     def out(self, j, rows):
-        k, cc = self.ring, self.at(self.ring.t, j)
         self.sbuf[j] = rows.reshape(self.sbuf.shape[1:])
-        for o in range(1, k.n):
-            d = k.to(o)
-            self.d[j, o] = k.send(
-                self.sbuf.at[j, d], self.full.at[k.g, :, cc], self.ss.at[j, o], self.rs.at[j, o], d, k.t)
-        self.full[k.g, :, cc] = self.sbuf[j, k.g]
+        for o in range(1, self.ring.n):
+            self.d[j, o].start()
+        self.full[self.ring.g, :, self.own[j]] = self.sbuf[j, self.ring.g]
 
     def cross(self, j):
-        k, ref = self.ring, self.full.at[:, :, self.at(self.ring.t, j)]
-        for o in range(1, k.n):
+        for o in range(1, self.ring.n):
             self.d[j, o].wait_recv()
-        self.x[j] = k.send(ref, ref, self.xs.at[j], self.xr.at[j], k.g, k.tx)
-        self.c.append(k.send(ref, ref, self.cs.at[j], self.cr.at[j], k.g, k.tc))
+        self.x[j].start()
+        self.c[j].start()
 
     def core(self, j):
-        k, ref = self.ring, self.full.at[:, :, self.at(self.ring.tx, j)]
         self.x[j].wait_recv()
-        self.c.append(k.send(ref, ref, self.c2s.at[j], self.c2r.at[j], k.g, k.tc))
+        self.c2[j].start()
 
     def finish(self):
-        for c in self.c:
+        for c in list(self.c.values()) + list(self.c2.values()):
             c.wait_recv()
+        for c in [*self.d.values(), *self.x.values(), *self.c.values(), *self.c2.values()]:
+            c.wait_send()
 
 
 def paired(reduce_one, gather_one, middle, nc):
@@ -932,10 +938,31 @@
 
 
 def attend_body(
-    x, gain, w_k, w_v, w_q, meta, meta_t, cos_t, sin_t,
-    normed, picked, keys, values, query, attn, scale, bias, turn_slots, k_scr, v_scr, q_scr, n_scr,
+    n, x, gain, w_k, w_v, w_q, meta, cos_t, sin_t, dy_part, dy_gate,
+    normed, picked, keys, values, query, attn, scale, bias, turn_slots, d_mbr, k_scr, v_scr, q_scr, n_scr, dy_rows,
+    xs, xr, cs, cr,
 ):
-    me = lax.axis_index("dp").astype(F32)
+    step = pl.program_id(0)
+    ring = Ring(n)
+    width = dy_part.shape[2]
+
+    near, far = [dy_rows.at[:, :, cols_of(q, 0, width, width)] for q in (ring.t, ring.tx)]
+    over_x = rcopy(near, near, xs, xr, ring.g, ring.tx)
+    to_core = [rcopy(ref, ref, cs.at[i], cr.at[i], ring.g, ring.tc) for i, ref in enumerate((near, far))]
+
+    @pl.when(step == 0)
+    def _():
+        greet([(ring.g, ring.tx), (ring.g, ring.tc)])
+        near[...] = dy_part[...]
+        over_x.start()
+        to_core[0].start()
+
+    @pl.when(step == 2)
+    def _():
+        over_x.wait_recv()
+        to_core[1].start()
+
+    me = ring.g.astype(F32)
     pair, rows, features = x.shape
     cap = picked.shape[1]
     heads = w_q.shape[1] // HD
@@ -948,7 +975,8 @@
     k_all, v_all = mm(n_scr[...], w_k[...]), mm(n_scr[...], w_v[...])
     slots = []
     for p in range(pair):
-        m, m_t = meta[p], meta_t[p]
+        m = meta[p]
+        m_t = m.T
         table = slot_table(m, META["ar0"], me, cap)
         at_pos = position_rows(m_t)
         rr = slice(p * rows, (p + 1) * rows)
@@ -975,27 +1003,36 @@
             probs = softmax_rows(scores).astype(BF)
             attn[p, :, hh] = mm(probs, v_scr[p, :, hh]).astype(BF)
 
-
-def attend(x_all, gain, w_k, w_v, w_q, meta, meta_t, cos_t, sin_t):
+    @pl.when(step == 3)
+    def _():
+        for c in to_core:
+            c.wait()
+        over_x.wait_send()
+        for e in range(n):
+            d_mbr[e] = (dy_rows[e].astype(F32) * dy_gate[e]).astype(BF)
+
+
+def attend(x_all, gain, w_k, w_v, w_q, meta, cos_t, sin_t, dy_part, dy_gate, cid):
     n, rows, features = x_all.shape
     hw, cap, pair = w_q.shape[1], CAP, 2
     sds = jax.ShapeDtypeStruct
     block = lambda *s: pl.BlockSpec((pair,) + s, lambda i: (i,) + (0,) * len(s))
     whole = lambda a: pl.BlockSpec(a.shape, lambda i: (0,) * a.ndim)
     return pl.pallas_call(
-        attend_body, grid=(n // pair,),
+        functools.partial(attend_body, n), grid=(n // pair,),
         out_shape=(
             sds((n, rows, features), BF), sds((n, cap, features), BF), sds((n, rows, hw), BF), sds((n, rows, hw), BF),
             sds((n, cap, hw), BF), sds((n, cap, hw), BF), sds((n, rows, 1), F32), sds((n, cap, rows), F32),
-            sds((n, cap, 2 * HD), F32)),
-        in_specs=[block(rows, features), whole(gain), whole(w_k), whole(w_v), whole(w_q), block(16, rows), block(rows, 16),
-                  whole(cos_t), whole(sin_t)],
+            sds((n, cap, 2 * HD), F32), sds((n, cap, features), BF)),
+        in_specs=[block(rows, features), whole(gain), whole(w_k), whole(w_v), whole(w_q), block(16, rows),
+                  whole(cos_t), whole(sin_t), whole(dy_part), whole(dy_gate)],
         out_specs=(
             block(rows, features), block(cap, features), block(rows, hw), block(rows, hw), block(cap, hw), block(cap, hw),
-            block(rows, 1), block(cap, rows), block(cap, 2 * HD)),
-        scratch_shapes=[VM((pair, rows, hw), BF), VM((pair, rows, hw), BF), VM((pair, cap, hw), BF), VM((pair * rows, features), BF)],
-        name="attend", compiler_params=pltpu.CompilerParams(vmem_limit_bytes=56 * 2**20),
-    )(x_all, gain, w_k, w_v, w_q, meta, meta_t, cos_t, sin_t)
+            block(rows, 1), block(cap, rows), block(cap, 2 * HD), pl.BlockSpec((n, cap, features), lambda i: (0, 0, 0))),
+        scratch_shapes=[VM((pair, rows, hw), BF), VM((pair, rows, hw), BF), VM((pair, cap, hw), BF), VM((pair * rows, features), BF),
+                        VM((n, cap, features), BF), DMA, DMA, DMA((2,)), DMA((2,))],
+        name="attend", compiler_params=params(cid),
+    )(x_all, gain, w_k, w_v, w_q, meta, cos_t, sin_t, dy_part, dy_gate)
 
 
 def attend_back_body(rows_in, gates, w_o, query, keys, values, bias, turn_slots, d_obr, d_attn, dq_pre, o_scr):
@@ -1037,10 +1074,11 @@
     )(rows_in, gates, w_o, query, keys, values, bias, turn_slots)
 
 
-def keys_back_body(query, d_attn, keys, values, meta, meta_t, cos_t, sin_t, d_kv, *, cap):
+def keys_back_body(query, d_attn, keys, values, meta, cos_t, sin_t, d_kv, *, cap):
     n = query.shape[0]
     hw = keys.shape[1]
-    m, m_t = meta[...], meta_t[...]
+    m = meta[...]
+    m_t = m.T
     tables = jnp.concatenate([slot_table(m, META["ar0"], float(e), cap) for e in range(n)], axis=0)
     bias = (mm(tables, allowed_pairs(m, m_t)) - 1.0) * 1e30
     at_pos = position_rows(m_t)
@@ -1060,50 +1098,394 @@
         d_kv[:, hh] = turned(d_k, cosine, -sine).astype(BF)
 
 
-def keys_back(query, d_attn, keys, values, meta, meta_t, cos_t, sin_t):
-    rows, hw = keys.shape
-    args = (query, d_attn, keys, values, meta, meta_t, cos_t, sin_t)
+def map_grad_body(normed, d_kv, out, d_cols):
+    hw = d_kv.shape[1] // 2
+
+    @pl.when(pl.program_id(0) == 0)
+    def _():
+        for i in range(hw // 128):
+            for c in range(2):
+                d_cols[:, (2 * i + c) * 128:(2 * i + c + 1) * 128] = d_kv[:, c * hw + i * 128:c * hw + (i + 1) * 128]
+
+    out[...] = mm_rows(normed[...], d_cols[...]).reshape(out.shape)
+
+
+def map_grad(normed, d_kv):
+    total, features = normed.shape
+    both = d_kv.shape[1]
+    size, tiles = 256, both // 128
+    out = pl.pallas_call(
+        map_grad_body, grid=(features // size,),
+        out_shape=jax.ShapeDtypeStruct((features, tiles, 128), F32),
+        in_specs=[pl.BlockSpec((total, size), lambda i: (0, i)), pl.BlockSpec((total, both), lambda i: (0, 0))],
+        out_specs=pl.BlockSpec((size, tiles, 128), lambda i: (i, 0, 0)), scratch_shapes=[VM((total, both), BF)],
+        name="map_grad", compiler_params=pltpu.CompilerParams(vmem_limit_bytes=56 * 2**20),
+    )(normed, d_kv)
+    return out.reshape(features, tiles // 2, 2, 128).transpose(0, 2, 1, 3).reshape(features, 2, both // 2)
+
+
+def tail_body(
+    n, dq_pre, w_q, d_attn, q_back, keys, values, meta, cos_t, sin_t, w_k, w_v,
+    x_own, scale, gain_t, d_hidden, mixed, gain_mlp_part, comb, d_kv_all, back, gains, *scratch,
+):
+    ring = Ring(n)
+    bufs = scratch[:7]
+    at_in, d_kv, kc_out, kc_in, kv_keep, kx_out, kx_in, sbuf, sq, sq_in, g_out, g_in, g_sum, d_norm = scratch[7:21]
+    (as_, ar, zs, zr, ws, wr, ys, yr, ks, kr, lxs, lxr, qs, qr, gs, gr, ts, tr) = scratch[21:39]
+    sems, fsems = scratch[39:45], scratch[45:]
+    rows, width = x_own.shape
+    hw = keys.shape[2]
+    features = 4 * width
+    keys, values, meta, scale = keys.at[ring.g], values.at[ring.g], meta.at[ring.g], scale.at[ring.g]
+    z, y = ring.g // 2, lax.rem(ring.g, 2)
+    depth = n // 2
+    ring.greet_everyone()
+
+    arrive = []
+    for o in range(1, n):
+        d = ring.to(o)
+        arrive.append(ring.send(d_attn.at[d], at_in.at[ring.g], as_.at[o], ar.at[o], d, ring.t))
+    at_in[ring.g] = d_attn[ring.g]
+    red = Reduce(
+        ring, lambda q: mm_t(dq_pre[...], w_q[cols_of(q, 0, width, width), :]), bufs, sems)
+    red.core()
+    for c in arrive:
+        c.wait_recv()
+    red.home(0)
+    keys_back_body(q_back, at_in, keys, values, meta, cos_t, sin_t, d_kv, cap=q_back.shape[1])
+    red.home(1)
+
+    halves = [(c, slice(c * hw, (c + 1) * hw)) for c in range(2)]
+    mine = d_kv_all.at[ring.g]
+    mine[...] = d_kv[...]
+    pairs = lambda zz, yy: zz * 2 + yy
+    across = []
+
+    def unit(zz, c):
+        return d_kv_all.at[pairs(zz, y), :, pl.ds(c * hw, hw)]
+
+    def step(up, hop, c, first):
+        zz = z - hop if up else z + hop
+        here = zz >= 0 if up else zz < depth
+        ss, rs = (zs, zr) if up else (ws, wr)
+        on, back_to = (z + 1, z - 1) if up else (z - 1, z + 1)
+
+        @pl.when(here)
+        def _():
+            ref = unit(zz, c)
+            if not first:
+                rcopy(ref, ref, ss.at[hop - 1, c], rs.at[hop - 1, c], pairs(back_to, y), ring.t).wait_recv()
+
+            @pl.when((on < depth) if up else (on >= 0))
+            def _():
+                rcopy(ref, ref, ss.at[hop, c], rs.at[hop, c], pairs(on, y), ring.t).start()
+
+            if up or not first:
+                rcopy(ref, ref, ys.at[zz, c], yr.at[zz, c], pairs(z, 1 - y), ring.t).start()
+
+    def drain(up, hop, c):
+        zz = z - hop if up else z + hop
+        here = zz >= 0 if up else zz < depth
+        ss, rs = (zs, zr) if up else (ws, wr)
+        on = z + 1 if up else z - 1
+
+        @pl.when(here & ((on < depth) if up else (on >= 0)))
+        def _():
+            ref = unit(zz, c)
+            rcopy(ref, ref, ss.at[hop, c], rs.at[hop, c], pairs(on, y), ring.t).wait_send()
+
+    def spread(hop):
+        for c, _ in halves:
+            step(True, hop, c, hop == 0)
+            step(False, hop, c, hop == 0)
+
+    spread(0)
+
+    def kv_part(q):
+        at = cols_of(q, 0, width, width)
+        return mm_t(d_kv[:, :hw], w_k[at, :]) + mm_t(d_kv[:, hw:], w_v[at, :])
+
+    kc_out[0] = kv_part(ring.tc).astype(BF)
+    kc_out[1] = kv_part(ring.tcx).astype(BF)
+    kc = ring.send(kc_out, kc_in, ks, kr, ring.g, ring.tc)
+    red.home(2)
+    kv_keep[1] = kv_part(ring.tx)
+    kc.wait_recv()
+    kx_out[...] = (kv_keep[1] + kc_in[1].astype(F32)).astype(BF)
+    kx = ring.send(kx_out, kx_in, lxs, lxr, ring.g, ring.tx)
+    kv_keep[0] = kv_part(ring.t)
+    red.home(3)
+    spread(1)
+    kx.wait_recv()
+    local = kv_keep[0] + kc_in[0].astype(F32) + kx_in[...].astype(F32)
+    cw = width // NC
+    squares = jnp.zeros((8, rows), F32)
+    for j in range(NC):
+        cc = slice(j * cw, (j + 1) * cw)
+        got = mm(comb[...], red.rows(j)) + local[:, cc]
+        d_norm[:, cc] = got
+        high, low = split_bf(x_own[:, cc] * gain_t[:, cc] * got)
+        ones = jnp.ones((8, cw), BF)
+        squares = squares + mm_t(ones, high) + mm_t(ones, low)
+        g_out[:, cc] = jnp.concatenate([
+            gain_mlp_part[:1, cc], jnp.sum(got * x_own[:, cc] * scale[...], axis=0, keepdims=True), jnp.zeros((6, cw), F32)], axis=0)
+    sq[...] = squares
+    shared = [ring.send(sq, sq_in.at[i], qs.at[i], qr.at[i], ring.g, q) for i, q in enumerate([ring.tc, ring.tx, ring.tcx])]
+    sums = []
+    for o in range(1, n):
+        sums.append(ring.send(g_out, g_in.at[ring.g], gs.at[o], gr.at[o], ring.to(o), ring.t))
+    g_in[ring.g] = g_out[...]
+    for c in shared:
+        c.wait_recv()
+    total = (sq[...] + sq_in[0] + sq_in[1] + sq_in[2])[:1]
+    eye = iota((rows, rows), 0) == iota((rows, rows), 1)
+    mean = jnp.sum(jnp.where(eye, total, 0.0), axis=1, keepdims=True) / features
+    s = scale[...]
+    in_grad = d_hidden[...] + s * (gain_t[...] * d_norm[...]) - x_own[...] * (s * s * s * mean)
+    per = rows // n
+    fin = Gather(ring, width, back, sbuf, fsems)
+    fin.out(0, jnp.concatenate(
+        [mixed[...].reshape(n, per, width), in_grad.astype(BF).reshape(n, per, width)], axis=1))
+    for c in sums:
+        c.wait_recv()
+    g_sum[...] = functools.reduce(lambda a, b: a + b, [g_in[e] for e in range(n)])
+    at_t = cols_of(ring.t, 0, width, width)
+    gains[:, at_t] = g_sum[...]
+    told = [ring.send(g_sum, gains.at[:, at_t], ts.at[i], tr.at[i], ring.g, q) for i, q in enumerate([ring.tc, ring.tx, ring.tcx])]
+    spread(2)
+    fin.cross(0)
+    spread(3)
+    fin.core(0)
+    fin.finish()
+    for c in told:
+        c.wait_recv()
+    for c, _ in halves:
+        for zz in range(depth):
+            ref = d_kv_all.at[pairs(zz, 1 - y), :, pl.ds(c * hw, hw)]
+            rcopy(ref, ref, ys.at[zz, c], yr.at[zz, c], pairs(z, 1 - y), ring.t).wait()
+        for hop in range(depth - 1):
+            drain(True, hop, c)
+            drain(False, hop, c)
+    ring.finish()
+
+
+def layer_tail(args, n, cid):
+    dq_pre, w_q, d_attn, q_back, keys = args[:5]
+    x_own = args[11]
+    rows, width = x_own.shape
+    cap, hw = d_attn.shape[1:]
+    cw, features, depth = width // NC, 4 * width, n // 2
+    sds = jax.ShapeDtypeStruct
+    per = 2 * rows // n
     return pl.pallas_call(
-        functools.partial(keys_back_body, cap=query.shape[1]),
-        out_shape=jax.ShapeDtypeStruct((rows, 2 * hw), BF),
-        in_specs=[pl.BlockSpec(memory_space=VM)] * len(args), out_specs=pl.BlockSpec(memory_space=VM),
-        name="keys_back", compiler_params=pltpu.CompilerParams(vmem_limit_bytes=56 * 2**20),
+        functools.partial(tail_body, n),
+        out_shape=(sds((n, rows, 2 * hw), BF), sds((n, per, features), BF), sds((8, features), F32)),
+        in_specs=[pl.BlockSpec(memory_space=VM)] * len(args), out_specs=[pl.BlockSpec(memory_space=VM)] * 3,
+        scratch_shapes=REDUCE_BUFS(NC, n, cap, cw) + [
+            VM((n, cap, hw), BF), VM((rows, 2 * hw), BF), VM((2, rows, width), BF), VM((2, rows, width), BF),
+            VM((2, rows, width), F32), VM((rows, width), BF), VM((rows, width), BF), VM((1, n, per, width), BF),
+            VM((8, rows), F32), VM((3, 8, rows), F32), VM((8, width), F32), VM((n, 8, width), F32), VM((8, width), F32),
+            VM((rows, width), F32),
+            DMA((n,)), DMA((n,)), DMA((depth, 2)), DMA((depth, 2)), DMA((depth, 2)), DMA((depth, 2)), DMA((depth, 2)), DMA((depth, 2)),
+            DMA, DMA, DMA, DMA, DMA((3,)), DMA((3,)), DMA((n,)), DMA((n,)), DMA((3,)), DMA((3,))]
+        + REDUCE_SEMS(NC, n) + GATHER_SEMS(1, n),
+        name="layer_tail", compiler_params=params(cid),
     )(*args)
 
 
-def slots_of(route_a, route_b, names, cap):
-    tokens = route_a.shape[-1]
-    member = (route_a == names) | (route_b == names)
-    before = (jnp.arange(tokens)[:, None] < jnp.arange(tokens)[None, :]).astype(BF)
-    rank = mm(member.astype(BF), before)
-    slot = jnp.arange(cap, dtype=F32)[None, :, None]
-    return ((rank[:, None, :] == slot) & member[:, None, :]).astype(BF)
-
-
-def slot_gate(table, route_a, route_b, gate_a, gate_b, names):
-    per_token = jnp.where(route_a == names, gate_a, 0.0) + jnp.where(route_b == names, gate_b, 0.0)
-    return jnp.sum(table.astype(F32) * per_token[:, None, :], axis=-1)
-
-
-def weigh(table, gates, rows):
-    slots = table.reshape(-1, table.shape[-1])
-    scaled = rows.reshape(slots.shape[0], -1).astype(F32) * gates.reshape(-1, 1)
-    high = scaled.astype(BF)
-    low = (scaled - high.astype(F32)).astype(BF)
-    return mm_rows(slots, high) + mm_rows(slots, low)
-
-
-def angles(positions):
-    half = HD // 2
-    frequency = jnp.exp(-math.log(THETA) * jnp.arange(half, dtype=F32) / half)
-    turned = positions[..., None] * frequency
-    return jnp.cos(turned)[..., None, :], jnp.sin(turned)[..., None, :]
-
-
-def turn(vectors, cosine, sine):
-    half = HD // 2
-    a, b = vectors[..., :half], vectors[..., half:]
-    return jnp.concatenate([a * cosine - b * sine, b * cosine + a * sine], axis=-1)
+def start_body(
+    n, tokens, out_grad, place_r, place_c, meta_w, w_kv, x_all, dy_own, meta_all, sorter_out,
+    att_rows, att_gate, mlp_rows, mlp_gate, in_gate, w_k, w_v, x_own, dy_part, dy_send, dy_slots, *sems,
+):
+    ms, mr, dys, dyr, dps, dpr, zs, zr, ws, wr, ys, yr, xs, xr, cs, cr = sems
+    ring = Ring(n)
+    g, t = ring.g, ring.t
+    rows, features = tokens.shape
+    width, per = features // 4, rows // n
+    z, y, depth = g // 2, lax.rem(g, 2), n // 2
+    pairs = lambda zz, yy: zz * 2 + yy
+    ring.greet_all()
+
+    def arrival(row, col):
+        g_row, g_col = row // rows, col // rows
+        before = (g_col == g_row) & (iota((rows, rows), 0) < iota((rows, rows), 1))
+        return g_row, jnp.sum(jnp.where(before, 1.0, 0.0), axis=0, keepdims=True).astype(jnp.int32)
+
+    col_g = jnp.sum(jnp.where(iota((rows, n), 1) == g, place_c[...], 0), axis=1, keepdims=True)
+    g_row, rank = arrival(place_r[pl.ds(g, 1), :], col_g)
+    sorter = jnp.where(g_row * per + rank == iota((rows, rows), 0), 1.0, 0.0).astype(BF)
+    sorter_out[...] = sorter
+
+    half = width // 2
+    chunks = [("b", t, half), ("a", t, 0), ("c", ring.tx, 0)]
+    cols = [pl.ds(pl.multiple_of(q * width + off, half), half) for _, q, off in chunks]
+    for cc in cols:
+        x_all[:, g, :, cc] = mm(sorter, tokens[:, cc]).astype(BF).reshape(n, per, half)
+
+    def unit(zz, yy, c):
+        return x_all.at[:, pairs(zz, yy), :, cols[c]]
+
+    def cross(zz, yy, c):
+        if chunks[c][0] == "b":
+            ref = unit(zz, yy, c)
+            rcopy(ref, ref, xs.at[pairs(zz, yy)], xr.at[pairs(zz, yy)], g, ring.tx).start()
+
+    def hop_on(up, hop, c):
+        zz = z - hop if up else z + hop
+        here = zz >= 0 if up else zz < depth
+        ss, rs = (zs, zr) if up else (ws, wr)
+        on, source = (z + 1, z - 1) if up else (z - 1, z + 1)
+
+        @pl.when(here)
+        def _():
+            ref = unit(zz, y, c)
+            if hop:
+                rcopy(ref, ref, ss.at[hop - 1, c], rs.at[hop - 1, c], pairs(source, y), t).wait_recv()
+
+            @pl.when((on < depth) if up else (on >= 0))
+            def _():
+                rcopy(ref, ref, ss.at[hop, c], rs.at[hop, c], pairs(on, y), t).start()
+
+            if up or hop:
+                rcopy(ref, ref, ys.at[zz, c], yr.at[zz, c], pairs(z, 1 - y), t).start()
+                cross(zz, y, c)
+
+    def from_y(zz, c):
+        ref = unit(zz, 1 - y, c)
+        rcopy(ref, ref, ys.at[zz, c], yr.at[zz, c], pairs(z, 1 - y), t).wait_recv()
+        cross(zz, 1 - y, c)
+
+    count = range(len(chunks))
+    for c in count:
+        hop_on(True, 0, c)
+        hop_on(False, 0, c)
+
+    spot = jnp.zeros((rows, rows), F32)
+    for s in range(n):
+        row, col = place_r[s:s + 1, :], place_c[:, s:s + 1]
+        s_row, s_rank = arrival(row, col)
+        put = jnp.where((s_row == g) & (s_rank + s * per == iota((rows, rows), 0)), 1.0, 0.0).astype(BF)
+        work = jnp.where(col - col // rows * rows == iota((rows, rows), 1), 1.0, 0.0).astype(BF)
+        spot = spot + mm(put, work)
+    spot = spot.astype(BF)
+    left, moved = meta_w[...], 0.0
+    for _ in range(3):
+        piece = left.astype(BF)
+        moved = moved + mm_t(piece, spot)
+        left = left - piece.astype(F32)
+    meta_all[g] = moved
+    sent = [ring.send(meta_all.at[g], meta_all.at[g], ms.at[o], mr.at[o], ring.to(o), t) for o in range(1, n)]
+
+    mine = pl.ds(pl.multiple_of(t * width, width), width)
+    dy_send[...] = mm(sorter, out_grad[:, mine]).astype(BF).reshape(n, per, width)
+    dealt = [ring.send(dy_send.at[ring.to(o)], dy_own.at[g], dys.at[o], dyr.at[o], ring.to(o), t) for o in range(1, n)]
+    dy_own[g] = dy_send[g]
+
+    def split(i):
+        rr = slice(i * 256, (i + 1) * 256)
+        w_k[rr] = w_kv[rr, 0, :]
+        w_v[rr] = w_kv[rr, 1, :]
+
+    def tables(first, gate, out_rows, out_gate):
+        m = meta_all[g]
+        for e in range(n):
+            out_rows[e] = slot_table(m, first, float(e), CAP)
+            out_gate[e] = slot_gates(m, first, gate, float(e), out_rows[e])
+
+    def hops(k):
+        for c in count:
+            hop_on(True, k, c)
+            hop_on(False, k, c)
+
+    tables(META["mr0"], META["mg0"], mlp_rows, mlp_gate)
+    split(0)
+    hops(1)
+    for c in dealt:
+        c.wait_recv()
+    slots = mm(mlp_rows[...].reshape(n * CAP, rows), dy_own[...].reshape(rows, width)).astype(BF)
+    dy_slots[...] = slots.reshape(n, CAP, width)
+    parts = [ring.send(dy_slots.at[ring.to(o)], dy_part.at[g], dps.at[o], dpr.at[o], ring.to(o), t) for o in range(1, n)]
+    dy_part[g] = dy_slots[g]
+    split(1)
+    split(2)
+    hops(2)
+    split(3)
+    tables(META["ar0"], META["ag0"], att_rows, att_gate)
+    hops(3)
+    split(4)
+    for c in sent:
+        c.wait_recv()
+    from_y(0, 0)
+    from_y(1, 0)
+    me = g.astype(F32)
+    for e in range(n):
+        m = meta_all[e]
+        in_gate[0, e] = slot_gates(m, META["ar0"], META["ag0"], me, slot_table(m, META["ar0"], me, CAP))
+        in_gate[1, e] = slot_gates(m, META["mr0"], META["mg0"], me, slot_table(m, META["mr0"], me, CAP))
+    from_y(2, 0)
+    from_y(3, 0)
+    split(5)
+
+    def whole(q, off):
+        return x_all.at[:, :, :, pl.ds(pl.multiple_of(q * width + off, half), half)]
+
+    cores = [ring.send(whole(t, half), whole(t, half), cs.at[0], cr.at[0], g, ring.tc)]
+    for c in (1, 2):
+        split(5 + c)
+        for zz in range(depth):
+            from_y(zz, c)
+        ref = whole(chunks[c][1], 0)
+        cores.append(ring.send(ref, ref, cs.at[c], cr.at[c], g, ring.tc))
+    for u in range(n):
+        ref = x_all.at[:, u, :, pl.ds(pl.multiple_of(ring.tx * width + half, half), half)]
+        rcopy(ref, ref, xs.at[u], xr.at[u], g, ring.tx).wait_recv()
+    cores.append(ring.send(whole(ring.tx, half), whole(ring.tx, half), cs.at[3], cr.at[3], g, ring.tc))
+    x_own[...] = x_all[g, :, :, mine].reshape(rows, width).astype(F32)
+    for c in cores + parts:
+        c.wait_recv()
+    for u in range(n):
+        ref = x_all.at[:, u, :, cols[0]]
+        rcopy(ref, ref, xs.at[u], xr.at[u], g, ring.tx).wait_send()
+    for c in count:
+        for zz in range(depth):
+            ref = unit(zz, y, c)
+            rcopy(ref, ref, ys.at[zz, c], yr.at[zz, c], pairs(z, 1 - y), t).wait_send()
+        for hop in range(depth - 1):
+            for up in (True, False):
+                zz = z - hop if up else z + hop
+                on = z + 1 if up else z - 1
+                ss, rs = (zs, zr) if up else (ws, wr)
+
+                @pl.when((zz >= 0) & (on < depth) if up else (zz < depth) & (on >= 0))
+                def _(zz=zz, on=on, ss=ss, rs=rs, hop=hop, c=c):
+                    ref = unit(zz, y, c)
+                    rcopy(ref, ref, ss.at[hop, c], rs.at[hop, c], pairs(on, y), t).wait_send()
+    ring.finish()
+
+
+def slot_gates(meta, first, gate, name, table):
+    per_token = (jnp.where(meta[first:first + 1] == name, meta[gate:gate + 1], 0.0)
+                 + jnp.where(meta[first + 1:first + 2] == name, meta[gate + 1:gate + 2], 0.0))
+    return jnp.sum(table.astype(F32) * per_token, axis=1, keepdims=True)
+
+
+def layer_start(tokens, out_grad, place_r, place_c, meta_w, w_kv, n, cid):
+    rows, features = tokens.shape
+    width, per, depth = features // 4, rows // n, n // 2
+    hw = w_kv.shape[2]
+    sds = jax.ShapeDtypeStruct
+    vm = pl.BlockSpec(memory_space=VM)
+    return pl.pallas_call(
+        functools.partial(start_body, n),
+        out_shape=(
+            sds((n, n, per, features), BF), sds((n, per, width), BF), sds((n, 16, rows), F32), sds((rows, rows), BF),
+            sds((n, CAP, rows), BF), sds((n, CAP, 1), F32), sds((n, CAP, rows), BF), sds((n, CAP, 1), F32),
+            sds((2, n, CAP, 1), F32), sds((features, hw), BF), sds((features, hw), BF), sds((rows, width), F32),
+            sds((n, CAP, width), BF)),
+        in_specs=[vm] * 6, out_specs=[vm] * 13,
+        scratch_shapes=[VM((n, per, width), BF), VM((n, CAP, width), BF)] + [DMA((n,))] * 6 + [DMA((depth, 3))] * 6 + [DMA((n,))] * 2 + [DMA((4,))] * 2,
+        name="layer_start", compiler_params=params(cid),
+    )(tokens, out_grad, place_r, place_c, meta_w, w_kv)
 
 
 def fast_local(
@@ -1119,20 +1501,6 @@
     part = lambda a: lax.dynamic_slice_in_dim(a, t * width, width, a.ndim - 1)
     counting = jnp.arange(rows, dtype=jnp.int32)
 
-    place = row_place.reshape(n, rows)
-    group = place // rows
-    earlier = (group[:, :, None] == group[:, None, :]) & (counting[None, :] < counting[:, None])
-    arrival = jnp.sum(earlier.astype(jnp.int32), axis=-1)
-    mine = lax.dynamic_index_in_dim(group * per + arrival, g, 0, keepdims=False)
-    sorter = (mine[None, :] == counting[:, None]).astype(BF)
-    x_sorted = mm(sorter, part(tokens)).astype(BF).reshape(n, per, width)
-    x_all = gather(x_sorted, n, deal=True, cid=1).reshape(n, rows, features)
-
-    here = (group == g) & True
-    spot = (jnp.arange(n, dtype=jnp.int32)[:, None] * per + arrival)
-    work_of = jnp.sum(
-        jnp.where(here[None] & (spot[None] == counting[:, None, None]), place[None] % rows, 0), axis=(1, 2)
-    )
     ends = jnp.cumsum(seq_lengths[0])
     segment = jnp.sum((counting[:, None] >= ends[None, :]).astype(jnp.int32), axis=1)
     begins = jnp.sum(
@@ -1143,79 +1511,39 @@
             att_routes[:, 0], att_routes[:, 1], att_gates[:, 0], att_gates[:, 1],
             mlp_routes[:, 0], mlp_routes[:, 1], mlp_gates[:, 0], mlp_gates[:, 1],
             counting - begins, segment, counting)] + [jnp.zeros((rows,), F32)] * 5)
-    moved = jnp.sum(
-        jnp.where(work_of[None, :, None] == counting[None, None, :], carried[:, None, :], 0.0), axis=2
-    )
-    meta_all = a2a_copy(moved, n, cid=8)
-    ar0, ar1, ag0, ag1, mr0, mr1, mg0, mg1, pos, seg, wpos = [meta_all[:, i] for i in range(11)]
-    me = g.astype(F32)
-    names = jnp.arange(n, dtype=F32)[:, None]
-    own = lambda a: lax.dynamic_index_in_dim(a, g, 0, keepdims=False)
-
-    att_in = slots_of(ar0, ar1, me, CAP)
-    att_in_gate = slot_gate(att_in, ar0, ar1, ag0, ag1, me)
-    mlp_in = slots_of(mr0, mr1, me, CAP)
-    mlp_in_gate = slot_gate(mlp_in, mr0, mr1, mg0, mg1, me)
-    o_ar0, o_ar1, o_ag0, o_ag1 = own(ar0)[None], own(ar1)[None], own(ag0)[None], own(ag1)[None]
-    o_mr0, o_mr1, o_mg0, o_mg1 = own(mr0)[None], own(mr1)[None], own(mg0)[None], own(mg1)[None]
-    att_out = slots_of(o_ar0, o_ar1, names, CAP)
-    att_out_gate = slot_gate(att_out, o_ar0, o_ar1, o_ag0, o_ag1, names)
-    mlp_out = slots_of(o_mr0, o_mr1, names, CAP)
-    mlp_out_gate = slot_gate(mlp_out, o_mr0, o_mr1, o_mg0, o_mg1, names)
-
-    meta_t = meta_all.transpose(0, 2, 1)
+    place = row_place.reshape(n, rows)
+    (x_all, dy_own, meta_all, sorter, att_out, att_gate, mlp_out, mlp_gate, in_gate, w_k, w_v, x_own,
+     dy_part) = layer_start(tokens, out_grad, place, place.T, carried, w_kv, n, cid=12)
+    x_all, dy_own = x_all.reshape(n, rows, features), dy_own.reshape(rows, width)
+    att_rows, mlp_rows = att_out.reshape(n * CAP, rows), mlp_out.reshape(n * CAP, rows)
+
     cos_t, sin_t = angle_tables(rows)
-    normed, picked, keys, values, query, attn, scale_attn, bias, turn_slots = attend(
-        x_all, gain_attn[None], w_kv[:, 0], w_kv[:, 1], w_query[0], meta_all, meta_t, cos_t, sin_t)
+    normed, picked, keys, values, query, attn, scale_attn, bias, turn_slots, d_mbr = attend(
+        x_all, gain_attn[None], w_k, w_v, w_query[0], meta_all, cos_t, sin_t, dy_part, in_gate[1], cid=13)
     normed_flat, picked = normed.reshape(n * rows, features), picked.reshape(n * CAP, features)
     attn = attn.reshape(n * CAP, hw)
     query_back = lax.all_to_all(query, "dp", split_axis=0, concat_axis=0, tiled=True)
-    x_own = part(own(x_all)).astype(F32)
-    att_rows = att_out.reshape(n * CAP, rows)
-    mlp_rows = mlp_out.reshape(n * CAP, rows)
     hidden, hid_rows, scale_mlp = hidden_rows(
-        attn, w_out[0], x_own, att_rows.T, att_out_gate.reshape(-1, 1), mlp_rows, n, cid=9)
-    dy_all = lax.all_gather(mm(sorter, out_grad).astype(BF), "dp", axis=0).reshape(n, n, per, features)
-    dy_all = dy_all.transpose(1, 0, 2, 3).reshape(n, rows, features)
-    d_mbr = jnp.einsum("gst,gtd->gsd", mlp_in, dy_all, preferred_element_type=F32) * mlp_in_gate[..., None]
-    d_mbr = d_mbr.astype(BF).reshape(n * CAP, features)
-    dy_own = part(own(dy_all)).astype(F32)
+        attn, w_out[0], x_own, att_rows.T, att_gate.reshape(-1, 1), mlp_rows, n, cid=9)
+
     gain_mlp_t, gain_attn_t = part(gain_mlp), part(gain_attn)
+    d_mbr = d_mbr.reshape(n * CAP, features)
     d_obr, d_hidden, mixed_rows, gain_mlp_part, normed2, inner, d_gate, d_up = expert_layer(
-        hid_rows, d_mbr, gain_mlp[None], w_gate[0], w_up[0], w_down[0], hidden, dy_own, gain_mlp_t[None], scale_mlp,
-        mlp_rows.T, mlp_out_gate.reshape(-1, 1), mlp_rows, att_rows, n, cid=10)
+        hid_rows, d_mbr, gain_mlp[None], w_gate[0], w_up[0], w_down[0], hidden, dy_own.astype(F32), gain_mlp_t[None],
+        scale_mlp, mlp_rows.T, mlp_gate.reshape(-1, 1), mlp_rows, att_rows, n, cid=10)
     w_gate_grad = mm_rows(normed2, d_gate)[None]
     w_up_grad = mm_rows(normed2, d_up)[None]
     w_down_grad = mm_rows(inner, d_mbr)[None]
 
     d_obr, d_attn, dq_pre = attend_back(
-        d_obr, att_in_gate[..., None], w_out[0], query, keys, values, bias, turn_slots)
-    d_attn_back = a2a(d_attn, n, cid=4)
-    d_obr, dq_pre = d_obr.reshape(n * CAP, features), dq_pre.reshape(n * CAP, hw)
+        d_obr, in_gate[0], w_out[0], query, keys, values, bias, turn_slots)
+    d_obr, dq_flat = d_obr.reshape(n * CAP, features), dq_pre.reshape(n * CAP, hw)
+    d_kv_all, back, gains = layer_tail(
+        (dq_flat, w_query[0], d_attn, query_back, keys, values, meta_all, cos_t, sin_t,
+         w_k, w_v, x_own, scale_attn, gain_attn_t[None], d_hidden, mixed_rows, gain_mlp_part, att_rows.T), n, cid=11)
     w_out_grad = mm_rows(attn, d_obr)[None]
-    w_query_grad = mm_rows(picked, dq_pre)[None]
-    d_norm_q = mm_t(dq_pre, w_query[0]).reshape(n, CAP, features)
-    d_kv = keys_back(query_back, d_attn_back, own(keys), own(values), own(meta_all), own(meta_t), cos_t, sin_t)
-    d_kv_all = a2a_copy(d_kv, n, cid=5)
-    w_kv_grad = jnp.einsum(
-        "ld,lck->dck", normed_flat, d_kv_all.reshape(n * rows, 2, hw), preferred_element_type=F32)
-    d_norm_kv = mm_t(d_kv, w_kv.reshape(features, 2 * hw)).reshape(rows // CAP, CAP, features)
-
-    d_norm = reduce(jnp.concatenate([d_norm_q, d_norm_kv], axis=0), n, cid=3)
-    d_normed = mm_rows(att_rows, d_norm[:n].reshape(n * CAP, width))
-    d_normed = d_normed + d_norm[n:].reshape(rows, width).astype(F32)
-    scale_own = own(scale_attn)
-    e1 = gain_attn_t * d_normed
-    sum_1 = lax.psum(jnp.sum(x_own * e1, axis=1, keepdims=True), "tensor")
-    in_grad = d_hidden + scale_own * e1 - x_own * (scale_own * scale_own * scale_own) * (sum_1 / features)
-    gain_attn_part = jnp.sum(d_normed * x_own * scale_own, axis=0)
-
-    gains = jnp.concatenate([gain_mlp_part[:1], gain_attn_part[None], jnp.zeros((6, width), F32)], axis=0)
-    gains = jnp.sum(gather(gains, n, bcast=True, cid=7), axis=0)
-    back = jnp.concatenate(
-        [mixed_rows.reshape(n, per, width), in_grad.astype(BF).reshape(n, per, width)], axis=1
-    )
-    back = gather(back, n, cid=6)
+    w_query_grad = mm_rows(picked, dq_flat)[None]
+    w_kv_grad = map_grad(normed_flat, d_kv_all.reshape(n * rows, 2 * hw))
     mixed = mm_rows(sorter, back[:, :per].reshape(rows, features)).astype(BF)
     tokens_grad = mm_rows(sorter, back[:, per:].reshape(rows, features)).astype(BF)
     return (

time: 528 us -> 365 us (0.69)
  Pallas kernels: 361 us -> 308 us
  local copies, waits for them, and re-layouts: 60.4 us -> 13.1 us
  other arithmetic: 18.4 us -> 3.17 us
  matrix products: 43.9 us -> 29.3 us
  between operations: 15 us -> 1 us
  starting transfers between devices: 15.2 us -> 3.76 us
  blocking collectives: 6.97 us -> 0 us
    pallas_call x9 -> x4, Pallas kernels: 206 us -> 153 us  [the longest x1 61.9 us: layer_tail(): pl.pallas_call(functools.partial(tail_body, n), out_shape=(sds((n, rows,...]
    unnamed x45 -> x26, local copies, waits for them, and re-layouts: 17.9 us -> 0.84 us
    reshape x5 -> x2, local copies, waits for them, and re-layouts: 15.3 us -> 2.19 us  [the longest x1 1.41 us: fast_local(): place = row_place.reshape(n, rows)]
    all_to_all x1, starting transfers between devices: 15.1 us -> 3.76 us  [fast_local(): lax.all_to_all(query, 'dp', split_axis=0, concat_axis=0, tiled=True)]
    dot_general x2 -> x0, matrix products: 8.44 us -> none  [the longest x1 6.4 us: fast_local(): jnp.einsum('ld,lck->dck', normed_flat, d_kv_all.reshape(n * rows, 2, hw),...]
    slice x3 -> x0, local copies, waits for them, and re-layouts: 7.59 us -> none  [the longest x1 5.95 us: fast_local(): w_kv[:, 1]]
    psum x1 -> x0, blocking collectives: 6.97 us -> none  [fast_local(): sum_1 = lax.psum(jnp.sum(x_own * e1, axis=1, keepdims=True), 'tensor')]
    dot_general x16 -> x7, matrix products: 35.5 us -> 29.3 us  [dot(): return lax.dot_general(a, b, dims, preferred_element_type=F32)]
  transfers between devices with their start and end apart: 2 -> 1, of which waited for: 0 -> 0; matrix products, arithmetic and copies ran while one was open for 10% -> 9% of each run, Pallas kernels for 48% -> 43%
where the time goes in v3:
time: 365 us; the launch traced here: 359 us
  Pallas kernels  308 us (84%)
  matrix products  29.3 us (8%)
  local copies, waits for them, and re-layouts  13.1 us (4%)
  starting transfers between devices  3.76 us (1%)
    pallas_call x1, Pallas kernels, expert_layer(): pl.pallas_call(functools.partial(expert_body, n), out_shape=(sds((n, r, f...  92.7 us
    pallas_call x1, Pallas kernels, layer_tail(): pl.pallas_call(functools.partial(tail_body, n), out_shape=(sds((n, rows,...  61.9 us
    pallas_call x1, Pallas kernels, layer_start(): pl.pallas_call(functools.partial(start_body, n), out_shape=(sds((n, n, pe...  49.2 us
    pallas_call x1, Pallas kernels, hidden_rows(): pl.pallas_call(functools.partial(hidden_body, n), out_shape=(jax.ShapeDty...  47.4 us
    pallas_call x1, Pallas kernels, attend(): pl.pallas_call(functools.partial(attend_body, n), grid=(n // pair,), out_...  30.8 us
    dot_general x7, matrix products, dot(): return lax.dot_general(a, b, dims, preferred_element_type=F32)  29.3 us
    pallas_call x1, Pallas kernels, attend_back(): pl.pallas_call(attend_back_body, grid=(n // pair,), out_shape=(sds((n, ca...  14.9 us
    pallas_call x1, Pallas kernels, map_grad(): pl.pallas_call(map_grad_body, grid=(features // size,), out_shape=jax.Sha...  11.5 us
  transfers between devices with their start and end apart: 1, of which 0 were waited for; matrix products, arithmetic and copies ran while one was open for 9% of the time, Pallas kernels for 43%

profile of v3, /device:TPU:0, one launch (start us, length us, event | category | flops | bytes accessed | tf_op | source)
XLA Modules:
  0.0 358.6 jit_solution(13402600341819262413)
XLA Ops:
  0.6 0.8 reduce-window.4
  1.5 0.7 fusion.1
  2.1 0.1 convert_reduce_fusion
  2.2 0.1 select_reduce_fusion
  2.3 1.4 copy.41
  3.7 0.8 convert_bitcast_fusion.1
  4.5 0.8 slice_bitcast_fusion.2
  5.3 1.2 stack.5.meta_w
  6.5 49.2 %layer_start.1 = (bf16[8,8,16,2048]{3,2,1,0:T(8,128)(2,1)}, bf16[8,16,512]{2,1,0:T(8,128)(2,1)}, f32[8,16,128]{2,1,0:T(8,128)}, bf16[128,128]{1,0:T(8,128)(2,1)}...) custom-call(bf16[128,2048]{1,0:T(8,128)(2,1)} %tokens.1, ...), custom_call_target="tpu_custom_call" | custom-call | tf_op jit(solution)/shard_map/layer_start/pallas_call | solution.py:1478
  55.7 1.9 slice_bitcast_fusion
  57.6 30.8 %attend.1 = (bf16[8,128,2048]{2,1,0:T(8,128)(2,1)}, bf16[8,64,2048]{2,1,0:T(8,128)(2,1)}, bf16[8,128,512]{2,1,0:T(8,128)(2,1)}, bf16[8,128,512]{2,1,0:T(8,128)(2...) custom-call(bf16[8,128,2048]{2,1,0:T(8,128)(2,1)} %bitcast.105, ...), custom_call_target="tpu_custom_call" | custom-call | tf_op jit(solution)/shard_map/attend/pallas_call | solution.py:1021
  88.3 3.8 %all-to-all-start = ((bf16[8,64,512]{2,1,0:T(8,128)(2,1)}), bf16[8,64,512]{2,1,0:T(8,128)(2,1)S(1)}, u32[]{:S(2)}, u32[]{:S(2)}) async-start(bf16[8,64,512]{2,1,0:T(8,128)(2,1)} %get-tuple-element.69.query), calls=%async_computation | async-start | bytes 1048576 | tf_op jit(solution)/shard_map/all_to_all | solution.py:1525
  92.1 1.3 dynamic_slice.7
  93.4 1.3 dynamic_slice.6
  94.8 0.8 copy.43
  95.6 0.8 copy.44.mlp_t
  96.3 0.7 bitcast_convert_fusion.dy_own
  97.1 47.4 %hidden_rows.1 = (f32[128,512]{1,0:T(8,128)}, bf16[8,64,2048]{2,1,0:T(8,128)(2,1)}, f32[128,1]{1,0:T(8,128)}) custom-call(bf16[512,512]{1,0:T(8,128)(2,1)} %bitcast.109, bf16[512,2048]{1,0:T(8,128)(2,1)} %bitcast.99, f32[128,512]{1,0:T(8,128)} %get-tuple-element.58.x_own, bf16[128,512]{1,0:T(8,128)(2,1)} %bitcast.115, f32[512,1]{1,0:T(8,128)} %bitcast.122, ...), custom_call_target="tpu_custom_call" | custom-call | tf_op jit(solution)/shard_map/hidden_rows/pallas_call | solution.py:709
  144.5 92.7 %expert_layer.1 = (bf16[8,64,2048]{2,1,0:T(8,128)(2,1)}, f32[128,512]{1,0:T(8,128)}, bf16[128,512]{1,0:T(8,128)(2,1)}, f32[8,512]{1,0:T(8,128)}, bf16[512,2048]{...) custom-call(bf16[8,64,2048]{2,1,0:T(8,128)(2,1)} %get-tuple-element.62.hid_rows, ...), custom_call_target="tpu_custom_call" | custom-call | tf_op jit(solution)/shard_map/expert_layer/pallas_call | solution.py:858
  237.2 14.9 %attend_back.1 = (bf16[8,64,2048]{2,1,0:T(8,128)(2,1)}, bf16[8,64,512]{2,1,0:T(8,128)(2,1)}, bf16[8,64,512]{2,1,0:T(8,128)(2,1)}) custom-call(bf16[8,64,2048]{2,1,0:T(8,128)(2,1)} %get-tuple-element.68.rows_in, f32[8,64,1]{2,1,0:T(8,128)} %get-tuple-element.92.gates, bf16[512,2048]{1,0:T(8,128)(2,1)} %bitcast.100, ...), custom_call_target="tpu_custom_call" | custom-call | tf_op jit(solution)/shard_map/attend_back/pallas_call | solution.py:1066
  252.1 5.0 %convolution_bitcast_fusion.3 = f32[1,512,2048]{2,1,0:T(8,128)} fusion(bf16[8,64,512]{2,1,0:T(8,128)(2,1)S(1)} %copy-done.1, bf16[8,64,2048]{2,1,0:T(8,128)(2,1)} %get-tuple-element.85), kind=kOutput, calls=%fused_computation.3 | convolution fusion | flops 1073741824 | bytes 6815744 | tf_op jit(solution)/shard_map/dot_general | solution.py:510
  257.2 6.1 %convolution_bitcast_fusion = f32[1,1408,2048]{2,1,0:T(8,128)} fusion(bf16[512,1408]{1,0:T(8,128)(2,1)S(1)} %copy-done.12, bf16[512,2048]{1,0:T(8,128)(2,1)S(1)} %bitcast.111), kind=kOutput, calls=%fused_computation | convolution fusion | flops 2952790016 | bytes 15073280 | tf_op jit(solution)/shard_map/dot_general | solution.py:510
  263.3 6.3 %convolution_bitcast_fusion.2 = f32[1,2048,1408]{2,1,0:T(8,128)} fusion(bf16[512,2048]{1,0:T(8,128)(2,1)S(1)} %copy-done.9, bf16[512,1408]{1,0:T(8,128)(2,1)S(1)} %copy-done.11), kind=kOutput, calls=%fused_computation.2 | convolution fusion | flops 2952790016 | bytes 15073280 | tf_op jit(solution)/shard_map/dot_general | solution.py:510
  269.6 3.3 convolution_bitcast_fusion.4
  272.9 6.3 %convolution_bitcast_fusion.1 = f32[1,2048,1408]{2,1,0:T(8,128)} fusion(bf16[512,2048]{1,0:T(8,128)(2,1)S(1)} %copy-done.9, bf16[512,1408]{1,0:T(8,128)(2,1)S(1)} %copy-done.10), kind=kOutput, calls=%fused_computation.1 | convolution fusion | flops 2952790016 | bytes 15073280 | tf_op jit(solution)/shard_map/dot_general | solution.py:510
  279.2 0.8 copy-done
  280.0 61.9 %layer_tail.1 = (bf16[8,128,1024]{2,1,0:T(8,128)(2,1)}, bf16[8,32,2048]{2,1,0:T(8,128)(2,1)}, f32[8,2048]{1,0:T(8,128)}) custom-call(bf16[512,512]{1,0:T(8,128)(2,1)} %bitcast.119, bf16[2048,512]{1,0:T(8,128)(2,1)} %bitcast.97, bf16[8,64,512]{2,1,0:T(8,128)(2,1)} %get-tuple-element.75.d_attn, bf16[8,64,512]{2,1,0:T(8,128)(2,1)} %copy-done, ...), custom_call_target="tpu_custom_call" | custom-call | tf_op jit(solution)/shard_map/layer_tail/pallas_call | solution.py:1280
  341.9 1.3 fusion.2
  343.1 1.1 convolution_convert_fusion
  344.3 1.1 convolution_convert_fusion.1
  345.4 1.5 fusion.3
  346.9 11.5 %map_grad.1 = f32[2048,8,128]{2,1,0:T(8,128)} custom-call(bf16[1024,2048]{1,0:T(8,128)(2,1)} %bitcast.104, bf16[1024,1024]{1,0:T(8,128)(2,1)} %bitcast.106), custom_call_target="tpu_custom_call" | custom-call | tf_op jit(solution)/shard_map/map_grad/pallas_call | solution.py:1117
  (30 shorter events, 0.1 us)
Async XLA Ops:
  57.6 37.2 %copy-start.4 = (bf16[8,64,128]{2,1,0:T(8,128)(2,1)S(1)}, bf16[8,64,128]{2,1,0:T(8,128)(2,1)}, u32[]{:S(2)}) copy-start(bf16[8,64,128]{2,1,0:T(8,128)(2,1)} %get-tuple-element.59) | copy-start | bytes 393220
  57.6 38.0 %copy-start.3 = (bf16[8,64,128]{2,1,0:T(8,128)(2,1)S(1)}, bf16[8,64,128]{2,1,0:T(8,128)(2,1)}, u32[]{:S(2)}) copy-start(bf16[8,64,128]{2,1,0:T(8,128)(2,1)} %get-tuple-element.61) | copy-start | bytes 393220
  57.6 38.8 %copy-start.6 = (bf16[8,16,512]{2,1,0:T(8,128)(2,1)S(1)}, bf16[8,16,512]{2,1,0:T(8,128)(2,1)}, u32[]{:S(2)}) copy-start(bf16[8,16,512]{2,1,0:T(8,128)(2,1)} %get-tuple-element.65) | copy-start | bytes 393220
  88.3 190.9 %all-to-all-start = ((bf16[8,64,512]{2,1,0:T(8,128)(2,1)}), bf16[8,64,512]{2,1,0:T(8,128)(2,1)S(1)}, u32[]{:S(2)}, u32[]{:S(2)}) async-start(bf16[8,64,512]{2,1,0:T(8,128)(2,1)} %get-tuple-element.69.query), calls=%async_computation | async-start | bytes 1048576 | tf_op jit(solution)/shard_map/all_to_all | solution.py:1525
  237.2 14.9 %copy-start.1 = (bf16[8,64,512]{2,1,0:T(8,128)(2,1)S(1)}, bf16[8,64,512]{2,1,0:T(8,128)(2,1)}, u32[]{:S(2)}) copy-start(bf16[8,64,512]{2,1,0:T(8,128)(2,1)} %get-tuple-element.57) | copy-start | bytes 1572868
  252.1 5.1 %copy-start.2 = (bf16[8,64,2048]{2,1,0:T(8,128)(2,1)S(1)}, bf16[8,64,2048]{2,1,0:T(8,128)(2,1)}, u32[]{:S(2)}) copy-start(bf16[8,64,2048]{2,1,0:T(8,128)(2,1)} %get-tuple-element.63) | copy-start | bytes 6291460
  252.1 5.0 %copy-start.12 = (bf16[512,1408]{1,0:T(8,128)(2,1)S(1)}, bf16[512,1408]{1,0:T(8,128)(2,1)}, u32[]{:S(2)}) copy-start(bf16[512,1408]{1,0:T(8,128)(2,1)} %get-tuple-element.89) | copy-start | bytes 4325380
  257.2 6.1 %copy-start.9 = (bf16[512,2048]{1,0:T(8,128)(2,1)S(1)}, bf16[512,2048]{1,0:T(8,128)(2,1)}, u32[]{:S(2)}) copy-start(bf16[512,2048]{1,0:T(8,128)(2,1)} %get-tuple-element.86) | copy-start | bytes 6291460
  257.2 6.1 %copy-start.11 = (bf16[512,1408]{1,0:T(8,128)(2,1)S(1)}, bf16[512,1408]{1,0:T(8,128)(2,1)}, u32[]{:S(2)}) copy-start(bf16[512,1408]{1,0:T(8,128)(2,1)} %get-tuple-element.87) | copy-start | bytes 4325380
  263.3 6.3 %copy-start.5 = (bf16[8,64,512]{2,1,0:T(8,128)(2,1)S(1)}, bf16[8,64,512]{2,1,0:T(8,128)(2,1)}, u32[]{:S(2)}) copy-start(bf16[8,64,512]{2,1,0:T(8,128)(2,1)} %get-tuple-element.74) | copy-start | bytes 1572868
  263.3 6.3 %copy-start.8 = (bf16[8,64,2048]{2,1,0:T(8,128)(2,1)S(1)}, bf16[8,64,2048]{2,1,0:T(8,128)(2,1)}, u32[]{:S(2)}) copy-start(bf16[8,64,2048]{2,1,0:T(8,128)(2,1)} %get-tuple-element.84) | copy-start | bytes 6291460
  269.6 3.3 copy-start.10
  279.2 0.8 copy-start
  341.8 1.3 copy-start.7

commit v4 on v3

--- a/solution.py
+++ b/solution.py
@@ -1035,45 +1035,6 @@
     )(x_all, gain, w_k, w_v, w_q, meta, cos_t, sin_t, dy_part, dy_gate)
 
 
-def attend_back_body(rows_in, gates, w_o, query, keys, values, bias, turn_slots, d_obr, d_attn, dq_pre, o_scr):
-    pair, cap, features = rows_in.shape
-    heads = w_o.shape[0] // HD
-    for p in range(pair):
-        o_scr[p * cap:(p + 1) * cap] = (rows_in[p].astype(F32) * gates[p]).astype(BF)
-    d_obr[...] = o_scr[...].reshape(pair, cap, features)
-    back = mm_t(o_scr[...], w_o[...]).astype(BF)
-    root = math.sqrt(HD)
-    for p in range(pair):
-        d_o = back[p * cap:(p + 1) * cap]
-        d_attn[p] = d_o
-        dq = []
-        for h in range(heads):
-            hh = slice(h * HD, (h + 1) * HD)
-            probs = softmax_rows(mm_t(query[p, :, hh], keys[p, :, hh]) / root + bias[p])
-            d_probs = mm_t(d_o[:, hh], values[p, :, hh])
-            delta = jnp.sum(d_probs * probs, axis=-1, keepdims=True)
-            d_scores = (probs * (d_probs - delta)).astype(BF)
-            dq.append(mm(d_scores, keys[p, :, hh]) / root)
-        dq = jnp.concatenate(dq, axis=1)
-        dq_pre[p] = turned(dq, turn_slots[p, :, :HD], -turn_slots[p, :, HD:]).astype(BF)
-
-
-def attend_back(rows_in, gates, w_o, query, keys, values, bias, turn_slots):
-    n, cap, features = rows_in.shape
-    hw, rows, pair = w_o.shape[0], keys.shape[1], 2
-    sds = jax.ShapeDtypeStruct
-    block = lambda *s: pl.BlockSpec((pair,) + s, lambda i: (i,) + (0,) * len(s))
-    return pl.pallas_call(
-        attend_back_body, grid=(n // pair,),
-        out_shape=(sds((n, cap, features), BF), sds((n, cap, hw), BF), sds((n, cap, hw), BF)),
-        in_specs=[block(cap, features), block(cap, 1), pl.BlockSpec(w_o.shape, lambda i: (0, 0)), block(cap, hw), block(rows, hw),
-                  block(rows, hw), block(cap, rows), block(cap, 2 * HD)],
-        out_specs=(block(cap, features), block(cap, hw), block(cap, hw)),
-        scratch_shapes=[VM((pair * cap, features), BF)],
-        name="attend_back", compiler_params=pltpu.CompilerParams(vmem_limit_bytes=56 * 2**20),
-    )(rows_in, gates, w_o, query, keys, values, bias, turn_slots)
-
-
 def keys_back_body(query, d_attn, keys, values, meta, cos_t, sin_t, d_kv, *, cap):
     n = query.shape[0]
     hw = keys.shape[1]
@@ -1124,16 +1085,38 @@
     return out.reshape(features, tiles // 2, 2, 128).transpose(0, 2, 1, 3).reshape(features, 2, both // 2)
 
 
+def attention_back(i, d_attn, query, keys, values, bias, turn_slots, dq_pre):
+    root = math.sqrt(HD)
+    dq = []
+    for h in range(query.shape[2] // HD):
+        hh = slice(h * HD, (h + 1) * HD)
+        k = keys[i, :, hh]
+        probs = softmax_rows(mm_t(query[i, :, hh], k) / root + bias[i])
+        d_probs = mm_t(d_attn[i, :, hh], values[i, :, hh])
+        delta = jnp.sum(d_probs * probs, axis=-1, keepdims=True)
+        dq.append(mm((probs * (d_probs - delta)).astype(BF), k) / root)
+    dq_pre[i] = turned(jnp.concatenate(dq, axis=1), turn_slots[i, :, :HD], -turn_slots[i, :, HD:]).astype(BF)
+
+
 def tail_body(
-    n, dq_pre, w_q, d_attn, q_back, keys, values, meta, cos_t, sin_t, w_k, w_v,
-    x_own, scale, gain_t, d_hidden, mixed, gain_mlp_part, comb, d_kv_all, back, gains, *scratch,
+    n, d_rows, in_gate, query, bias, turn_slots, q_back, keys, values, meta, cos_t, sin_t,
+    x_own, scale, gain_t, d_hidden, hidden, mbr, mlp_gate, mlp_rows, att_rows, gain_mlp_part, wo_hbm, wq_hbm, wk_hbm, wv_hbm,
+    d_kv_all, back, gains, d_obr, dq_pre, *scratch,
 ):
     ring = Ring(n)
-    bufs = scratch[:7]
-    at_in, d_kv, kc_out, kc_in, kv_keep, kx_out, kx_in, sbuf, sq, sq_in, g_out, g_in, g_sum, d_norm = scratch[7:21]
-    (as_, ar, zs, zr, ws, wr, ys, yr, ks, kr, lxs, lxr, qs, qr, gs, gr, ts, tr) = scratch[21:39]
-    sems, fsems = scratch[39:45], scratch[45:]
+    (at_in, d_kv, kc_out, kc_in, kv_keep, kx_out, kx_in, sbuf, sq, sq_in, g_out, g_in, g_sum, d_norm, d_attn, mixed, comb, mlp_t,
+     wo, w_q, w_k, w_v, whole, pbuf, pbuf3, cbuf, cbuf3, cin, cin3) = scratch[:29]
+    xbuf, xin, dbuf, rbuf, xbuf3, xin3, dbuf3, rbuf3 = scratch[29:37]
+    (as_, ar, zs, zr, ws, wr, ys, yr, ks, kr, lxs, lxr, qs, qr, gs, gr, ts, tr, wsem) = scratch[37:56]
+    sems, sems3, fsems = scratch[56:62], scratch[62:68], scratch[68:]
+    loads = [pltpu.make_async_copy(a, b, wsem.at[i]) for i, (a, b) in enumerate(
+        [(wo_hbm, wo), (wq_hbm, w_q), (wk_hbm, w_k), (wv_hbm, w_v)])]
+    for c in loads:
+        c.start()
     rows, width = x_own.shape
+    cw = width // NC
+    slots, cap = query.shape[0] * query.shape[1], query.shape[1]
+    all_keys, all_values = keys, values
     hw = keys.shape[2]
     features = 4 * width
     keys, values, meta, scale = keys.at[ring.g], values.at[ring.g], meta.at[ring.g], scale.at[ring.g]
@@ -1141,19 +1124,43 @@
     depth = n // 2
     ring.greet_everyone()
 
+    red3 = ChunkReduce(ring, lambda j: mbr[j].astype(F32), whole, pbuf3, (cbuf3, xbuf3, dbuf3), (cin3, xin3, rbuf3), sems3)
+    for j in range(NC):
+        red3.core(j)
+    for e in range(n):
+        d_obr[e] = (d_rows[e].astype(F32) * in_gate[e]).astype(BF)
+    loads[0].wait()
+    d_attn[...] = mm_t(d_obr[...].reshape(slots, features), wo[...]).astype(BF).reshape(d_attn.shape)
     arrive = []
     for o in range(1, n):
         d = ring.to(o)
         arrive.append(ring.send(d_attn.at[d], at_in.at[ring.g], as_.at[o], ar.at[o], d, ring.t))
     at_in[ring.g] = d_attn[ring.g]
-    red = Reduce(
-        ring, lambda q: mm_t(dq_pre[...], w_q[cols_of(q, 0, width, width), :]), bufs, sems)
-    red.core()
+
+    def group_back(i, _):
+        attention_back(i, d_attn, query, all_keys, all_values, bias, turn_slots, dq_pre)
+        return _
+
+    red3.cross(0)
+    lax.fori_loop(0, n // 2, group_back, 0)
+    for j in range(1, NC):
+        red3.cross(j)
+    lax.fori_loop(n // 2, n, group_back, 0)
+    loads[1].wait()
+
+    def back_cols(j):
+        dq = dq_pre[...].reshape(slots, hw)
+        return jnp.concatenate([mm_t(dq, w_q[q * width + j * cw:q * width + (j + 1) * cw, :]) for q in range(4)], axis=1)
+
+    red = ChunkReduce(ring, back_cols, whole, pbuf, (cbuf, xbuf, dbuf), (cin, xin, rbuf), sems)
+    for j in range(NC):
+        red.core(j)
+        if j:
+            red.cross(j - 1)
+    red.cross(NC - 1)
     for c in arrive:
         c.wait_recv()
-    red.home(0)
-    keys_back_body(q_back, at_in, keys, values, meta, cos_t, sin_t, d_kv, cap=q_back.shape[1])
-    red.home(1)
+    keys_back_body(q_back, at_in, keys, values, meta, cos_t, sin_t, d_kv, cap=cap)
 
     halves = [(c, slice(c * hw, (c + 1) * hw)) for c in range(2)]
     mine = d_kv_all.at[ring.g]
@@ -1200,6 +1207,12 @@
             step(False, hop, c, hop == 0)
 
     spread(0)
+    red.home(0)
+    red.home(1)
+    comb[...] = att_rows[...].T
+    mlp_t[...] = mlp_rows[...].T
+    loads[2].wait()
+    loads[3].wait()
 
     def kv_part(q):
         at = cols_of(q, 0, width, width)
@@ -1216,9 +1229,10 @@
     kv_keep[0] = kv_part(ring.t)
     red.home(3)
     spread(1)
+    for j in range(NC):
+        red3.home(j)
     kx.wait_recv()
     local = kv_keep[0] + kc_in[0].astype(F32) + kx_in[...].astype(F32)
-    cw = width // NC
     squares = jnp.zeros((8, rows), F32)
     for j in range(NC):
         cc = slice(j * cw, (j + 1) * cw)
@@ -1230,11 +1244,16 @@
         g_out[:, cc] = jnp.concatenate([
             gain_mlp_part[:1, cc], jnp.sum(got * x_own[:, cc] * scale[...], axis=0, keepdims=True), jnp.zeros((6, cw), F32)], axis=0)
     sq[...] = squares
+    spread(2)
     shared = [ring.send(sq, sq_in.at[i], qs.at[i], qr.at[i], ring.g, q) for i, q in enumerate([ring.tc, ring.tx, ring.tcx])]
     sums = []
     for o in range(1, n):
         sums.append(ring.send(g_out, g_in.at[ring.g], gs.at[o], gr.at[o], ring.to(o), ring.t))
     g_in[ring.g] = g_out[...]
+    for j in range(NC):
+        cc = slice(j * cw, (j + 1) * cw)
+        high, low = split_bf(red3.rows(j).astype(F32) * mlp_gate[...])
+        mixed[:, cc] = (hidden[:, cc] + mm(mlp_t[...], high) + mm(mlp_t[...], low)).astype(BF)
     for c in shared:
         c.wait_recv()
     total = (sq[...] + sq_in[0] + sq_in[1] + sq_in[2])[:1]
@@ -1243,7 +1262,8 @@
     s = scale[...]
     in_grad = d_hidden[...] + s * (gain_t[...] * d_norm[...]) - x_own[...] * (s * s * s * mean)
     per = rows // n
-    fin = Gather(ring, width, back, sbuf, fsems)
+    fin = ChunkGather(
+        ring, lambda j, q, e: back.at[slice(None) if e is None else e, :, cols_of(q, 0, width, width)], sbuf, fsems)
     fin.out(0, jnp.concatenate(
         [mixed[...].reshape(n, per, width), in_grad.astype(BF).reshape(n, per, width)], axis=1))
     for c in sums:
@@ -1252,11 +1272,10 @@
     at_t = cols_of(ring.t, 0, width, width)
     gains[:, at_t] = g_sum[...]
     told = [ring.send(g_sum, gains.at[:, at_t], ts.at[i], tr.at[i], ring.g, q) for i, q in enumerate([ring.tc, ring.tx, ring.tcx])]
-    spread(2)
     fin.cross(0)
     spread(3)
     fin.core(0)
-    fin.finish()
+    fin.here(0)
     for c in told:
         c.wait_recv()
     for c, _ in halves:
@@ -1267,30 +1286,42 @@
             drain(True, hop, c)
             drain(False, hop, c)
     ring.finish()
-
-
-def layer_tail(args, n, cid):
-    dq_pre, w_q, d_attn, q_back, keys = args[:5]
-    x_own = args[11]
+    fin.sent()
+    for r in (red, red3):
+        r.sent_core()
+        r.sent_rest()
+
+
+def layer_tail(args, weights, n, cid):
+    d_rows, query, keys, x_own = args[0], args[2], args[6], args[11]
     rows, width = x_own.shape
-    cap, hw = d_attn.shape[1:]
+    cap, hw = query.shape[1:]
     cw, features, depth = width // NC, 4 * width, n // 2
+    slots = n * cap
     sds = jax.ShapeDtypeStruct
     per = 2 * rows // n
+    one, two = VM((NC, n, cap, cw), BF), VM((NC, 2, n, cap, cw), BF)
+    part = VM((NC, 2, n, cap, cw), F32)
+    any_, vm = pl.BlockSpec(memory_space=pl.ANY), pl.BlockSpec(memory_space=VM)
     return pl.pallas_call(
         functools.partial(tail_body, n),
-        out_shape=(sds((n, rows, 2 * hw), BF), sds((n, per, features), BF), sds((8, features), F32)),
-        in_specs=[pl.BlockSpec(memory_space=VM)] * len(args), out_specs=[pl.BlockSpec(memory_space=VM)] * 3,
-        scratch_shapes=REDUCE_BUFS(NC, n, cap, cw) + [
+        out_shape=(
+            sds((n, rows, 2 * hw), BF), sds((n, per, features), BF), sds((8, features), F32),
+            sds((n, cap, features), BF), sds((n, cap, hw), BF)),
+        in_specs=[vm] * len(args) + [any_] * 4, out_specs=[vm] * 5,
+        scratch_shapes=[
             VM((n, cap, hw), BF), VM((rows, 2 * hw), BF), VM((2, rows, width), BF), VM((2, rows, width), BF),
             VM((2, rows, width), F32), VM((rows, width), BF), VM((rows, width), BF), VM((1, n, per, width), BF),
             VM((8, rows), F32), VM((3, 8, rows), F32), VM((8, width), F32), VM((n, 8, width), F32), VM((8, width), F32),
-            VM((rows, width), F32),
+            VM((rows, width), F32), VM((n, cap, hw), BF), VM((rows, width), BF), VM((rows, slots), BF), VM((rows, slots), BF),
+            VM((hw, features), BF), VM((features, hw), BF), VM((features, hw), BF), VM((features, hw), BF),
+            VM((slots, 4 * cw), F32), part, part, two, two, two, two] + [one] * 8 + [
             DMA((n,)), DMA((n,)), DMA((depth, 2)), DMA((depth, 2)), DMA((depth, 2)), DMA((depth, 2)), DMA((depth, 2)), DMA((depth, 2)),
-            DMA, DMA, DMA, DMA, DMA((3,)), DMA((3,)), DMA((n,)), DMA((n,)), DMA((3,)), DMA((3,))]
-        + REDUCE_SEMS(NC, n) + GATHER_SEMS(1, n),
-        name="layer_tail", compiler_params=params(cid),
-    )(*args)
+            DMA, DMA, DMA, DMA, DMA((3,)), DMA((3,)), DMA((n,)), DMA((n,)), DMA((3,)), DMA((3,)), DMA((4,))]
+        + REDUCE_SEMS(NC, n) * 2 + GATHER_SEMS(1, n),
+        name="layer_tail", compiler_params=pltpu.CompilerParams(
+            collective_id=cid, has_side_effects=True, vmem_limit_bytes=62 * 2**20),
+    )(*args, *weights)
 
 
 def start_body(
@@ -1488,6 +1519,329 @@
     )(tokens, out_grad, place_r, place_c, meta_w, w_kv)
 
 
+def tile_list(size, step):
+    return [(a, min(step, size - a)) for a in range(0, size, step)]
+
+
+class ChunkReduce:
+    def __init__(self, ring, partial, whole, pbuf, sent, got, sems):
+        self.ring, self.partial, self.whole, self.pbuf = ring, partial, whole, pbuf
+        self.cbuf, self.xbuf, self.dbuf = sent
+        self.cin, self.xin, self.rbuf = got
+        cs, cr, xs, xr, ds, dr = sems
+        k, (nc, n, _, _) = ring, self.xbuf.shape
+        self.c = [rcopy(self.cbuf.at[j], self.cin.at[j], cs.at[j], cr.at[j], k.g, k.tc) for j in range(nc)]
+        self.x = [rcopy(self.xbuf.at[j], self.xin.at[j], xs.at[j], xr.at[j], k.g, k.tx) for j in range(nc)]
+        self.d = [
+            [rcopy(self.dbuf.at[j, k.to(o)], self.rbuf.at[j, k.g], ds.at[j, o], dr.at[j, o], k.to(o), k.t) for o in range(1, n)]
+            for j in range(nc)]
+
+    def core(self, j):
+        k = self.ring
+        n, r, cw = self.xbuf.shape[1:]
+        self.whole[...] = self.partial(j)
+        take = lambda q: self.whole[:, pl.ds(pl.multiple_of(q * cw, cw), cw)].reshape(n, r, cw)
+        self.cbuf[j, 0] = take(k.tc).astype(BF)
+        self.cbuf[j, 1] = take(k.tcx).astype(BF)
+        self.c[j].start()
+        self.pbuf[j, 0] = take(k.t)
+        self.pbuf[j, 1] = take(k.tx)
+
+    def cross(self, j):
+        self.c[j].wait_recv()
+        self.xbuf[j] = (self.pbuf[j, 1] + self.cin[j, 1].astype(F32)).astype(BF)
+        self.x[j].start()
+
+    def home(self, j):
+        g = self.ring.g
+        self.x[j].wait_recv()
+        self.dbuf[j] = (self.pbuf[j, 0] + self.cin[j, 0].astype(F32) + self.xin[j].astype(F32)).astype(BF)
+        for c in self.d[j]:
+            c.start()
+        self.rbuf[j, g] = self.dbuf[j, g]
+
+    def rows(self, j):
+        for c in self.d[j]:
+            c.wait_recv()
+        return self.rbuf[j].reshape(-1, self.rbuf.shape[-1])
+
+    def sent_core(self):
+        for c in self.c:
+            c.wait_send()
+
+    def sent_rest(self):
+        for c in self.x + [c for row in self.d for c in row]:
+            c.wait_send()
+
+
+class ChunkGather:
+    def __init__(self, ring, place, sbuf, sems):
+        self.ring, self.place, self.sbuf = ring, place, sbuf
+        ss, rs, xs, xr, cs, cr, c2s, c2r = sems
+        k, (nc, n, _, cw) = ring, sbuf.shape
+        self.d = [
+            [rcopy(sbuf.at[j, k.to(o)], place(j, k.t, k.g), ss.at[j, o], rs.at[j, o], k.to(o), k.t) for o in range(1, n)]
+            for j in range(nc)]
+        pair = lambda j, q, a, b, to: rcopy(place(j, q, None), place(j, q, None), a.at[j], b.at[j], k.g, to)
+        self.x = [pair(j, k.t, xs, xr, k.tx) for j in range(nc)]
+        self.c = [pair(j, k.t, cs, cr, k.tc) for j in range(nc)]
+        self.c2 = [pair(j, k.tx, c2s, c2r, k.tc) for j in range(nc)]
+
+    def out(self, j, rows):
+        self.sbuf[j] = rows.reshape(self.sbuf.shape[1:])
+        for c in self.d[j]:
+            c.start()
+        self.place(j, self.ring.t, self.ring.g)[...] = self.sbuf[j, self.ring.g]
+
+    def cross(self, j):
+        for c in self.d[j]:
+            c.wait_recv()
+        self.x[j].start()
+        self.c[j].start()
+
+    def core(self, j):
+        self.x[j].wait_recv()
+        self.c2[j].start()
+
+    def here(self, j):
+        self.c[j].wait_recv()
+        self.c2[j].wait_recv()
+
+    def sent(self):
+        for c in [c for row in self.d for c in row] + self.x + self.c + self.c2:
+            c.wait_send()
+
+
+def middle_body(
+    n, attn, x_own, att_rows, att_gate, mlp_rows, dy_own, gain_p, gain_t, d_mbr, query, wo_hbm, wg_hbm, wu_hbm, wd_hbm,
+    d_rows, d_hidden, hidden, mbr, gain_part, n2, inner, d_gate, d_up, q_back, *scratch,
+):
+    (wo, wg, wu, wd, hid, att_t, mlp_t, whole, gate_acc, up_acc, d_in, pbuf, cbuf, xbuf, dbuf,
+     cin1, xin1, rb1, cin2, xin2, rb2, sb1, sb2, sq, sq_in, r_own, r_in, r_to, r_back, s_col) = scratch[:30]
+    wsem, qs, qr, as_, ar, rss, rsr, rds, rdr = scratch[30:39]
+    s1, s2s, g1, g2 = scratch[39:45], scratch[45:51], scratch[51:59], scratch[59:67]
+    ring = Ring(n)
+    g, t = ring.g, ring.t
+    rows, width = x_own.shape
+    cw = width // NC
+    features, ff = 4 * width, wg.shape[1]
+    slots = attn.shape[0]
+
+    loads = {"wo": [], "wg": [], "wu": []}
+    for j in range(NC):
+        for q in range(4):
+            to, at = pl.ds((j * 4 + q) * cw, cw), pl.ds(q * width + j * cw, cw)
+            i = j * 4 + q
+            loads["wo"].append(pltpu.make_async_copy(wo_hbm.at[:, at], wo.at[:, to], wsem.at[0, i]))
+            loads["wg"].append(pltpu.make_async_copy(wg_hbm.at[at, :], wg.at[to, :], wsem.at[1, i]))
+            loads["wu"].append(pltpu.make_async_copy(wu_hbm.at[at, :], wu.at[to, :], wsem.at[2, i]))
+    loads["wd"] = [pltpu.make_async_copy(wd_hbm, wd, wsem.at[3, 0])]
+    for name in ("wo", "wd", "wg", "wu"):
+        for c in loads[name]:
+            c.start()
+
+    def loaded(name):
+        for c in loads[name]:
+            c.wait()
+
+    chunk = lambda j: pl.ds(j * 4 * cw, 4 * cw)
+    att_t[...] = att_rows[...].T
+    mlp_t[...] = mlp_rows[...].T
+    ring.greet_everyone()
+    asked = [rcopy(query.at[ring.to(o)], q_back.at[g], as_.at[o], ar.at[o], ring.to(o), t) for o in range(1, n)]
+
+    red1 = ChunkReduce(
+        ring, lambda j: mm(attn[...], wo[:, chunk(j)]), whole, pbuf, (cbuf, xbuf, dbuf), (cin1, xin1, rb1), s1)
+    gat1 = ChunkGather(
+        ring, lambda j, q, e: hid.at[j, slice(None) if e is None else e, :, pl.ds(pl.multiple_of(q * cw, cw), cw)], sb1, g1)
+    shared = [rcopy(sq, sq_in.at[i], qs.at[i], qr.at[i], g, q) for i, q in enumerate([ring.tc, ring.tx, ring.tcx])]
+    ones = jnp.ones((8, cw), BF)
+
+    def hidden_chunk(j):
+        high, low = split_bf(red1.rows(j).astype(F32) * att_gate[...])
+        got = x_own[:, j * cw:(j + 1) * cw] + mm(att_t[...], high) + mm(att_t[...], low)
+        hidden[:, j * cw:(j + 1) * cw] = got
+        gat1.out(j, mm(mlp_rows[...], got.astype(BF)).astype(BF))
+        high, low = split_bf(got * got)
+        squares = mm_t(ones, high) + mm_t(ones, low)
+        sq[...] = squares if j == 0 else sq[...] + squares
+        if j == NC - 1:
+            for c in shared:
+                c.start()
+
+    pieces = tile_list(ff, 512)
+
+    def d_inner(i):
+        if i == 0:
+            loaded("wd")
+        a, w = pieces[i]
+        d_in[:, a:a + w] = mm_t(d_mbr[...], wd[a:a + w, :])
+
+    def absorb(j):
+        gat1.here(j)
+        v = hid[j].reshape(slots, 4 * cw).astype(F32)
+        part = jnp.sum(v * v, axis=1, keepdims=True)
+        s_col[...] = part if j == 0 else s_col[...] + part
+        u = (v * gain_p[:, j * 4 * cw:(j + 1) * 4 * cw]).astype(BF)
+        for a, w in pieces:
+            cc = slice(a, a + w)
+            gate, up = mm(u, wg[chunk(j), cc]), mm(u, wu[chunk(j), cc])
+            gate_acc[:, cc] = gate if j == 0 else gate_acc[:, cc] + gate
+            up_acc[:, cc] = up if j == 0 else up_acc[:, cc] + up
+
+    loaded("wo")
+    for j in range(NC):
+        red1.core(j)
+        if j:
+            red1.cross(j - 1)
+    red1.cross(NC - 1)
+    plan = [(2 * j, 0, functools.partial(red1.home, j)) for j in range(NC)]
+    plan += [(2 * j + 3, 1, functools.partial(hidden_chunk, j)) for j in range(NC)]
+    plan += [(2 * j + 7, 2, functools.partial(gat1.cross, j)) for j in range(NC)]
+    plan += [(2 * j + 9, 3, functools.partial(gat1.core, j)) for j in range(NC)]
+    plan += [(2 * i + 1.5, 4, functools.partial(d_inner, i)) for i in range(len(pieces))]
+    plan += [(2 * j + 10.5, 5, functools.partial(absorb, j)) for j in range(NC)]
+    plan += [(10.2, 0, lambda: (loaded("wg"), loaded("wu")))]
+    plan += [(9.5, 0, lambda: [c.start() for c in asked])]
+    for _, _, run in sorted(plan, key=lambda s: s[:2]):
+        run()
+
+    s_col[...] = lax.rsqrt(s_col[...] / features + EPSILON)
+    r_own[...] = jnp.zeros_like(r_own)
+
+    def units(at, size):
+        s = s_col[...]
+        gate, up, d = gate_acc[:, at] * s, up_acc[:, at] * s, d_in[:, at]
+        sig = jax.nn.sigmoid(gate)
+        silu = gate * sig
+        inner[:, at] = (silu * up).astype(BF)
+        du = (d * silu).astype(BF)
+        dg = (d * up * sig * (1.0 + gate * (1.0 - sig))).astype(BF)
+        d_up[:, at] = du
+        d_gate[:, at] = dg
+        r_own[...] += mm_t(jnp.ones((8, size), BF), (gate * dg.astype(F32) + up * du.astype(F32)).astype(BF))
+
+    def unit_tile(i, _):
+        units(pl.ds(pl.multiple_of(i * 128, 128), 128), 128)
+        return _
+
+    lax.fori_loop(0, ff // 128, unit_tile, 0)
+    red1.sent_core()
+    red1.sent_rest()
+    for c in shared:
+        c.wait_recv()
+    total = (sq[...] + sq_in[0] + sq_in[1] + sq_in[2])[:1]
+    eye = iota((rows, rows), 0) == iota((rows, rows), 1)
+    scale = lax.rsqrt(jnp.sum(jnp.where(eye, total, 0.0), axis=1, keepdims=True) / features + EPSILON)
+
+    told = [rcopy(r_own, r_in.at[i], rss.at[i], rsr.at[i], g, q) for i, q in enumerate([ring.tc, ring.tx, ring.tcx])]
+    for c in told:
+        c.start()
+    half = lambda d: pl.ds(pl.multiple_of(d // 2 * 128, 128), 128)
+    pairs = [rcopy(r_to.at[:, half(ring.to(o))], r_back.at[g], rds.at[o], rdr.at[o], ring.to(o), t) for o in range(1, n)]
+
+    def share_r():
+        for c in told:
+            c.wait_recv()
+        r_to[...] = r_own[...] + r_in[0] + r_in[1] + r_in[2]
+        for c in pairs:
+            c.start()
+        r_back[g] = r_to[:, half(g)]
+
+    total_r = {}
+
+    def take_r():
+        for c in pairs:
+            c.wait_recv()
+        odd = lax.rem(g, 2) == 1
+        got = jnp.concatenate([jnp.where(odd, r_back[e][:, 64:], r_back[e][:, :64]) for e in range(n)], axis=1)
+        high, low = split_bf(got)
+        total_r[0] = (mm_t(mlp_t[...], high) + mm_t(mlp_t[...], low))[:, :1] / features
+
+    red2 = ChunkReduce(
+        ring, lambda j: mm_t(d_gate[...], wg[chunk(j), :]) + mm_t(d_up[...], wu[chunk(j), :]), whole, pbuf,
+        (cbuf, xbuf, dbuf), (cin2, xin2, rb2), s2s)
+    gat2 = ChunkGather(
+        ring, lambda j, q, e: d_rows.at[slice(None) if e is None else e, :, cols_of(q, j, width, cw)], sb2, g2)
+
+    def mixed_cols(j):
+        for q in range(4):
+            mbr[j, :, q * cw:(q + 1) * cw] = mm(inner[...], wd[:, q * width + j * cw:q * width + (j + 1) * cw]).astype(BF)
+
+    def d_hidden_chunk(j):
+        got = red2.rows(j)
+        if j == 0:
+            take_r()
+        cc = slice(j * cw, (j + 1) * cw)
+        h = hidden[:, cc]
+        d_n = mm(mlp_t[...], got)
+        d_h = dy_own[:, cc].astype(F32) + scale * (gain_t[:, cc] * d_n) - h * (scale * scale) * total_r[0]
+        d_hidden[:, cc] = d_h
+        gain_part[:, cc] = jnp.broadcast_to(jnp.sum(d_n * h * scale, axis=0, keepdims=True), (8, cw))
+        gat2.out(j, mm(att_rows[...], d_h.astype(BF)).astype(BF))
+
+    def keep_normed(j):
+        for q in range(4):
+            at, to = slice((j * 4 + q) * cw, (j * 4 + q + 1) * cw), slice(q * width + j * cw, q * width + (j + 1) * cw)
+            v = hid[j, :, :, q * cw:(q + 1) * cw].reshape(slots, cw).astype(F32)
+            n2[:, to] = (v * s_col[...] * gain_p[:, at]).astype(BF)
+
+    for j in range(NC):
+        red2.core(j)
+        if j == 0:
+            share_r()
+        else:
+            red2.cross(j - 1)
+    red2.cross(NC - 1)
+    plan = [(2 * j, 0, functools.partial(red2.home, j)) for j in range(NC)]
+    plan += [(2 * j + 3, 1, functools.partial(d_hidden_chunk, j)) for j in range(NC)]
+    plan += [(2 * j + 7, 2, functools.partial(gat2.cross, j)) for j in range(NC)]
+    plan += [(2 * j + 9, 3, functools.partial(gat2.core, j)) for j in range(NC)]
+    plan += [(2 * j + 1.5, 4, functools.partial(keep_normed, j)) for j in range(NC)]
+    plan += [(2 * j + 4.5, 5, functools.partial(mixed_cols, j)) for j in range(NC)]
+    for _, _, run in sorted(plan, key=lambda s: s[:2]):
+        run()
+    for c in asked:
+        c.wait_recv()
+    q_back[g] = query[g]
+    for j in range(NC):
+        gat2.here(j)
+    for c in asked + shared + told + pairs:
+        c.wait_send()
+    gat1.sent()
+    gat2.sent()
+    red2.sent_core()
+    red2.sent_rest()
+
+
+def middle(attn, x_own, att_rows, att_gate, mlp_rows, dy_own, gain, gain_t, d_mbr, query, wo, wg, wu, wd, n, cid):
+    slots, (rows, width) = attn.shape[0], x_own.shape
+    r, cw, features, ff, hw = slots // n, width // NC, 4 * width, wg.shape[1], attn.shape[1]
+    gain_p = gain.reshape(4, NC, cw).transpose(1, 0, 2).reshape(1, features)
+    any_, vm = pl.BlockSpec(memory_space=pl.ANY), pl.BlockSpec(memory_space=VM)
+    sds = jax.ShapeDtypeStruct
+    one, two = VM((NC, n, r, cw), BF), VM((NC, 2, n, r, cw), BF)
+    return pl.pallas_call(
+        functools.partial(middle_body, n),
+        out_shape=(
+            sds((n, r, features), BF), sds((rows, width), F32), sds((rows, width), F32), sds((NC, slots, 4 * cw), BF), sds((8, width), F32),
+            sds((slots, features), BF), sds((slots, ff), BF), sds((slots, ff), BF), sds((slots, ff), BF), sds((n, r, hw), BF)),
+        in_specs=[vm] * 10 + [any_] * 4, out_specs=[vm] * 10,
+        scratch_shapes=[
+            VM((hw, features), BF), VM((features, ff), BF), VM((features, ff), BF), VM((ff, features), BF),
+            VM((NC, n, r, 4 * cw), BF), VM((rows, slots), BF), VM((rows, slots), BF),
+            VM((slots, 4 * cw), F32), VM((slots, ff), F32), VM((slots, ff), F32), VM((slots, ff), F32),
+            VM((NC, 2, n, r, cw), F32), two, one, one]
+        + [two, one, one] * 2 + [one, one]
+        + [VM((8, rows), F32), VM((3, 8, rows), F32), VM((8, slots), F32), VM((3, 8, slots), F32), VM((8, slots), F32),
+           VM((n, 8, 128), F32), VM((slots, 1), F32)]
+        + [DMA((4, 16)), DMA((3,)), DMA((3,)), DMA((n,)), DMA((n,)), DMA((3,)), DMA((3,)), DMA((n,)), DMA((n,))]
+        + REDUCE_SEMS(NC, n) * 2 + GATHER_SEMS(NC, n) * 2,
+        name="middle", compiler_params=pltpu.CompilerParams(
+            collective_id=cid, has_side_effects=True, vmem_limit_bytes=63 * 2**20),
+    )(attn, x_own, att_rows, att_gate, mlp_rows, dy_own, gain_p, gain_t, d_mbr, query, wo, wg, wu, wd)
+
+
 def fast_local(
     tokens, out_grad, row_place, seq_lengths, att_routes, att_gates, mlp_routes, mlp_gates,
     gain_attn, w_kv, w_query, w_out, gain_mlp, w_gate, w_up, w_down,
@@ -1522,25 +1876,21 @@
         x_all, gain_attn[None], w_k, w_v, w_query[0], meta_all, cos_t, sin_t, dy_part, in_gate[1], cid=13)
     normed_flat, picked = normed.reshape(n * rows, features), picked.reshape(n * CAP, features)
     attn = attn.reshape(n * CAP, hw)
-    query_back = lax.all_to_all(query, "dp", split_axis=0, concat_axis=0, tiled=True)
-    hidden, hid_rows, scale_mlp = hidden_rows(
-        attn, w_out[0], x_own, att_rows.T, att_gate.reshape(-1, 1), mlp_rows, n, cid=9)
+    d_mbr = d_mbr.reshape(n * CAP, features)
 
     gain_mlp_t, gain_attn_t = part(gain_mlp), part(gain_attn)
-    d_mbr = d_mbr.reshape(n * CAP, features)
-    d_obr, d_hidden, mixed_rows, gain_mlp_part, normed2, inner, d_gate, d_up = expert_layer(
-        hid_rows, d_mbr, gain_mlp[None], w_gate[0], w_up[0], w_down[0], hidden, dy_own.astype(F32), gain_mlp_t[None],
-        scale_mlp, mlp_rows.T, mlp_gate.reshape(-1, 1), mlp_rows, att_rows, n, cid=10)
+    d_rows, d_hidden, hidden, mbr, gain_mlp_part, normed2, inner, d_gate, d_up, query_back = middle(
+        attn, x_own, att_rows, att_gate.reshape(-1, 1), mlp_rows, dy_own, gain_mlp, gain_mlp_t[None],
+        d_mbr, query, w_out[0], w_gate[0], w_up[0], w_down[0], n, cid=9)
     w_gate_grad = mm_rows(normed2, d_gate)[None]
     w_up_grad = mm_rows(normed2, d_up)[None]
     w_down_grad = mm_rows(inner, d_mbr)[None]
 
-    d_obr, d_attn, dq_pre = attend_back(
-        d_obr, in_gate[0], w_out[0], query, keys, values, bias, turn_slots)
+    d_kv_all, back, gains, d_obr, dq_pre = layer_tail(
+        (d_rows, in_gate[0], query, bias, turn_slots, query_back, keys, values, meta_all, cos_t, sin_t, x_own, scale_attn,
+         gain_attn_t[None], d_hidden, hidden, mbr, mlp_gate.reshape(-1, 1), mlp_rows, att_rows, gain_mlp_part),
+        (w_out[0], w_query[0], w_k, w_v), n, cid=11)
     d_obr, dq_flat = d_obr.reshape(n * CAP, features), dq_pre.reshape(n * CAP, hw)
-    d_kv_all, back, gains = layer_tail(
-        (dq_flat, w_query[0], d_attn, query_back, keys, values, meta_all, cos_t, sin_t,
-         w_k, w_v, x_own, scale_attn, gain_attn_t[None], d_hidden, mixed_rows, gain_mlp_part, att_rows.T), n, cid=11)
     w_out_grad = mm_rows(attn, d_obr)[None]
     w_query_grad = mm_rows(picked, dq_flat)[None]
     w_kv_grad = map_grad(normed_flat, d_kv_all.reshape(n * rows, 2 * hw))

time: 365 us -> 328 us (0.90)
  the two profiles are of different devices: /device:TPU:0 before, /device:TPU:5 now
where the time goes in v4:
time: 328 us; the launch traced here: 322 us
  Pallas kernels  278 us (85%)
  matrix products  27.5 us (8%)
  local copies, waits for them, and re-layouts  12.2 us (4%)
    pallas_call x1, Pallas kernels, middle(): pl.pallas_call(functools.partial(middle_body, n), out_shape=(sds((n, r, f...  103 us
    pallas_call x1, Pallas kernels, layer_tail(): pl.pallas_call(functools.partial(tail_body, n), out_shape=(sds((n, rows,...  86.6 us
    pallas_call x1, Pallas kernels, layer_start(): pl.pallas_call(functools.partial(start_body, n), out_shape=(sds((n, n, pe...  47.4 us
    pallas_call x1, Pallas kernels, attend(): pl.pallas_call(functools.partial(attend_body, n), grid=(n // pair,), out_...  30.3 us
    dot_general x7, matrix products, dot(): return lax.dot_general(a, b, dims, preferred_element_type=F32)  27.5 us
    pallas_call x1, Pallas kernels, map_grad(): pl.pallas_call(map_grad_body, grid=(features // size,), out_shape=jax.Sha...  11.6 us

profile of v4, /device:TPU:5, one launch (start us, length us, event | category | flops | bytes accessed | tf_op | source)
XLA Modules:
  0.0 321.8 jit_solution(10139136689895569022)
XLA Ops:
  0.6 0.8 reduce-window.4
  1.5 0.1 convert_reduce_fusion
  1.6 0.7 fusion.1
  2.2 0.1 select_reduce_fusion
  2.3 1.3 dynamic_slice.7
  3.7 1.3 dynamic_slice.6
  5.0 0.8 convert_bitcast_fusion.1
  5.8 0.8 slice_bitcast_fusion.2
  6.5 1.2 stack.5.meta_w
  7.7 1.3 copy.39
  9.0 1.4 copy.37
  10.5 47.4 %layer_start.1 = (bf16[8,8,16,2048]{3,2,1,0:T(8,128)(2,1)}, bf16[8,16,512]{2,1,0:T(8,128)(2,1)}, f32[8,16,128]{2,1,0:T(8,128)}, bf16[128,128]{1,0:T(8,128)(2,1)}...) custom-call(bf16[128,2048]{1,0:T(8,128)(2,1)} %tokens.1, ...), custom_call_target="tpu_custom_call" | custom-call | tf_op jit(solution)/shard_map/layer_start/pallas_call | solution.py:1509
  57.9 1.9 slice_bitcast_fusion
  59.7 30.3 %attend.1 = (bf16[8,128,2048]{2,1,0:T(8,128)(2,1)}, bf16[8,64,2048]{2,1,0:T(8,128)(2,1)}, bf16[8,128,512]{2,1,0:T(8,128)(2,1)}, bf16[8,128,512]{2,1,0:T(8,128)(2...) custom-call(bf16[8,128,2048]{2,1,0:T(8,128)(2,1)} %bitcast.102, ...), custom_call_target="tpu_custom_call" | custom-call | tf_op jit(solution)/shard_map/attend/pallas_call | solution.py:1021
  90.0 102.5 %middle.1 = (bf16[8,64,2048]{2,1,0:T(8,128)(2,1)}, f32[128,512]{1,0:T(8,128)}, f32[128,512]{1,0:T(8,128)}, bf16[4,512,512]{2,1,0:T(8,128)(2,1)}, f32[8,512]{1,0:...) custom-call(bf16[512,512]{1,0:T(8,128)(2,1)} %bitcast.106, ...), custom_call_target="tpu_custom_call" | custom-call | tf_op jit(solution)/shard_map/middle/pallas_call | solution.py:1824
  192.5 86.6 %layer_tail.1 = (bf16[8,128,1024]{2,1,0:T(8,128)(2,1)}, bf16[8,32,2048]{2,1,0:T(8,128)(2,1)}, f32[8,2048]{1,0:T(8,128)}, bf16[8,64,2048]{2,1,0:T(8,128)(2,1)}, bf16[8,64,512]{2,1,0:T(8,128)(2,1)}) custom-call(bf16[8,64,2048]{2,1,0:T(8,128)(2,1)} %get-tuple-element.63.d_rows, f32[8,64,1]{2,1,0:T(8,128)} %get-tuple-element.88.in_gate, ...), custom_call_target="tpu_custom_call" | custom-call | tf_op jit(solution)/shard_map/layer_tail/pallas_call | solution.py:1306
  279.2 0.0 copy-start.3
  279.2 0.0 copy-start.4
  279.2 0.0 copy-start.9
  279.2 1.4 fusion.2
  280.6 0.0 copy-done.3
  280.6 1.1 convolution_convert_fusion
  281.8 1.1 convolution_convert_fusion.1
  282.9 1.5 fusion.3
  284.4 0.0 copy-done.9
  284.4 3.3 %convolution_bitcast_fusion.4 = f32[1,2048,512]{2,1,0:T(8,128)} fusion(bf16[8,64,2048]{2,1,0:T(8,128)(2,1)S(1)} %copy-done.4, bf16[8,64,512]{2,1,0:T(8,128)(2,1)S(1)} %copy-done.9), kind=kOutput, calls=%fused_computation.4 | convolution fusion | flops 1073741824 | bytes 6815744 | tf_op jit(solution)/shard_map/dot_general | solution.py:510
  287.8 3.3 %convolution_bitcast_fusion.3 = f32[1,512,2048]{2,1,0:T(8,128)} fusion(bf16[8,64,512]{2,1,0:T(8,128)(2,1)S(1)} %copy-done.1, bf16[8,64,2048]{2,1,0:T(8,128)(2,1)S(1)} %copy-done), kind=kOutput, calls=%fused_computation.3 | convolution fusion | flops 1073741824 | bytes 6815744 | tf_op jit(solution)/shard_map/dot_general | solution.py:510
  291.1 11.6 %map_grad.1 = f32[2048,8,128]{2,1,0:T(8,128)} custom-call(bf16[1024,2048]{1,0:T(8,128)(2,1)} %bitcast.101, bf16[1024,1024]{1,0:T(8,128)(2,1)} %bitcast.103), custom_call_target="tpu_custom_call" | custom-call | tf_op jit(solution)/shard_map/map_grad/pallas_call | solution.py:1078
  302.7 0.0 copy-done.2
  302.7 6.1 %convolution_bitcast_fusion = f32[1,1408,2048]{2,1,0:T(8,128)} fusion(bf16[512,1408]{1,0:T(8,128)(2,1)S(1)} %copy-done.8, bf16[512,2048]{1,0:T(8,128)(2,1)S(1)} %bitcast.108), kind=kOutput, calls=%fused_computation | convolution fusion | flops 2952790016 | bytes 15073280 | tf_op jit(solution)/shard_map/dot_general | solution.py:510
  308.8 6.3 %convolution_bitcast_fusion.2 = f32[1,2048,1408]{2,1,0:T(8,128)} fusion(bf16[512,2048]{1,0:T(8,128)(2,1)S(1)} %copy-done.5, bf16[512,1408]{1,0:T(8,128)(2,1)S(1)} %copy-done.7), kind=kOutput, calls=%fused_computation.2 | convolution fusion | flops 2952790016 | bytes 15073280 | tf_op jit(solution)/shard_map/dot_general | solution.py:510
  315.1 6.3 %convolution_bitcast_fusion.1 = f32[1,2048,1408]{2,1,0:T(8,128)} fusion(bf16[512,2048]{1,0:T(8,128)(2,1)S(1)} %copy-done.5, bf16[512,1408]{1,0:T(8,128)(2,1)S(1)} %copy-done.6), kind=kOutput, calls=%fused_computation.1 | convolution fusion | flops 2952790016 | bytes 15073280 | tf_op jit(solution)/shard_map/dot_general | solution.py:510
  (18 shorter events, 0.0 us)
Async XLA Ops:
  279.2 1.5 copy-start.3
  279.2 5.2 %copy-start.4 = (bf16[8,64,2048]{2,1,0:T(8,128)(2,1)S(1)}, bf16[8,64,2048]{2,1,0:T(8,128)(2,1)}, u32[]{:S(2)}) copy-start(bf16[8,64,2048]{2,1,0:T(8,128)(2,1)} %get-tuple-element.79) | copy-start | bytes 6291460
  279.2 5.2 %copy-start.9 = (bf16[8,64,512]{2,1,0:T(8,128)(2,1)S(1)}, bf16[8,64,512]{2,1,0:T(8,128)(2,1)}, u32[]{:S(2)}) copy-start(bf16[8,64,512]{2,1,0:T(8,128)(2,1)} %get-tuple-element.80) | copy-start | bytes 1572868
  284.4 3.3 %copy-start = (bf16[8,64,2048]{2,1,0:T(8,128)(2,1)S(1)}, bf16[8,64,2048]{2,1,0:T(8,128)(2,1)}, u32[]{:S(2)}) copy-start(bf16[8,64,2048]{2,1,0:T(8,128)(2,1)} %get-tuple-element.81) | copy-start | bytes 6291460
  284.4 3.3 %copy-start.1 = (bf16[8,64,512]{2,1,0:T(8,128)(2,1)S(1)}, bf16[8,64,512]{2,1,0:T(8,128)(2,1)}, u32[]{:S(2)}) copy-start(bf16[8,64,512]{2,1,0:T(8,128)(2,1)} %get-tuple-element.55) | copy-start | bytes 1572868
  291.1 11.6 %copy-start.2 = (bf16[8,64,2048]{2,1,0:T(8,128)(2,1)S(1)}, bf16[8,64,2048]{2,1,0:T(8,128)(2,1)}, u32[]{:S(2)}) copy-start(bf16[8,64,2048]{2,1,0:T(8,128)(2,1)} %get-tuple-element.61) | copy-start | bytes 6291460
  291.1 11.6 %copy-start.8 = (bf16[512,1408]{1,0:T(8,128)(2,1)S(1)}, bf16[512,1408]{1,0:T(8,128)(2,1)}, u32[]{:S(2)}) copy-start(bf16[512,1408]{1,0:T(8,128)(2,1)} %get-tuple-element.85) | copy-start | bytes 4325380
  302.7 6.2 %copy-start.5 = (bf16[512,2048]{1,0:T(8,128)(2,1)S(1)}, bf16[512,2048]{1,0:T(8,128)(2,1)}, u32[]{:S(2)}) copy-start(bf16[512,2048]{1,0:T(8,128)(2,1)} %get-tuple-element.82) | copy-start | bytes 6291460
  302.7 6.2 %copy-start.7 = (bf16[512,1408]{1,0:T(8,128)(2,1)S(1)}, bf16[512,1408]{1,0:T(8,128)(2,1)}, u32[]{:S(2)}) copy-start(bf16[512,1408]{1,0:T(8,128)(2,1)} %get-tuple-element.83) | copy-start | bytes 4325380
  308.8 6.3 %copy-start.6 = (bf16[512,1408]{1,0:T(8,128)(2,1)S(1)}, bf16[512,1408]{1,0:T(8,128)(2,1)}, u32[]{:S(2)}) copy-start(bf16[512,1408]{1,0:T(8,128)(2,1)} %get-tuple-element.84) | copy-start | bytes 4325380
